TPU v7x, 32 devices: a whole 2x2x4 slice. The times are simulated.
32 devices in a mesh: dp: 4 (over y, x), seq: 8 (over z, core).
Axes of the slice: x: 2, y: 2, z: 4, core: 2. Of those that a mesh axis runs over, the one named last changes fastest.
Arguments:
- tokens: bfloat16 [32768, 768], P(('dp', 'seq')), may hold values from -6 to 6
- w_qkv: bfloat16 [768, 2304], P(('dp', 'seq')), may hold values from -0.21875 to 0.21875
- w_out: bfloat16 [768, 768], P(('dp', 'seq')), may hold values from -0.625 to 0.625
- w_up: bfloat16 [768, 3072], P(('dp', 'seq')), may hold values from -0.21875 to 0.21875
- w_down: bfloat16 [3072, 768], P(('dp', 'seq')), may hold values from -0.109375 to 0.109375
- vectors: bfloat16 [8, 768], P(None, ('dp', 'seq'))
- up_bias: bfloat16 [3072], P(('dp', 'seq')), may hold values from -3 to 3
- cluster_route: int32 [4, 12, 8192], P('dp'), may hold values from 0 to 1023, as said below
- upstream: bfloat16 [32768, 768], P(('dp', 'seq')), may hold values from -6 to 6
Outputs:
- layer_out: bfloat16 [32768, 768], P(('dp', 'seq'))
- grad_tokens: bfloat16 [32768, 768], P(('dp', 'seq'))
- grad_qkv: float32 [768, 2304], P(('dp', 'seq'))
- grad_out: float32 [768, 768], P(('dp', 'seq'))
- grad_up: float32 [768, 3072], P(('dp', 'seq'))
- grad_down: float32 [3072, 768], P(('dp', 'seq'))
- grad_vectors: float32 [8, 768], P(None, ('dp', 'seq'))
- grad_up_bias: float32 [3072], P(('dp', 'seq'))
Inputs may be any that keep to these rules, and one draw needn't show every extreme that they name: Each block of 1024 rows holds, in order, 6 sequences of 128 rows and then 16 sequences of 16 rows; sequence number s is made of its rows in all 8 blocks of the group. For each group g, head h and block k, the entries cluster_route[g, h, k * 1024 : (k + 1) * 1024] are a permutation of 0 to 1023; entry k * 1024 + j * 128 + i names the row, within block k, of the token in slot j * 1024 + i * 8 + k. All tokens of one cluster belong to one sequence.
All inputs are finite; a program needn't handle non-finite values.
Results may differ from a plain program's by a relative error of at most 0.014.
Values may be sent and summed in bfloat16 or wider, within the bound.
A program may use at most 192 MiB of HBM per device.

v0:
```python
import jax
import jax.numpy as jnp
from jax import lax
from jax.sharding import PartitionSpec as P

H = 12
CL = 128


epsilon = 1e-06


def normalize(resid, norm_gain, norm_shift):
    average = jnp.mean(resid, axis=-1, keepdims=True)
    centred = resid - average
    spread = jnp.mean(centred * centred, axis=-1, keepdims=True)
    scaled = lax.rsqrt(spread + epsilon)
    normed = centred * scaled
    return (normed * norm_gain + norm_shift, normed, scaled)


def norm_back(grad_output, normed, scaled, norm_gain):
    grad_norm = grad_output * norm_gain
    first_term = jnp.mean(grad_norm, axis=-1, keepdims=True)
    second_term = jnp.mean(grad_norm * normed, axis=-1, keepdims=True)
    return scaled * (grad_norm - first_term - normed * second_term)


def exact_gelu(value):
    return jax.nn.gelu(value, approximate=False)


def order_table(sending):
    heads, rows_here = sending.shape
    columns = jnp.arange(rows_here, dtype=jnp.int32)[None, None, :]
    return (sending[:, :, None] == columns).astype(jnp.bfloat16)


def to_slots(source_rows, table):
    moved = jnp.einsum("hrs,skhe->rkhe", table, source_rows, preferred_element_type=jnp.float32)
    return moved.astype(jnp.bfloat16)


def to_tokens(source_rows, table):
    moved = jnp.einsum("hrs,rkhe->skhe", table, source_rows, preferred_element_type=jnp.float32)
    return moved.astype(jnp.bfloat16)


def cluster_scores(query_c, key_c, scale_factor):
    return (
        jnp.einsum("cahe,cbhe->hcab", query_c, key_c, preferred_element_type=jnp.float32)
        * scale_factor
    )


def shards(tokens, w_qkv, w_out, w_up, w_down, vectors, up_bias, cluster_route, upstream):
    lane_count = lax.axis_size("seq")
    lane_index = lax.axis_index("seq")
    wide_qkv, wide_out, wide_up, wide_down, wide_vectors, wide_bias = (
        lax.all_gather(w_qkv, ("dp", "seq"), axis=0, tiled=True),
        lax.all_gather(w_out, ("dp", "seq"), axis=0, tiled=True),
        lax.all_gather(w_up, ("dp", "seq"), axis=0, tiled=True),
        lax.all_gather(w_down, ("dp", "seq"), axis=0, tiled=True),
        lax.all_gather(vectors, ("dp", "seq"), axis=1, tiled=True),
        lax.all_gather(up_bias, ("dp", "seq"), axis=0, tiled=True),
    )
    rows_here = tokens.shape[0]
    model_width = tokens.shape[1]
    head_size = model_width // H
    portion = rows_here // lane_count
    clusters = rows_here // CL
    scale_factor = head_size ** (-0.5)
    vector_rows = wide_vectors.astype(jnp.float32)
    route_rows = cluster_route[0]
    by_target = lax.dynamic_slice_in_dim(route_rows, lane_index * rows_here, rows_here, 1)
    sending = jnp.swapaxes(by_target.reshape(H, lane_count, portion), 1, 2).reshape(H, rows_here)
    table = order_table(sending)
    projected = jnp.dot(tokens, wide_qkv, preferred_element_type=jnp.float32)
    shifts = jnp.concatenate(
        [vector_rows[0], jnp.zeros((model_width,), jnp.float32), vector_rows[1]]
    )
    projected = (projected + shifts).astype(jnp.bfloat16).reshape(rows_here, 3, H, head_size)
    outgoing = to_slots(projected, table)
    arrived = lax.all_to_all(
        outgoing.reshape(portion, lane_count, 3 * model_width),
        "seq",
        split_axis=1,
        concat_axis=1,
        tiled=True,
    )
    slot_qkv = arrived.reshape(clusters, CL, 3, H, head_size)
    query_c = slot_qkv[:, :, 0]
    key_c = slot_qkv[:, :, 1]
    value_c = slot_qkv[:, :, 2]
    scores = cluster_scores(query_c, key_c, scale_factor)
    row_peak = jnp.max(scores, axis=-1, keepdims=True)
    exponent = jnp.exp(scores - row_peak)
    row_total = jnp.sum(exponent, axis=-1, keepdims=True)
    soft_weights = exponent / row_total
    log_total = row_peak + jnp.log(row_total)
    heads_slot = jnp.einsum(
        "hcab,cbhe->cahe",
        soft_weights.astype(jnp.bfloat16),
        value_c,
        preferred_element_type=jnp.float32,
    ).astype(jnp.bfloat16)
    returned = lax.all_to_all(
        heads_slot.reshape(portion, lane_count, model_width),
        "seq",
        split_axis=1,
        concat_axis=1,
        tiled=True,
    )
    mixed_heads = to_tokens(returned.reshape(rows_here, 1, H, head_size), table).reshape(
        rows_here, model_width
    )
    attention = jnp.dot(mixed_heads, wide_out, preferred_element_type=jnp.float32) + vector_rows[2]
    first_norm, first_normed, first_scaled = normalize(
        tokens.astype(jnp.float32) + attention, vector_rows[4], vector_rows[5]
    )
    first_low = first_norm.astype(jnp.bfloat16)
    widened = jnp.dot(first_low, wide_up, preferred_element_type=jnp.float32) + wide_bias.astype(
        jnp.float32
    )
    activated, gelu_pull = jax.vjp(exact_gelu, widened)
    activated_low = activated.astype(jnp.bfloat16)
    narrowed = (
        jnp.dot(activated_low, wide_down, preferred_element_type=jnp.float32) + vector_rows[3]
    )
    output, second_normed, second_scaled = normalize(
        first_norm + narrowed, vector_rows[6], vector_rows[7]
    )
    back_qkv, back_out, back_up, back_down = (
        lax.all_gather(w_qkv, ("dp", "seq"), axis=0, tiled=True),
        lax.all_gather(w_out, ("dp", "seq"), axis=0, tiled=True),
        lax.all_gather(w_up, ("dp", "seq"), axis=0, tiled=True),
        lax.all_gather(w_down, ("dp", "seq"), axis=0, tiled=True),
    )
    grad_output = upstream.astype(jnp.float32)
    grad_gain_two = jnp.sum(grad_output * second_normed, axis=0)
    grad_shift_two = jnp.sum(grad_output, axis=0)
    grad_second = norm_back(grad_output, second_normed, second_scaled, vector_rows[6])
    grad_narrow = grad_second.astype(jnp.bfloat16)
    grad_down_w = jnp.einsum(
        "tf,td->fd", activated_low, grad_narrow, preferred_element_type=jnp.float32
    )
    grad_down_bias = jnp.sum(grad_narrow.astype(jnp.float32), axis=0)
    grad_active = jnp.einsum(
        "td,fd->tf", grad_narrow, back_down, preferred_element_type=jnp.float32
    )
    grad_wide = gelu_pull(grad_active)[0].astype(jnp.bfloat16)
    grad_up_w = jnp.einsum("td,tf->df", first_low, grad_wide, preferred_element_type=jnp.float32)
    grad_lift_bias = jnp.sum(grad_wide.astype(jnp.float32), axis=0)
    grad_first = grad_second + jnp.einsum(
        "tf,df->td", grad_wide, back_up, preferred_element_type=jnp.float32
    )
    grad_gain_one = jnp.sum(grad_first * first_normed, axis=0)
    grad_shift_one = jnp.sum(grad_first, axis=0)
    grad_resid = norm_back(grad_first, first_normed, first_scaled, vector_rows[4])
    grad_attn = grad_resid.astype(jnp.bfloat16)
    grad_out_w = jnp.einsum("td,te->de", mixed_heads, grad_attn, preferred_element_type=jnp.float32)
    grad_out_bias = jnp.sum(grad_attn.astype(jnp.float32), axis=0)
    grad_mixed = jnp.einsum(
        "te,de->td", grad_attn, back_out, preferred_element_type=jnp.float32
    ).astype(jnp.bfloat16)
    grad_sending = to_slots(grad_mixed.reshape(rows_here, 1, H, head_size), table)
    grad_slot = lax.all_to_all(
        grad_sending.reshape(portion, lane_count, model_width),
        "seq",
        split_axis=1,
        concat_axis=1,
        tiled=True,
    )
    grad_slot = grad_slot.reshape(clusters, CL, H, head_size)
    scores = cluster_scores(query_c, key_c, scale_factor)
    soft_weights = jnp.exp(scores - log_total)
    grad_soft = jnp.einsum(
        "cahe,cbhe->hcab", grad_slot, value_c, preferred_element_type=jnp.float32
    )
    inner_sum = jnp.sum(soft_weights * grad_soft, axis=-1, keepdims=True)
    grad_scores = (soft_weights * (grad_soft - inner_sum)).astype(jnp.bfloat16)
    grad_query = (
        jnp.einsum("hcab,cbhe->cahe", grad_scores, key_c, preferred_element_type=jnp.float32)
        * scale_factor
    )
    grad_key = (
        jnp.einsum("hcab,cahe->cbhe", grad_scores, query_c, preferred_element_type=jnp.float32)
        * scale_factor
    )
    grad_value = jnp.einsum(
        "hcab,cahe->cbhe",
        soft_weights.astype(jnp.bfloat16),
        grad_slot,
        preferred_element_type=jnp.float32,
    )
    grad_slots = jnp.stack([grad_query, grad_key, grad_value], axis=2).astype(jnp.bfloat16)
    came_back = lax.all_to_all(
        grad_slots.reshape(portion, lane_count, 3 * model_width),
        "seq",
        split_axis=1,
        concat_axis=1,
        tiled=True,
    )
    grad_proj = to_tokens(came_back.reshape(rows_here, 3, H, head_size), table).reshape(
        rows_here, 3 * model_width
    )
    grad_qkv_w = jnp.einsum("td,tf->df", tokens, grad_proj, preferred_element_type=jnp.float32)
    bias_sums = jnp.sum(grad_proj.astype(jnp.float32), axis=0).reshape(3, model_width)
    grad_tokens = (
        jnp.einsum("tf,df->td", grad_proj, back_qkv, preferred_element_type=jnp.float32)
        + grad_resid
    ).astype(jnp.bfloat16)
    grad_vector_rows = jnp.stack(
        [
            bias_sums[0],
            bias_sums[2],
            grad_out_bias,
            grad_down_bias,
            grad_gain_one,
            grad_shift_one,
            grad_gain_two,
            grad_shift_two,
        ]
    )
    shares = (
        lax.psum_scatter(grad_qkv_w, ("dp", "seq"), scatter_dimension=0, tiled=True),
        lax.psum_scatter(grad_out_w, ("dp", "seq"), scatter_dimension=0, tiled=True),
        lax.psum_scatter(grad_up_w, ("dp", "seq"), scatter_dimension=0, tiled=True),
        lax.psum_scatter(grad_down_w, ("dp", "seq"), scatter_dimension=0, tiled=True),
        lax.psum_scatter(grad_vector_rows, ("dp", "seq"), scatter_dimension=1, tiled=True),
        lax.psum_scatter(grad_lift_bias, ("dp", "seq"), scatter_dimension=0, tiled=True),
    )
    return (
        output.astype(jnp.bfloat16),
        grad_tokens,
        shares[0],
        shares[1],
        shares[2],
        shares[3],
        shares[4],
        shares[5],
    )


def solution(mesh):
    placed = (
        P(("dp", "seq"), None),
        P(("dp", "seq"), None),
        P(("dp", "seq"), None),
        P(("dp", "seq"), None),
        P(("dp", "seq"), None),
        P(None, ("dp", "seq")),
        P(("dp", "seq")),
        P("dp", None, None),
        P(("dp", "seq"), None),
    )
    return jax.shard_map(
        shards,
        mesh=mesh,
        in_specs=placed,
        out_specs=(
            P(("dp", "seq"), None),
            P(("dp", "seq"), None),
            P(("dp", "seq"), None),
            P(("dp", "seq"), None),
            P(("dp", "seq"), None),
            P(("dp", "seq"), None),
            P(None, ("dp", "seq")),
            P(("dp", "seq")),
        ),
        check_vma=False,
    )
```

profile of v0, /device:TPU:1, one launch (start us, length us, event | category | flops | bytes accessed | tf_op | source)
XLA Modules:
  0.0 1085.2 jit_solution(4485815842057325501)
XLA Ops:
  7.9 43.8 %all-gather = bf16[32,24,8]{1,2,0:T(8,128)(2,1)S(1)} all-gather(bf16[1,24,8]{1,2,0:T(8,128)(2,1)} %bitcast.107), channel_id=1, replica_groups=mesh['dp'=4,'seq'=8] {'dp','seq'}, dimensions={0}, use_global_device_ids=true | all-gather | bytes 12672 | tf_op jit(solution)/shard_map/all_gather | solution.py:64
  53.4 20.4 %all-gather.6.cloned.1.call-done = bf16[768,2304]{1,0:T(8,128)(2,1)} async-done(((bf16[24,2304]{1,0:T(8,128)(2,1)}), bf16[768,2304]{1,0:T(8,128)(2,1)}) %all-gather.6.cloned.1.call-update) | async-done | bytes 3538960 | tf_op jit(solution)/shard_map/all_gather | solution.py:60
  73.8 8.5 add_convert_fusion.1
  88.9 14.2 %convert_bitcast_fusion.1 = bf16[1024,3,12,64]{0,3,1,2:T(8,128)(2,1)} fusion(s32[12,1024]{1,0:T(8,128)S(1)} %eq.15, bf16[1024,3,12,64]{0,3,2,1:T(8,128)(2,1)} %bitcast.104), kind=kOutput, calls=%fused_computation.47 | convolution fusion | flops 4846780416 | bytes 9486336 | tf_op jit(solution)/shard_map/hrs,skhe->rkhe/dot_general | solution.py:40
  103.1 15.2 %copy.110 = bf16[1024,3,12,64]{3,2,1,0:T(8,128)(2,1)} copy(bf16[1024,3,12,64]{0,3,1,2:T(8,128)(2,1)} %convert_bitcast_fusion.1) | data formatting | bytes 9437184 | tf_op jit(solution)/shard_map/convert_element_type | solution.py:41
  118.3 15.6 %reshape.129 = bf16[128,8,2304]{2,1,0:T(8,128)(2,1)} reshape(bf16[1024,3,12,64]{3,2,1,0:T(8,128)(2,1)} %copy.110) | data formatting | bytes 9437184 | tf_op jit(solution)/shard_map/reshape | solution.py:85
  145.5 111.8 %all-to-all-done = bf16[128,8,2304]{2,0,1:T(8,128)(2,1)} async-done(((bf16[128,8,2304]{2,0,1:T(8,128)(2,1)}), bf16[128,8,2304]{2,0,1:T(8,128)(2,1)}, u32[]{:S(2)}, u32[]{:S(2)}) %all-to-all-start) | async-done | bytes 4718624 | tf_op jit(solution)/shard_map/all_to_all | solution.py:84
  257.2 7.0 copy.112
  264.2 14.9 %reshape.130 = bf16[8,128,3,12,64]{4,3,2,1,0:T(8,128)(2,1)} reshape(bf16[128,8,2304]{2,1,0:T(8,128)(2,1)} %copy.112) | data formatting | bytes 9437184 | tf_op jit(solution)/shard_map/reshape | solution.py:91
  279.2 12.8 %slice_bitcast_fusion = (bf16[8,128,12,64]{3,2,1,0:T(8,128)(2,1)}, bf16[8,128,12,64]{3,2,1,0:T(8,128)(2,1)}, bf16[8,128,12,64]{3,2,1,0:T(8,128)(2,1)}, bf16[8,12...) fusion(bf16[8,128,3,12,64]{4,3,2,1,0:T(8,128)(2,1)} %reshape.130), kind=kLoop, calls=%fused_computation.133 | loop fusion | bytes 14155776 | tf_op jit(solution)/shard_map/squeeze | solution.py:93
  331.6 57.6 %all-reduce = bf16[3072]{0:T(1024)(128)(2,1)S(1)} all-reduce(bf16[3072]{0:T(1024)(128)(2,1)S(1)} %dynamic-update-slice), channel_id=1, replica_groups=mesh['dp'=4,'seq'=8] {'dp','seq'}, use_global_device_ids=true, to_apply=%add | all-reduce | flops 3072 | bytes 12288
  398.8 13.8 %fusion.66 = bf16[12,64,1024]{2,1,0:T(8,128)(2,1)} fusion(s32[12,1024]{1,0:T(8,128)S(1)} %eq.15, bf16[1024,12,64]{2,1,0:T(8,128)(2,1)} %reshape.132), kind=kOutput, calls=%fused_computation.94 | convolution fusion | flops 1623982080 | bytes 3194880 | tf_op jit(solution)/shard_map/hrs,rkhe->skhe/dot_general | solution.py:45
  418.1 37.8 %multiply_convert_fusion = (bf16[1024,3072]{1,0:T(8,128)(2,1)}, f32[1024,3072]{1,0:T(8,128)}, f32[1024,3072]{1,0:T(8,128)}) fusion(f32[3072]{0:T(1024)S(1)} %convert_element_type.115, bf16[768,3072]{1,0:T(8,128)(2,1)} %all-gather.10.cloned.1.call-done, f32[1024,768]{0,1:T(8,128)} %copy-done.4, f32[768]{0:T(1024)S(1)} %get-tuple-element.53, ...), kind=kOutput, calls=%fused_computation.15 | convolution fusion | flops 5043388416 | bytes 39348224 | tf_op jit(solution)/shard_map/dot_general | solution.py:122
  456.0 9.6 fusion.115
  471.2 17.5 %convert_reduce_fusion = (f32[3072]{0:T(1024)S(1)}, bf16[1024,3072]{1,0:T(8,128)(2,1)}) fusion(f32[1024,3072]{1,0:T(8,128)} %get-tuple-element.65, bf16[1024,768]{0,1:T(8,128)(2,1)S(1)} %get-tuple-element.61, bf16[3072,768]{1,0:T(8,128)(2,1)} %all-gather.12.cloned.1.call-done, f32[1024,3072]{1,0:T(8,128)} %get-tuple-element.79, ...), kind=kOutput, calls=%fused_computation.13 | convolution fusion | flops 4885312512 | bytes 37773312 | tf_op jit(solution)/shard_map/td,fd->tf/dot_general | solution.py:148
  488.7 11.3 %multiply_reduce_fusion.2 = (f32[768]{0:T(1024)S(1)}, f32[1024]{0:T(1024)S(1)}, f32[1024]{0:T(1024)S(1)}, f32[768]{0:T(1024)S(1)}, f32[1024,768]{0,1:T(8,128)S(1)}) fusion(f32[1024,768]{0,1:T(8,128)} %copy-done.4, f32[1024]{0:T(1024)S(1)} %add_rsqrt_fusion.1, f32[1024]{0:T(1024)S(1)} %broadcast_multiply_fusion.5, f32[768]{0:T(1024)S(1)} %get-tuple-element.54, ...), kind=kOutput, calls=%fused_computation.69 | convolution fusion | flops 4845989888 | bytes 22065152 | tf_op jit(solution)/shard_map/tf,df->td/dot_general | solution.py:154
  505.8 10.5 fusion.108
  521.0 12.1 %fusion.102 = bf16[1024,1,12,64]{0,3,2,1:T(8,128)(2,1)S(1)} fusion(bf16[1024,12,64]{0,2,1:T(8,128)(2,1)S(1)} %bitcast.110, s32[12,1024]{1,0:T(8,128)S(1)} %copy-done.23), kind=kOutput, calls=%fused_computation.105 | convolution fusion | flops 1623982080 | bytes 3194880 | tf_op jit(solution)/shard_map/hrs,skhe->rkhe/dot_general | solution.py:40
  548.8 10.2 fusion.116
  559.1 36.2 %all-to-all-done.2 = bf16[128,8,768]{2,0,1:T(8,128)(2,1)S(1)} async-done(((bf16[128,8,768]{2,0,1:T(8,128)(2,1)}), bf16[128,8,768]{2,0,1:T(8,128)(2,1)S(1)}, u32[]{:S(2)}, u32[]{:S(2)}) %all-to-all-start.2) | async-done | bytes 1572896 | tf_op jit(solution)/shard_map/all_to_all | solution.py:167
  603.4 9.6 fusion.34
  616.4 8.3 multiply_convert_fusion.1
  634.2 14.1 %copy.135 = bf16[8,128,3,12,64]{4,3,2,1,0:T(8,128)(2,1)} copy(bf16[8,128,3,12,64]{1,4,3,0,2:T(8,128)(2,1)} %pad_maximum_fusion) | data formatting | bytes 9437184 | tf_op jit(solution)/shard_map/stack | solution.py:196
  648.4 16.1 %convert_element_type.128 = bf16[128,8,2304]{2,1,0:T(8,128)(2,1)} reshape(bf16[8,128,3,12,64]{4,3,2,1,0:T(8,128)(2,1)} %copy.135) | data formatting | bytes 9437184 | tf_op jit(solution)/shard_map/convert_element_type | solution.py:196
  667.7 152.1 %all_to_all.20 = bf16[128,8,2304]{2,0,1:T(8,128)(2,1)S(1)} all-to-all(bf16[128,8,2304]{2,0,1:T(8,128)(2,1)S(1)} %copy.136), channel_id=1, replica_groups=mesh['dp'=4,'seq'=8] {'seq'}, dimensions={1} | all-to-all | bytes 9437184 | tf_op jit(solution)/shard_map/all_to_all | solution.py:197
  824.5 15.1 %reshape.137 = bf16[1024,3,12,64]{3,2,1,0:T(8,128)(2,1)} reshape(bf16[128,8,2304]{2,1,0:T(8,128)(2,1)} %copy.137) | data formatting | bytes 9437184 | tf_op jit(solution)/shard_map/reshape | solution.py:204
  839.6 19.1 %convert_reduce_fusion.1 = (f32[3,12,64]{2,0,1:T(4,128)S(1)}, bf16[1024,3,12,64]{0,3,1,2:T(8,128)(2,1)}) fusion(s32[12,1024]{1,0:T(8,128)S(1)} %copy-done.23, bf16[1024,3,12,64]{3,2,1,0:T(8,128)(2,1)} %reshape.137), kind=kOutput, calls=%fused_computation.30 | convolution fusion | flops 4851496960 | bytes 9495552 | tf_op jit(solution)/shard_map/hrs,rkhe->skhe/dot_general | solution.py:45
  869.9 8.3 copy.156
  881.6 8.4 add_convert_fusion.2
  891.6 41.0 %all-reduce.3 = (f32[8,768]{1,0:T(8,128)S(1)}, f32[3072]{0:T(1024)S(1)}) all-reduce(f32[8,768]{1,0:T(8,128)S(1)} %stack.47, f32[3072]{0:T(1024)S(1)} %get-tuple-element.85), channel_id=6, replica_groups=mesh['dp'=4,'seq'=8] {'dp','seq'}, use_global_device_ids=true, to_apply=%region_22.0.clone | all-reduce | flops 9216 | bytes 73728
  933.9 18.3 %reduce-scatter.12.cloned.1.call-done = f32[96,768]{1,0:T(8,128)} async-done(((f32[3072,768]{1,0:T(8,128)}), f32[96,768]{1,0:T(8,128)}) %reduce-scatter.12.cloned.1.call-update) | async-done | bytes 294928 | tf_op jit(solution)/shard_map/reduce_scatter | solution.py:229
  952.2 125.7 %reduce-scatter.14.cloned.1.call-done = f32[24,2304]{1,0:T(8,128)} async-done(((f32[768,2304]{1,0:T(8,128)}), f32[24,2304]{1,0:T(8,128)}) %reduce-scatter.14.cloned.1.call-update) | async-done | bytes 221200
  (167 shorter events, 153.3 us)
Async XLA Ops:
  7.2 44.9 %copy-start = (s32[1,12,8192]{2,0,1:T(1,128)S(1)}, s32[1,12,8192]{2,0,1:T(1,128)}, u32[]{:S(2)}) copy-start(s32[1,12,8192]{2,0,1:T(1,128)} %param.16) | copy-start | bytes 1179652
  7.2 66.6 %all-gather.6.cloned.1.call-start = ((), (), s32[]{:S(2)}) async-start(), calls=%async_computation.8 | async-start | bytes 3649536 | tf_op jit(solution)/shard_map/all_gather | solution.py:60
  52.8 346.1 %copy-start.22 = (s32[12,1024]{1,0:T(8,128)}, s32[12,1024]{1,0:T(8,128)S(1)}, u32[]{:S(2)}) copy-start(s32[12,1024]{1,0:T(8,128)S(1)} %eq.15) | copy-start | bytes 147460
  139.3 117.9 %all-to-all-start = ((bf16[128,8,2304]{2,0,1:T(8,128)(2,1)}), bf16[128,8,2304]{2,0,1:T(8,128)(2,1)}, u32[]{:S(2)}, u32[]{:S(2)}) async-start(bf16[128,8,2304]{2,0,1:T(8,128)(2,1)} %copy.111), calls=%async_computation | async-start | bytes 9437184 | tf_op jit(solution)/shard_map/all_to_all | solution.py:84
  144.0 268.6 %all-gather.8.cloned.1.call-start = ((), (), s32[]{:S(2)}) async-start(), calls=%async_computation.9 | async-start | bytes 1216512 | tf_op jit(solution)/shard_map/all_gather | solution.py:61
  144.7 273.4 %all-gather.10.cloned.1.call-start = ((), (), s32[]{:S(2)}) async-start(), calls=%async_computation.10 | async-start | bytes 4866048 | tf_op jit(solution)/shard_map/all_gather | solution.py:62
  307.4 5.4 copy-start.2
  309.2 3.6 copy-start.20
  309.2 3.6 copy-start.9
  323.2 8.2 copy-start.30
  324.7 4.7 copy-start.15
  324.7 66.3 %all-to-all-start.1 = ((bf16[128,8,768]{2,0,1:T(8,128)(2,1)}), bf16[128,8,768]{2,0,1:T(8,128)(2,1)S(1)}, u32[]{:S(2)}, u32[]{:S(2)}) async-start(bf16[128,8,768]{2,0,1:T(8,128)(2,1)} %copy.118), calls=%async_computation.1 | async-start | bytes 3145728 | tf_op jit(solution)/shard_map/all_to_all | solution.py:107
  328.7 127.2 %all-gather.12.cloned.1.call-start = ((), (), s32[]{:S(2)}) async-start(), calls=%async_computation.11 | async-start | bytes 4866048 | tf_op jit(solution)/shard_map/all_gather | solution.py:63
  329.3 604.6 %reduce-scatter.8.cloned.1.call-start = ((), (), s32[]{:S(2)}) async-start(), calls=%async_computation.12 | async-start | bytes 2433024 | tf_op jit(solution)/shard_map/reduce_scatter | solution.py:227
  398.8 13.8 %copy-start.17 = (bf16[1024,768]{0,1:T(8,128)(2,1)S(1)}, bf16[1024,768]{0,1:T(8,128)(2,1)}, u32[]{:S(2)}) copy-start(bf16[1024,768]{0,1:T(8,128)(2,1)} %copy.104) | copy-start | bytes 4718596
  418.1 37.8 %copy-start.29 = (f32[768]{0:T(1024)S(1)}, f32[768]{0:T(1024)}, u32[]{:S(2)}) copy-start(f32[768]{0:T(1024)} %get-tuple-element.52) | copy-start | bytes 9220
  455.9 10.1 copy-start.24
  471.2 17.5 %copy-start.18 = (bf16[1024,768]{0,1:T(8,128)(2,1)}, bf16[1024,768]{0,1:T(8,128)(2,1)S(1)}, u32[]{:S(2)}) copy-start(bf16[1024,768]{0,1:T(8,128)(2,1)S(1)} %get-tuple-element.61) | copy-start | bytes 4718596
  488.7 11.3 %copy-start.5 = (f32[1024,768]{0,1:T(8,128)S(1)}, f32[1024,768]{0,1:T(8,128)}, u32[]{:S(2)}) copy-start(f32[1024,768]{0,1:T(8,128)} %copy-done.4) | copy-start | bytes 9437188
  505.7 428.1 %reduce-scatter.10.cloned.1.call-start = ((), (), s32[]{:S(2)}) async-start(), calls=%async_computation.13 | async-start | bytes 9732096 | tf_op jit(solution)/shard_map/reduce_scatter | solution.py:228
  543.2 5.6 copy-start.19
  544.7 50.6 %all-to-all-start.2 = ((bf16[128,8,768]{2,0,1:T(8,128)(2,1)}), bf16[128,8,768]{2,0,1:T(8,128)(2,1)S(1)}, u32[]{:S(2)}, u32[]{:S(2)}) async-start(bf16[128,8,768]{2,0,1:T(8,128)(2,1)} %copy.125), calls=%async_computation.2 | async-start | bytes 3145728 | tf_op jit(solution)/shard_map/all_to_all | solution.py:167
  548.8 403.4 %reduce-scatter.12.cloned.1.call-start = ((), (), s32[]{:S(2)}) async-start(), calls=%async_computation.14 | async-start | bytes 9732096 | tf_op jit(solution)/shard_map/reduce_scatter | solution.py:229
  559.0 518.9 %reduce-scatter.14.cloned.1.call-start = ((), (), s32[]{:S(2)}) async-start(), calls=%async_computation.15 | async-start | bytes 7299072
  597.2 19.2 %slice-start = ((s8[6291456]{0:T(1024)(128)(4,1)}), s8[2097152]{0:T(1024)(128)(4,1)S(1)}, s32[]{:S(2)}) async-start(s8[6291456]{0:T(1024)(128)(4,1)} %bitcast.100), calls=%async_computation.16 | async-start | bytes 4194304
  603.4 9.6 copy-start.3
  603.4 9.6 copy-start.7
  603.4 13.0 %slice-start.1 = ((s8[6291456]{0:T(1024)(128)(4,1)}), s8[4194304]{0:T(1024)(128)(4,1)S(1)}, s32[]{:S(2)}) async-start(s8[6291456]{0:T(1024)(128)(4,1)} %bitcast.100), calls=%async_computation.17 | async-start | bytes 8388608
  624.7 5.6 copy-start.12
  624.7 5.7 copy-start.32
  858.7 5.3 copy-start.16
  881.6 196.3 %copy-start.1 = (s32[1,12,8192]{2,0,1:T(1,128)S(1)}, s32[1,12,8192]{2,0,1:T(1,128)}, u32[]{:S(2)}) copy-start(s32[1,12,8192]{2,0,1:T(1,128)} %param.16) | copy-start | bytes 1179652
  (14 other events, 26.8 us)
Sparse Core Ops, SparseCore 0:
  11.0 62.7 all-gather.5
  147.8 57.5 all-gather.7
  208.5 90.7 all-gather.9
  332.3 72.4 all-gather.11
  505.9 108.2 reduce-scatter.7
  621.5 188.8 reduce-scatter.9
  816.9 135.2 reduce-scatter.11
  959.4 118.4 reduce-scatter.13
where the time goes:
time: 1100 us; the launch traced here: 1090 us
  waiting for transfers between devices  315 us (29%)
  blocking collectives  294 us (27%)
  local copies, waits for them, and re-layouts  215 us (20%)
  matrix products  209 us (19%)
  other arithmetic  23.2 us (2%)
  between operations  15.1 us (1%)
  starting transfers between devices  13.3 us (1%)
    all_to_all x1, blocking collectives, shards(): lax.all_to_all(grad_slots.reshape(portion, lane_count, 3 * model_width),...  152 us
    unnamed x9, waiting for transfers between devices  128 us
    all_to_all x1, waiting for transfers between devices, shards(): lax.all_to_all(outgoing.reshape(portion, lane_count, 3 * model_width), 's...  112 us
    unnamed x2, blocking collectives  98.6 us
    all_gather x1, blocking collectives, shards(): lax.all_gather(vectors, ('dp', 'seq'), axis=1, tiled=True)  43.8 us
    unnamed x82, local copies, waits for them, and re-layouts  40.5 us
    dot_general x1, matrix products, shards(): jnp.dot(first_low, wide_up, preferred_element_type=jnp.float32)  37.8 us
    all_to_all x1, waiting for transfers between devices, shards(): lax.all_to_all(grad_sending.reshape(portion, lane_count, model_width), 's...  36.2 us
  transfers between devices with their start and end apart: 11, of which 5 were waited for; matrix products, arithmetic and copies ran while one was open for 30% of the time, Pallas kernels for 0%

commit v1 on v0

--- a/solution.py
+++ b/solution.py
@@ -1,6 +1,10 @@
+import functools
+
 import jax
 import jax.numpy as jnp
 from jax import lax
+from jax.experimental import pallas as pl
+from jax.experimental.pallas import tpu as pltpu
 from jax.sharding import PartitionSpec as P
 
 H = 12
@@ -242,31 +246,557 @@
     )
 
 
+MESH = pl.DeviceIdType.MESH
+NZ = 4
+BLK = 128
+
+class Links:
+    def __init__(self, send_sems, recv_sems):
+        self.send_sems, self.recv_sems, self.count, self.drains = send_sems, recv_sems, 0, []
+        self.dp, self.sq = lax.axis_index("dp"), lax.axis_index("seq")
+        self.x, self.y = lax.rem(self.dp, 2), self.dp // 2
+        self.core, self.z = lax.rem(self.sq, 2), self.sq // 2
+        self.sib = self.sq + 1 - 2 * self.core
+        self.dp_x = self.dp + 1 - 2 * self.x
+        self.dp_y = self.dp + 2 - 4 * self.y
+
+    def new(self):
+        self.count += 1
+        return self.count - 1
+
+    def copy(self, i, src, dst, dp, sq):
+        return pltpu.make_async_remote_copy(
+            src_ref=src, dst_ref=dst, send_sem=self.send_sems.at[i], recv_sem=self.recv_sems.at[i],
+            device_id=(dp, sq), device_id_type=MESH)
+
+    def enter(self, near=True, line=True):
+        barrier = pltpu.get_barrier_semaphore()
+        n = 0
+        if near:
+            for dp in (self.dp_x, self.dp_y):
+                pl.semaphore_signal(barrier, inc=1, device_id=(dp, self.sq), device_id_type=MESH)
+                n += 1
+        if line:
+            for j in range(1, 2 * NZ):
+                pl.semaphore_signal(barrier, inc=1, device_id=(self.dp, lax.rem(self.sq + j, 2 * NZ)), device_id_type=MESH)
+                n += 1
+        pl.semaphore_wait(barrier, n)
+
+    def drain(self):
+        for d in self.drains:
+            d()
+
+
+def mult(v, m):
+    return pl.multiple_of(v, m)
+
+
+def gather(L, shard, full, half_buf, r, split):
+    half = full.shape[1] // 2
+    a, b = split
+    big = 2 * r
+    mine = pl.ds(mult(L.core * half, 128), half)
+    other = pl.ds(mult((1 - L.core) * half, 128), half)
+    cols_a = pl.ds(mult(L.core * half, 128), a)
+    cols_b = pl.ds(mult(L.core * half + a, 128), b)
+    chip = lambda z: pl.ds(mult((L.dp * NZ + z) * big, 16), big)
+    quarter = lambda dp, n=1: pl.ds(mult(dp * NZ * big, 16), n * NZ * big)
+    i0 = L.new()
+    fr = [None] + [L.new() for _ in range(3)]
+    fl = [None] + [L.new() for _ in range(3)]
+    ax, by, ay, bx0, bx1, c0, c1, c2 = [L.new() for _ in range(8)]
+    first = L.copy(i0, shard.at[:, other], half_buf, L.dp, L.sib)
+
+    def right(d, z0):
+        return L.copy(fr[d], full.at[chip(z0), mine], full.at[chip(z0), mine], L.dp, L.sq + 2)
+
+    def left(d, z0):
+        return L.copy(fl[d], full.at[chip(z0), mine], full.at[chip(z0), mine], L.dp, L.sq - 2)
+
+    def send_line(d):
+        @pl.when((L.z >= d - 1) & (L.z < NZ - 1))
+        def _():
+            right(d, L.z - d + 1).start()
+
+        @pl.when((L.z <= NZ - d) & (L.z > 0))
+        def _():
+            left(d, L.z + d - 1).start()
+
+    def drain_line(d):
+        @pl.when((L.z >= d - 1) & (L.z < NZ - 1))
+        def _():
+            right(d, L.z - d + 1).wait_send()
+
+        @pl.when((L.z <= NZ - d) & (L.z > 0))
+        def _():
+            left(d, L.z + d - 1).wait_send()
+
+    def recv_line(d):
+        @pl.when(L.z >= d)
+        def _():
+            right(d, L.z - d).wait_recv()
+
+        @pl.when(L.z + d <= NZ - 1)
+        def _():
+            left(d, L.z + d).wait_recv()
+
+    def same(i, rows, cols, dp, sq):
+        ref = full.at[rows, cols]
+        return L.copy(i, ref, ref, dp, sq)
+
+    def s0():
+        first.start()
+        L.drains.append(first.wait_send)
+
+    def s1():
+        first.wait_recv()
+        own, got = shard[:, mine], half_buf[...]
+
+        @pl.when(L.core == 0)
+        def _():
+            full[chip(L.z), mine] = jnp.concatenate([own, got], axis=0)
+
+        @pl.when(L.core == 1)
+        def _():
+            full[chip(L.z), mine] = jnp.concatenate([got, own], axis=0)
+        send_line(1)
+        L.drains.append(functools.partial(drain_line, 1))
+
+    def s2():
+        recv_line(1)
+        send_line(2)
+        L.drains.append(functools.partial(drain_line, 2))
+
+    def s3():
+        recv_line(2)
+        send_line(3)
+        L.drains.append(functools.partial(drain_line, 3))
+
+    def go(cs):
+        for c in cs:
+            c.start()
+            L.drains.append(c.wait_send)
+
+    def s4():
+        recv_line(3)
+        q = quarter(L.dp)
+        go([same(ax, q, cols_a, L.dp_x, L.sq), same(by, q, cols_b, L.dp_y, L.sq), same(c0, q, mine, L.dp, L.sib)])
+
+    def s5():
+        same(ax, quarter(L.dp_x), cols_a, L.dp_x, L.sq).wait_recv()
+        go([same(ay, quarter(2 * L.y, 2), cols_a, L.dp_y, L.sq)])
+        same(by, quarter(L.dp_y), cols_b, L.dp_y, L.sq).wait_recv()
+        go([same(bx0, quarter(L.dp), cols_b, L.dp_x, L.sq), same(bx1, quarter(L.dp_y), cols_b, L.dp_x, L.sq)])
+
+    def s6():
+        same(bx0, quarter(L.dp_x), cols_b, L.dp_x, L.sq).wait_recv()
+        go([same(c1, quarter(L.dp_x), mine, L.dp, L.sib)])
+        same(ay, quarter(2 * (1 - L.y), 2), cols_a, L.dp_y, L.sq).wait_recv()
+        same(bx1, quarter(3 - L.dp), cols_b, L.dp_x, L.sq).wait_recv()
+        go([same(c2, quarter(2 * (1 - L.y), 2), mine, L.dp, L.sib)])
+
+    def s7():
+        same(c0, quarter(L.dp), other, L.dp, L.sib).wait_recv()
+        same(c1, quarter(L.dp_x), other, L.dp, L.sib).wait_recv()
+        same(c2, quarter(2 * (1 - L.y), 2), other, L.dp, L.sib).wait_recv()
+    return [s0, s1, s2, s3, s4, s5, s6, s7]
+
+
+def spread(L, src, dst, local_sem):
+    ids = [None] + [L.new() for _ in range(2 * NZ - 1)]
+    block = lambda s: pl.ds(mult(s * BLK, BLK), BLK)
+    keep = pltpu.make_async_copy(src.at[block(L.sq)], dst.at[block(L.sq)], local_sem)
+
+    def move(j, to, frm):
+        return L.copy(ids[j], src.at[block(to)], dst.at[block(frm)], L.dp, to)
+
+    def begin():
+        keep.start()
+        for j in range(1, 2 * NZ):
+            c = move(j, lax.rem(L.sq + j, 2 * NZ), L.sq)
+            c.start()
+            L.drains.append(c.wait_send)
+
+    def finish():
+        keep.wait()
+        for j in range(1, 2 * NZ):
+            move(j, L.sq, lax.rem(L.sq + 2 * NZ - j, 2 * NZ)).wait_recv()
+    return begin, finish
+
+
+def add_into(dst, rows0, cols, src, n):
+    step = 48
+
+    def one(i, _):
+        here = pl.ds(mult(i * step, 16), step)
+        there = pl.ds(mult(rows0 + i * step, 16), step)
+        dst[there, cols] = (dst[there, cols].astype(jnp.float32) + src[here, :].astype(jnp.float32)).astype(jnp.bfloat16)
+        return 0
+    lax.fori_loop(0, n // step, one, 0)
+
+
+def reduce_scratch(r, c, split):
+    half, (a, b), big = c // 2, split, 2 * r
+    bf = lambda *s: pltpu.VMEM(s, jnp.bfloat16)
+    return [bf(32 * r, half), bf(8 * big, a), bf(4 * big, b), bf(4 * big, b), bf(4 * big, a), bf(4 * big, b),
+            bf(3, big, half), bf(3, big, half), pltpu.VMEM((2, r, half), jnp.float32), pltpu.VMEM((r, half), jnp.float32)]
+
+
+N_REDUCE = 14
+
+
+def reduce(L, part, out, scratch, r, split):
+    acc, a1, b1x, b1y, a2, b2, from_l, from_r, fin, got = scratch
+    half = part.shape[1] // 2
+    a, b = split
+    big = 2 * r
+    mine = pl.ds(mult(L.core * half, 128), half)
+    other = pl.ds(mult((1 - L.core) * half, 128), half)
+    ca, cb = pl.ds(0, a), pl.ds(a, b)
+    quarter = lambda dp, n=1: pl.ds(mult(dp * NZ * big, 16), n * NZ * big)
+    chip = lambda z: pl.ds(mult((L.dp * NZ + z) * big, 16), big)
+    i0, ia1, ibx, iby, ia2, ib2, ifin = [L.new() for _ in range(7)]
+    ir = [None] + [L.new() for _ in range(3)]
+    il = [L.new() for _ in range(3)]
+    q = lambda dp: dp * NZ * big
+    other_y = quarter(2 * (1 - L.y), 2)
+
+    def go(*cs):
+        for c in cs:
+            c.start()
+            L.drains.append(c.wait_send)
+
+    core_copy = L.copy(i0, part.at[:, other], acc, L.dp, L.sib)
+    a1_copy = L.copy(ia1, acc.at[other_y, ca], a1, L.dp_y, L.sq)
+    bx_copy = L.copy(ibx, acc.at[quarter(L.dp_x), cb], b1x, L.dp_x, L.sq)
+    by_copy = L.copy(iby, acc.at[quarter(3 - L.dp), cb], b1y, L.dp_x, L.sq)
+    a2_copy = L.copy(ia2, acc.at[quarter(L.dp_x), ca], a2, L.dp_x, L.sq)
+    b2_copy = L.copy(ib2, acc.at[quarter(L.dp_y), cb], b2, L.dp_y, L.sq)
+
+    def s0():
+        go(core_copy)
+
+    def s1():
+        core_copy.wait_recv()
+        step = 48
+
+        def one(i, _):
+            here = pl.ds(mult(i * step, 16), step)
+            acc[here, :] = (acc[here, :].astype(jnp.float32) + part[here, mine].astype(jnp.float32)).astype(jnp.bfloat16)
+            return 0
+        lax.fori_loop(0, acc.shape[0] // step, one, 0)
+        go(a1_copy, bx_copy, by_copy)
+
+    def s2():
+        a1_copy.wait_recv()
+        add_into(acc, q(2 * L.y), ca, a1, 8 * big)
+        go(a2_copy)
+        bx_copy.wait_recv()
+        by_copy.wait_recv()
+        add_into(acc, q(L.dp_y), cb, b1y, 4 * big)
+        go(b2_copy)
+        add_into(acc, q(L.dp), cb, b1x, 4 * big)
+
+    def s3():
+        a2_copy.wait_recv()
+        add_into(acc, q(L.dp), ca, a2, 4 * big)
+        b2_copy.wait_recv()
+        add_into(acc, q(L.dp), cb, b2, 4 * big)
+
+    full_cols = pl.ds(0, half)
+
+    def hop_r(t, src):
+        return L.copy(ir[t], src, from_l.at[t - 1], L.dp, L.sq + 2)
+
+    def hop_l(t, src):
+        return L.copy(il[t], src, from_r.at[t], L.dp, L.sq - 2)
+
+    def merge(buf, k, t):
+        buf[k] = (buf[k].astype(jnp.float32) + acc[chip(t), :].astype(jnp.float32)).astype(jnp.bfloat16)
+
+    def line(s):
+        @pl.when(L.z == s)
+        def _():
+            for t in range(NZ - 1, s, -1):
+                if s == 0:
+                    hop_r(t, acc.at[chip(t), full_cols]).start()
+                else:
+                    hop_r(t, from_l.at[t - 1]).wait_recv()
+                    merge(from_l, t - 1, t)
+                    hop_r(t, from_l.at[t - 1]).start()
+
+        @pl.when(L.z == NZ - 1 - s)
+        def _():
+            for t in range(0, NZ - 1 - s):
+                if s == 0:
+                    hop_l(t, acc.at[chip(t), full_cols]).start()
+                else:
+                    hop_l(t, from_r.at[t]).wait_recv()
+                    merge(from_r, t, t)
+                    hop_l(t, from_r.at[t]).start()
+
+        def drain():
+            @pl.when(L.z == s)
+            def _():
+                for t in range(NZ - 1, s, -1):
+                    hop_r(t, from_l.at[t - 1]).wait_send()
+
+            @pl.when(L.z == NZ - 1 - s)
+            def _():
+                for t in range(0, NZ - 1 - s):
+                    hop_l(t, from_r.at[t]).wait_send()
+        L.drains.append(drain)
+
+    fin_copy = L.copy(ifin, fin.at[1 - L.core], got, L.dp, L.sib)
+
+    def s7():
+        for z in range(NZ):
+            @pl.when(L.z == z)
+            def _(z=z):
+                total = acc[chip(z), :].astype(jnp.float32)
+                if z > 0:
+                    hop_r(z, from_l.at[z - 1]).wait_recv()
+                    total = total + from_l[z - 1].astype(jnp.float32)
+                if z < NZ - 1:
+                    hop_l(z, from_r.at[z]).wait_recv()
+                    total = total + from_r[z].astype(jnp.float32)
+                fin[...] = total.reshape(2, r, half)
+        go(fin_copy)
+
+    def s8():
+        out[:, mine] = fin[L.core]
+        fin_copy.wait_recv()
+        out[:, other] = got[...]
+    return [s0, s1, s2, s3] + [functools.partial(line, s) for s in range(3)] + [s7, s8]
+
+
+def one_hot(slots, rows):
+    row = lax.broadcasted_iota(jnp.int32, (rows, slots.shape[1]), 0)
+    return jnp.where(slots == row, 1.0, 0.0).astype(jnp.bfloat16)
+
+
+def head_lanes(width):
+    row = lax.broadcasted_iota(jnp.int32, (2 * BLK, width), 0)
+    lane = lax.rem(lax.broadcasted_iota(jnp.int32, (2 * BLK, width), 1), 128)
+    return (row < BLK) == (lane < 64)
+
+
+def dot(a, b, ca, cb):
+    return lax.dot_general(a, b, (((ca,), (cb,)), ((), ())), preferred_element_type=jnp.float32)
+
+
+def attend_fwd(scale, q_ref, k_ref, v_ref, perm_ref, mixed_ref, slot_ref, prob_ref, head_ref):
+    nblk = q_ref.shape[0] // BLK
+    share = BLK // nblk
+    keep = head_lanes(384)
+    for k in range(nblk):
+        here = pl.ds(k * BLK, BLK)
+        packed = jnp.concatenate([q_ref[here, :], k_ref[here, :], v_ref[here, :]], axis=1)
+        table = one_hot(perm_ref[0, k:k + 1, :], BLK)
+        moved = jnp.where(keep, dot(table, packed, 0, 0), 0.0).astype(jnp.bfloat16)
+        slot_ref[0, :, :, pl.ds(k * share, share), :] = moved.reshape(2, nblk, share, 384)
+    for h in range(2):
+        for c in range(nblk):
+            q, kk, v = slot_ref[0, h, c, :, 0:128], slot_ref[0, h, c, :, 128:256], slot_ref[0, h, c, :, 256:384]
+            scores = dot(q, kk, 1, 1) * scale
+            e = jnp.exp(scores - jnp.max(scores, axis=-1, keepdims=True))
+            probs = (e / jnp.sum(e, axis=-1, keepdims=True)).astype(jnp.bfloat16)
+            prob_ref[0, h, c] = probs
+            head_ref[h, c] = dot(probs, v, 1, 0).astype(jnp.bfloat16)
+    for k in range(nblk):
+        table = one_hot(perm_ref[0, k:k + 1, :], BLK)
+        back = head_ref[:, :, pl.ds(k * share, share), :].reshape(2 * BLK, BLK)
+        mixed_ref[pl.ds(k * BLK, BLK), :] = dot(table, back, 1, 0).astype(jnp.bfloat16)
+
+
+def attend_bwd(scale, dm_ref, perm_ref, slot_ref, prob_ref, dq_ref, dk_ref, dv_ref, sums_ref, up_ref, grad_ref):
+    nblk = dm_ref.shape[0] // BLK
+    share = BLK // nblk
+    keep = head_lanes(128)
+    for k in range(nblk):
+        table = one_hot(perm_ref[0, k:k + 1, :], BLK)
+        moved = jnp.where(keep, dot(table, dm_ref[pl.ds(k * BLK, BLK), :], 0, 0), 0.0).astype(jnp.bfloat16)
+        up_ref[:, :, pl.ds(k * share, share), :] = moved.reshape(2, nblk, share, 128)
+    for h in range(2):
+        for c in range(nblk):
+            q, kk, v = slot_ref[0, h, c, :, 0:128], slot_ref[0, h, c, :, 128:256], slot_ref[0, h, c, :, 256:384]
+            probs, up = prob_ref[0, h, c], up_ref[h, c]
+            dprobs = dot(up, v, 1, 1)
+            p32 = probs.astype(jnp.float32)
+            inner = jnp.sum(p32 * dprobs, axis=-1, keepdims=True)
+            dscores = (p32 * (dprobs - inner)).astype(jnp.bfloat16)
+            grad_ref[h, c, :, 0:128] = (dot(dscores, kk, 1, 0) * scale).astype(jnp.bfloat16)
+            grad_ref[h, c, :, 128:256] = (dot(dscores, q, 0, 0) * scale).astype(jnp.bfloat16)
+            grad_ref[h, c, :, 256:384] = dot(probs, up, 0, 0).astype(jnp.bfloat16)
+    total = jnp.zeros((1, 384), jnp.float32)
+    for k in range(nblk):
+        table = one_hot(perm_ref[0, k:k + 1, :], BLK)
+        back = grad_ref[:, :, pl.ds(k * share, share), :].reshape(2 * BLK, 384)
+        here = pl.ds(k * BLK, BLK)
+        moved = dot(table, back, 1, 0)
+        total = total + jnp.sum(moved, axis=0, keepdims=True)
+        moved = moved.astype(jnp.bfloat16)
+        dq_ref[here, :] = moved[:, 0:128]
+        dk_ref[here, :] = moved[:, 128:256]
+        dv_ref[here, :] = moved[:, 256:384]
+    sums_ref[...] = jnp.broadcast_to(total, (8, 384))
+
+
+SIZES = {"qkv": (24, 2560, (640, 640)), "out": (24, 768, (256, 128)), "up": (24, 3072, (768, 768)), "down": (96, 768, (128, 256))}
+ALL = ("dp", "seq")
+VM = pl.BlockSpec(memory_space=pltpu.VMEM)
+BF = jnp.bfloat16
+LIMIT = 60 * 2**20
+
+
+def gather_kernel(names, na, *refs):
+    n = len(names)
+    ins, outs, sc = refs[:n + na], refs[n + na:2 * (n + na)], refs[2 * (n + na):]
+    L = Links(sc[n], sc[n + 1])
+    L.enter()
+    progs = [gather(L, ins[i], outs[i], sc[i], SIZES[nm][0], SIZES[nm][2]) for i, nm in enumerate(names)]
+    sp = [spread(L, ins[n + i], outs[n + i], sc[n + 2].at[i]) for i in range(na)]
+    for k in range(8):
+        for p in progs:
+            p[k]()
+        if k == 3:
+            for b, _ in sp:
+                b()
+    for _, f in sp:
+        f()
+    L.drain()
+
+
+def gather_call(names, shards, rows):
+    na, n = len(rows), len(names)
+    count = 15 * n + 7 * na
+    outs = [jax.ShapeDtypeStruct((32 * SIZES[nm][0], SIZES[nm][1]), BF) for nm in names]
+    outs += [jax.ShapeDtypeStruct(a.shape, BF) for a in rows]
+    return pl.pallas_call(
+        functools.partial(gather_kernel, names, na), out_shape=outs, in_specs=[VM] * (n + na), out_specs=[VM] * (n + na),
+        scratch_shapes=[pltpu.VMEM((SIZES[nm][0], SIZES[nm][1] // 2), BF) for nm in names]
+        + [pltpu.SemaphoreType.DMA((count,)), pltpu.SemaphoreType.DMA((count,)), pltpu.SemaphoreType.DMA((max(na, 1),))],
+        compiler_params=pltpu.CompilerParams(collective_id=0, has_side_effects=True, vmem_limit_bytes=LIMIT),
+    )(*shards, *rows)
+
+
+def reduce_kernel(names, na, *refs):
+    n = len(names)
+    ins, outs, sc = refs[:n + na], refs[n + na:2 * (n + na)], refs[2 * (n + na):]
+    L = Links(sc[10 * n], sc[10 * n + 1])
+    L.enter()
+    progs = [reduce(L, ins[i], outs[i], sc[10 * i:10 * i + 10], SIZES[nm][0], SIZES[nm][2]) for i, nm in enumerate(names)]
+    sp = [spread(L, ins[n + i], outs[n + i], sc[10 * n + 2].at[i]) for i in range(na)]
+    for b, _ in sp:
+        b()
+    for k in range(9):
+        for p in progs:
+            p[k]()
+    for _, f in sp:
+        f()
+    L.drain()
+
+
+def reduce_call(names, parts, rows, cid):
+    na, n = len(rows), len(names)
+    count = N_REDUCE * n + 7 * na
+    outs = [jax.ShapeDtypeStruct(SIZES[nm][:2], jnp.float32) for nm in names]
+    outs += [jax.ShapeDtypeStruct(a.shape, BF) for a in rows]
+    return pl.pallas_call(
+        functools.partial(reduce_kernel, names, na), out_shape=outs, in_specs=[VM] * (n + na), out_specs=[VM] * (n + na),
+        scratch_shapes=sum([reduce_scratch(*SIZES[nm]) for nm in names], [])
+        + [pltpu.SemaphoreType.DMA((count,)), pltpu.SemaphoreType.DMA((count,)), pltpu.SemaphoreType.DMA((max(na, 1),))],
+        compiler_params=pltpu.CompilerParams(collective_id=cid, has_side_effects=True, vmem_limit_bytes=LIMIT),
+    )(*parts, *rows)
+
+
+def slot_rows(route, me):
+    heads, n = route.shape[0], 2 * NZ
+    per = route.reshape(heads, n, -1)
+    mine = (per[:, 0] // BLK) == me
+    place = jnp.cumsum(mine.astype(jnp.int32), axis=1) - 1
+    pick = (mine[:, None, :] & (place[:, None, :] == jnp.arange(BLK)[None, :, None])).astype(BF)
+    local = jnp.where(mine[:, None, :], per - me * BLK, 0).astype(BF)
+    rows = jnp.einsum("hke,hse->hks", local, pick, preferred_element_type=jnp.float32).astype(jnp.int32)
+    return rows.reshape(heads // 2, 2, n, BLK).transpose(0, 2, 1, 3).reshape(heads // 2, n, 2 * BLK)
+
+
+def homes(tokens, w_qkv, w_out, w_up, w_down, vectors, up_bias, cluster_route, upstream):
+    me = lax.axis_index("seq")
+    rows_here, width = tokens.shape
+    pairs = H // 2
+    scale = (width // H) ** -0.5
+    aux = jnp.pad(vectors.T, ((0, 0), (0, 248))) + jnp.pad(up_bias[None, :], ((0, 23), (8, 152)))
+    full_qkv, full_out, full_up, full_down, x, g = gather_call(
+        ("qkv", "out", "up", "down"), [jnp.concatenate([w_qkv, aux], axis=1), w_out, w_up, w_down], [tokens, upstream])
+    perm = slot_rows(cluster_route[0], me)
+    vec = full_qkv[:, 2304:2312].T.astype(jnp.float32)
+    ub = full_qkv[::24, 2312:2408].reshape(-1).astype(jnp.float32)
+    w = full_qkv[:, :2304]
+    shifts = jnp.concatenate([vec[0], jnp.zeros((width,), jnp.float32), vec[1]])
+    qkv = (jnp.dot(x, w, preferred_element_type=jnp.float32) + shifts).astype(BF)
+    col = lambda o: pl.BlockSpec((rows_here, 128), lambda p, o=o: (0, p + o))
+    perm_spec = pl.BlockSpec((1, 8, 256), lambda p: (p, 0, 0))
+    slot_spec = pl.BlockSpec((1, 2, 8, BLK, 384), lambda p: (p, 0, 0, 0, 0))
+    prob_spec = pl.BlockSpec((1, 2, 8, BLK, BLK), lambda p: (p, 0, 0, 0, 0))
+    mixed, slots, probs = pl.pallas_call(
+        functools.partial(attend_fwd, scale), grid=(pairs,),
+        out_shape=[jax.ShapeDtypeStruct((rows_here, width), BF), jax.ShapeDtypeStruct((pairs, 2, 8, BLK, 384), BF),
+                   jax.ShapeDtypeStruct((pairs, 2, 8, BLK, BLK), BF)],
+        in_specs=[col(0), col(pairs), col(2 * pairs), perm_spec], out_specs=[col(0), slot_spec, prob_spec],
+        scratch_shapes=[pltpu.VMEM((2, 8, BLK, BLK), BF)],
+        compiler_params=pltpu.CompilerParams(vmem_limit_bytes=LIMIT),
+    )(qkv, qkv, qkv, perm)
+    attention = jnp.dot(mixed, full_out, preferred_element_type=jnp.float32) + vec[2]
+    first, n1, s1 = normalize(x.astype(jnp.float32) + attention, vec[4], vec[5])
+    low = first.astype(BF)
+    wide = jnp.dot(low, full_up, preferred_element_type=jnp.float32) + ub
+    act, pull = jax.vjp(exact_gelu, wide)
+    act = act.astype(BF)
+    narrow = jnp.dot(act, full_down, preferred_element_type=jnp.float32) + vec[3]
+    out, n2, s2 = normalize(first + narrow, vec[6], vec[7])
+    gf = g.astype(jnp.float32)
+    gain2, shift2 = jnp.sum(gf * n2, axis=0), jnp.sum(gf, axis=0)
+    d_second = norm_back(gf, n2, s2, vec[6])
+    d_narrow = d_second.astype(BF)
+    g_down = jnp.einsum("tf,td->fd", act, d_narrow, preferred_element_type=jnp.float32).astype(BF)
+    down_bias = jnp.sum(d_narrow.astype(jnp.float32), axis=0)
+    d_wide = pull(jnp.einsum("td,fd->tf", d_narrow, full_down, preferred_element_type=jnp.float32))[0].astype(BF)
+    g_up = jnp.einsum("td,tf->df", low, d_wide, preferred_element_type=jnp.float32).astype(BF)
+    g_ub = jnp.sum(d_wide.astype(jnp.float32), axis=0)
+    d_first = d_second + jnp.einsum("tf,df->td", d_wide, full_up, preferred_element_type=jnp.float32)
+    gain1, shift1 = jnp.sum(d_first * n1, axis=0), jnp.sum(d_first, axis=0)
+    d_res = norm_back(d_first, n1, s1, vec[4])
+    d_attn = d_res.astype(BF)
+    g_out = jnp.einsum("td,te->de", mixed, d_attn, preferred_element_type=jnp.float32).astype(BF)
+    out_bias = jnp.sum(d_attn.astype(jnp.float32), axis=0)
+    d_mixed = jnp.einsum("te,de->td", d_attn, full_out, preferred_element_type=jnp.float32).astype(BF)
+    dq, dk, dv, sums = pl.pallas_call(
+        functools.partial(attend_bwd, scale), grid=(pairs,),
+        out_shape=[jax.ShapeDtypeStruct((rows_here, width), BF)] * 3 + [jax.ShapeDtypeStruct((8 * pairs, 384), jnp.float32)],
+        in_specs=[col(0), perm_spec, slot_spec, prob_spec], out_specs=[col(0)] * 3 + [pl.BlockSpec((8, 384), lambda p: (p, 0))],
+        scratch_shapes=[pltpu.VMEM((2, 8, BLK, BLK), BF), pltpu.VMEM((2, 8, BLK, 384), BF)],
+        compiler_params=pltpu.CompilerParams(vmem_limit_bytes=LIMIT),
+    )(d_mixed, perm, slots, probs)
+    sums = sums[::8].reshape(pairs, 3, 128)
+    d_proj = jnp.concatenate([dq, dk, dv], axis=1)
+    g_qkv = jnp.einsum("td,tf->df", x, d_proj, preferred_element_type=jnp.float32).astype(BF)
+    gx = (jnp.einsum("tf,df->td", d_proj, w, preferred_element_type=jnp.float32) + d_res).astype(BF)
+    g_vec = jnp.stack([sums[:, 0].reshape(-1), sums[:, 2].reshape(-1), out_bias, down_bias, gain1, shift1, gain2, shift2])
+    g_aux = jnp.pad(g_vec.T, ((0, 0), (0, 248)))
+    g_aux = g_aux.reshape(32, 24, 256) + jnp.pad(g_ub.reshape(32, 1, 96), ((0, 0), (0, 23), (8, 152)))
+    part = jnp.concatenate([g_qkv, g_aux.reshape(768, 256).astype(BF)], axis=1)
+    r_out, r_up, r_down, out_rows = reduce_call(("out", "up", "down"), [g_out, g_up, g_down], [out.astype(BF)], 1)
+    r_qkv, gx_rows = reduce_call(("qkv",), [part], [gx], 2)
+    return (out_rows, gx_rows, r_qkv[:, :2304], r_out, r_up, r_down, r_qkv[:, 2304:2312].T, r_qkv[0, 2312:2408])
+
+
 def solution(mesh):
-    placed = (
-        P(("dp", "seq"), None),
-        P(("dp", "seq"), None),
-        P(("dp", "seq"), None),
-        P(("dp", "seq"), None),
-        P(("dp", "seq"), None),
-        P(None, ("dp", "seq")),
-        P(("dp", "seq")),
-        P("dp", None, None),
-        P(("dp", "seq"), None),
-    )
+    small = dict(mesh.shape) == {"dp": 4, "seq": 2 * NZ}
+    rows = P(ALL, None)
     return jax.shard_map(
-        shards,
-        mesh=mesh,
-        in_specs=placed,
-        out_specs=(
-            P(("dp", "seq"), None),
-            P(("dp", "seq"), None),
-            P(("dp", "seq"), None),
-            P(("dp", "seq"), None),
-            P(("dp", "seq"), None),
-            P(("dp", "seq"), None),
-            P(None, ("dp", "seq")),
-            P(("dp", "seq")),
-        ),
+        homes if small else shards, mesh=mesh,
+        in_specs=(rows,) * 5 + (P(None, ALL), P(ALL), P("dp", None, None), rows),
+        out_specs=(rows,) * 6 + (P(None, ALL), P(ALL)),
         check_vma=False,
     )

time: 1100 us -> 487 us (0.44)
  Pallas kernels: 0 us -> 320 us
  waiting for transfers between devices: 315 us -> 0 us
  blocking collectives: 294 us -> 0 us
  local copies, waits for them, and re-layouts: 215 us -> 20.3 us
  matrix products: 209 us -> 118 us
  between operations: 15.1 us -> 1.49 us
  starting transfers between devices: 13.3 us -> 0 us
    pallas_call x0 -> x5, Pallas kernels: none -> 320 us  [the longest x2 138 us: reduce_call(): pl.pallas_call(functools.partial(reduce_kernel, names, na), out_shape=out...]
    all_to_all x1 -> x0, blocking collectives: 152 us -> none  [shards(): lax.all_to_all(grad_slots.reshape(portion, lane_count, 3 * model_width),...]
    all_to_all x3 -> x0, waiting for transfers between devices: 148 us -> none  [the longest x1 112 us: shards(): lax.all_to_all(outgoing.reshape(portion, lane_count, 3 * model_width), 's...]
    unnamed x9 -> x0, waiting for transfers between devices: 128 us -> none
    unnamed x2 -> x0, blocking collectives: 98.6 us -> none
    dot_general x22 -> x13, matrix products: 209 us -> 118 us  [the longest x1 37.9 us: homes(): wide = jnp.dot(low, full_up, preferred_element_type=jnp.float32) + ub]
    reshape x9 -> x2, local copies, waits for them, and re-layouts: 70.5 us -> 0.1 us  [the longest x1 0.09 us: homes(): g_ub.reshape(32, 1, 96)]
    convert_element_type x9 -> x1, local copies, waits for them, and re-layouts: 53.6 us -> 0.08 us  [homes(): ub = full_qkv[::24, 2312:2408].reshape(-1).astype(jnp.float32)]
  transfers between devices with their start and end apart: 11 -> 0, of which waited for: 5 -> 0; matrix products, arithmetic and copies ran while one was open for 30% -> 0% of each run, Pallas kernels for 0% -> 0%
where the time goes in v1:
time: 487 us; the launch traced here: 478 us
  Pallas kernels  320 us (66%)
  matrix products  118 us (24%)
  local copies, waits for them, and re-layouts  20.3 us (4%)
  other arithmetic  18.8 us (4%)
    pallas_call x2, Pallas kernels, reduce_call(): pl.pallas_call(functools.partial(reduce_kernel, names, na), out_shape=out...  138 us
    pallas_call x1, Pallas kernels, gather_call(): pl.pallas_call(functools.partial(gather_kernel, names, na), out_shape=out...  110 us
    dot_general x1, matrix products, homes(): wide = jnp.dot(low, full_up, preferred_element_type=jnp.float32) + ub  37.9 us
    pallas_call x1, Pallas kernels, homes(): pl.pallas_call(functools.partial(attend_fwd, scale), grid=(pairs,), out_s...  36.9 us
    pallas_call x1, Pallas kernels, homes(): pl.pallas_call(functools.partial(attend_bwd, scale), grid=(pairs,), out_s...  34.9 us
    dot_general x1, matrix products, homes(): jnp.einsum('td,fd->tf', d_narrow, full_down, preferred_element_type=jnp.f...  18.7 us
    unnamed x54, local copies, waits for them, and re-layouts  11.7 us
    dot_general x1, matrix products, homes(): jnp.einsum('tf,td->fd', act, d_narrow, preferred_element_type=jnp.float32)  10.5 us

profile of v1, /device:TPU:1, one launch (start us, length us, event | category | flops | bytes accessed | tf_op | source)
XLA Modules:
  0.0 478.1 jit_solution(6399154008002105827)
XLA Ops:
  2.1 1.6 pad_maximum_fusion.1.refs_0_
  3.7 1.9 reduce.2
  6.0 3.4 reduce-window.6
  10.2 1.9 fusion.24
  12.1 110.2 %shard_map.152 = (bf16[768,2560]{1,0:T(8,128)(2,1)}, bf16[768,768]{1,0:T(8,128)(2,1)}, bf16[768,3072]{1,0:T(8,128)(2,1)}, bf16[3072,768]{1,0:T(8,128)(2,1)}, bf1...) custom-call(bf16[24,2560]{1,0:T(8,128)(2,1)} %pad_maximum_fusion.1.refs_0_, bf16[24,768]{1,0:T(8,128)(2,1)} %refs_1_.1, ...), custom_call_target="tpu_custom_call" | custom-call | tf_op jit(solution)/shard_map/pallas_call | solution.py:675
  124.5 1.6 slice_reduce_fusion
  126.2 7.5 %add_convert_fusion.1.q_ref.k_ref.v_ref = bf16[1024,2304]{1,0:T(8,128)(2,1)} fusion(bf16[1024,768]{1,0:T(8,128)(2,1)S(1)} %copy-done.12, f32[2304]{0:T(1024)S(1)} %pad_maximum_fusion.2, bf16[768,2560]{1,0:T(8,128)(2,1)} %get-tuple-element.28), kind=kOutput, calls=%fused_computation.18 | convolution fusion | flops 3628597248 | bytes 9839616 | tf_op jit(solution)/shard_map/dot_general | solution.py:737
  133.7 36.9 %shard_map.153 = (bf16[1024,768]{1,0:T(8,128)(2,1)}, bf16[6,2,8,128,384]{4,3,2,1,0:T(8,128)(2,1)}, bf16[6,2,8,128,128]{4,3,2,1,0:T(8,128)(2,1)}) custom-call(bf16[1024,2304]{1,0:T(8,128)(2,1)} %add_convert_fusion.1.q_ref.k_ref.v_ref, bf16[1024,2304]{1,0:T(8,128)(2,1)} %add_convert_fusion.1.q_ref.k_ref.v_ref, ...), custom_call_target="tpu_custom_call" | custom-call | tf_op jit(solution)/shard_map/pallas_call | solution.py:742
  170.5 3.6 fusion.46
  174.7 37.9 %multiply_convert_fusion = (bf16[1024,3072]{1,0:T(8,128)(2,1)S(1)}, f32[1024,3072]{1,0:T(8,128)}, f32[1024,3072]{1,0:T(8,128)}) fusion(f32[3072]{0:T(1024)S(1)} %reshape.117, bf16[768,3072]{1,0:T(8,128)(2,1)} %get-tuple-element.31, f32[1024,768]{1,0:T(8,128)S(1)} %get-tuple-element.96, f32[768]{0:T(1024)S(1)} %get-tuple-element.81, ...), kind=kOutput, calls=%fused_computation.4 | convolution fusion | flops 5043388416 | bytes 39348224 | tf_op jit(solution)/shard_map/dot_general | solution.py:753
  212.6 5.5 %fusion.47 = (f32[1024]{0:T(1024)S(1)}, f32[1024,768]{1,0:T(8,128)S(1)}) fusion(f32[768]{0:T(1024)S(1)} %get-tuple-element.80, bf16[1024,3072]{1,0:T(8,128)(2,1)S(1)} %get-tuple-element.90, bf16[3072,768]{1,0:T(8,128)(2,1)S(1)} %bitcast.64, f32[768]{0:T(1024)S(1)} %get-tuple-element.81, f32[768]{0:T(1024)S(1)} %get-tuple-element.82, ...), kind=kOutput, calls=%fused_computation.117 | convolution fusion | flops 4837342208 | bytes 17323008 | tf_op jit(solution)/shard_map/dot_general | solution.py:756
  219.5 2.8 fusion.15
  222.3 2.4 convert_reduce_fusion.2
  224.7 18.7 %convert_reduce_fusion = (f32[3072]{0:T(1024)S(1)}, bf16[1024,3072]{1,0:T(8,128)(2,1)}) fusion(f32[1024,3072]{1,0:T(8,128)} %get-tuple-element.91, bf16[3072,768]{1,0:T(8,128)(2,1)} %get-tuple-element.32, f32[1024,768]{1,0:T(8,128)} %get-tuple-element.87, f32[1024,3072]{1,0:T(8,128)} %get-tuple-element.97, f32[3072]{0:T(1024)S(1)} %reshape.117), kind=kOutput, calls=%fused_computation.2 | convolution fusion | flops 4886098944 | bytes 39346176 | tf_op jit(solution)/shard_map/td,fd->tf/dot_general | solution.py:764
  243.4 10.5 %convolution_convert_fusion.refs_2_ = bf16[3072,768]{1,0:T(8,128)(2,1)} fusion(bf16[1024,3072]{1,0:T(8,128)(2,1)} %copy-done.17, f32[1024,768]{1,0:T(8,128)} %get-tuple-element.87), kind=kOutput, calls=%fused_computation.22 | convolution fusion | flops 4834983936 | bytes 14155776 | tf_op jit(solution)/shard_map/tf,td->fd/dot_general | solution.py:762
  253.9 8.4 %multiply_reduce_fusion = (f32[768]{0:T(1024)S(1)}, f32[1024]{0:T(1024)S(1)}, f32[1024]{0:T(1024)S(1)}, f32[768]{0:T(1024)S(1)}, f32[1024,768]{1,0:T(8,128)S(1)}) fusion(f32[1024,768]{1,0:T(8,128)S(1)} %get-tuple-element.96, f32[1024]{0:T(1024)S(1)} %add_rsqrt_fusion.1, f32[1024]{0:T(1024)S(1)} %broadcast_multiply_fusion.5, f32[768]{0:T(1024)S(1)} %get-tuple-element.82, ...), kind=kOutput, calls=%fused_computation.37 | convolution fusion | flops 4839698432 | bytes 20472832 | tf_op jit(solution)/shard_map/tf,df->td/dot_general | solution.py:767
  262.4 1.1 convert_reduce_fusion.3
  263.5 8.3 %convolution_convert_fusion.1.refs_1_ = bf16[768,3072]{1,0:T(8,128)(2,1)} fusion(bf16[1024,3072]{1,0:T(8,128)(2,1)S(1)} %copy-done.16, f32[1024,768]{1,0:T(8,128)S(1)} %get-tuple-element.96, f32[768]{0:T(1024)S(1)} %get-tuple-element.81, f32[768]{0:T(1024)S(1)} %get-tuple-element.82, f32[1024]{0:T(1024)S(1)} %add_rsqrt_fusion.1, ...), kind=kOutput, calls=%fused_computation.23 | convolution fusion | flops 4838129664 | bytes 14170112 | tf_op jit(solution)/shard_map/td,tf->df/dot_general | solution.py:765
  271.8 2.5 convolution_convert_fusion.4.refs_0_
  274.3 88.0 %shard_map.154 = (f32[24,768]{1,0:T(8,128)}, f32[24,3072]{1,0:T(8,128)}, f32[96,768]{1,0:T(8,128)}, bf16[1024,768]{1,0:T(8,128)(2,1)}) custom-call(bf16[768,768]{1,0:T(8,128)(2,1)} %convolution_convert_fusion.4.refs_0_, bf16[768,3072]{1,0:T(8,128)(2,1)} %convolution_convert_fusion.1.refs_1_, bf16[3072,768]{1,0:T(8,128)(2,1)} %convolution_convert_fusion.refs_2_, ...), custom_call_target="tpu_custom_call" | custom-call | tf_op jit(solution)/shard_map/pallas_call | solution.py:705
  362.4 3.8 convolution_convert_fusion.3.dm_ref
  366.3 34.9 %shard_map.155 = (bf16[1024,768]{1,0:T(8,128)(2,1)}, bf16[1024,768]{1,0:T(8,128)(2,1)}, bf16[1024,768]{1,0:T(8,128)(2,1)}, f32[48,384]{1,0:T(8,128)}) custom-call(bf16[1024,768]{1,0:T(8,128)(2,1)} %convolution_convert_fusion.3.dm_ref, s32[6,8,256]{2,1,0:T(8,128)} %bitcast.56, bf16[6,2,8,128,384]{4,3,2,1,0:T(8,128)(2,1)} %get-tuple-element.35.slot_ref, ...), custom_call_target="tpu_custom_call" | custom-call | tf_op jit(solution)/shard_map/pallas_call | solution.py:774
  403.9 1.7 constant_dynamic-update-slice_fusion.2
  406.1 1.6 copy-done.11
  407.8 4.9 %add_convert_fusion.2.refs_1_ = bf16[1024,768]{1,0:T(8,128)(2,1)} fusion(f32[1024,768]{1,0:T(8,128)S(1)} %copy-done.3, bf16[1024,2304]{1,0:T(8,128)(2,1)S(1)} %constant_dynamic-update-slice_fusion, bf16[768,2560]{1,0:T(8,128)(2,1)S(1)} %copy-done.11), kind=kOutput, calls=%fused_computation.36 | convolution fusion | flops 3625451520 | bytes 12976128 | tf_op jit(solution)/shard_map/tf,df->td/dot_general | solution.py:784
  412.7 4.2 convolution_convert_fusion.2
  416.9 2.2 pad_maximum_fusion.refs_0_
  419.1 49.8 %shard_map.156 = (f32[24,2560]{1,0:T(8,128)}, bf16[1024,768]{1,0:T(8,128)(2,1)}) custom-call(bf16[768,2560]{1,0:T(8,128)(2,1)} %pad_maximum_fusion.refs_0_, bf16[1024,768]{1,0:T(8,128)(2,1)} %add_convert_fusion.2.refs_1_), custom_call_target="tpu_custom_call" | custom-call | tf_op jit(solution)/shard_map/pallas_call | solution.py:705
  469.0 1.4 slice_bitcast_fusion.3
  471.1 1.6 slice.79
  473.4 1.1 copy.51
  474.5 1.1 copy.52
  (91 shorter events, 13.6 us)
Async XLA Ops:
  123.5 2.7 copy-start.12
  133.7 36.9 %copy-start.15 = (bf16[768,768]{1,0:T(8,128)(2,1)S(1)}, bf16[768,768]{1,0:T(8,128)(2,1)}, u32[]{:S(2)}) copy-start(bf16[768,768]{1,0:T(8,128)(2,1)} %get-tuple-element.30) | copy-start | bytes 3538948
  170.5 42.0 %slice-start = ((s8[4718592]{0:T(1024)(128)(4,1)}), s8[4194304]{0:T(1024)(128)(4,1)S(1)}, s32[]{:S(2)}) async-start(s8[4718592]{0:T(1024)(128)(4,1)} %bitcast.63), calls=%async_computation | async-start | bytes 8388608
  174.7 37.9 %slice-start.1 = ((s8[4718592]{0:T(1024)(128)(4,1)}), s8[524288]{0:T(1024)(128)(4,1)S(1)}, s32[]{:S(2)}) async-start(s8[4718592]{0:T(1024)(128)(4,1)} %bitcast.63), calls=%async_computation.1 | async-start | bytes 1048576
  212.6 5.5 %copy-start.17 = (bf16[1024,3072]{1,0:T(8,128)(2,1)}, bf16[1024,3072]{1,0:T(8,128)(2,1)S(1)}, u32[]{:S(2)}) copy-start(bf16[1024,3072]{1,0:T(8,128)(2,1)S(1)} %get-tuple-element.90) | copy-start | bytes 18874372
  218.1 1.4 copy-start
  243.4 10.5 %copy-start.1 = (f32[1024,768]{1,0:T(8,128)S(1)}, f32[1024,768]{1,0:T(8,128)}, u32[]{:S(2)}) copy-start(f32[1024,768]{1,0:T(8,128)} %get-tuple-element.87) | copy-start | bytes 9437188
  243.4 10.5 %copy-start.16 = (bf16[1024,3072]{1,0:T(8,128)(2,1)S(1)}, bf16[1024,3072]{1,0:T(8,128)(2,1)}, u32[]{:S(2)}) copy-start(bf16[1024,3072]{1,0:T(8,128)(2,1)} %get-tuple-element.102) | copy-start | bytes 18874372
  263.5 8.3 %copy-start.2 = (f32[1024,768]{1,0:T(8,128)}, f32[1024,768]{1,0:T(8,128)S(1)}, u32[]{:S(2)}) copy-start(f32[1024,768]{1,0:T(8,128)S(1)} %get-tuple-element.89) | copy-start | bytes 9437188
  263.5 8.3 %copy-start.14 = (bf16[1024,768]{1,0:T(8,128)(2,1)S(1)}, bf16[1024,768]{1,0:T(8,128)(2,1)}, u32[]{:S(2)}) copy-start(bf16[1024,768]{1,0:T(8,128)(2,1)} %get-tuple-element.29) | copy-start | bytes 4718596
  274.3 88.1 %copy-start.3 = (f32[1024,768]{1,0:T(8,128)S(1)}, f32[1024,768]{1,0:T(8,128)}, u32[]{:S(2)}) copy-start(f32[1024,768]{1,0:T(8,128)} %copy-done.2) | copy-start | bytes 9437188
  403.6 1.9 copy-start.6
  403.7 2.3 copy-start.5
  405.5 2.2 copy-start.11
  407.8 4.9 %copy-start.13 = (bf16[1024,768]{1,0:T(8,128)(2,1)S(1)}, bf16[1024,768]{1,0:T(8,128)(2,1)}, u32[]{:S(2)}) copy-start(bf16[1024,768]{1,0:T(8,128)(2,1)} %get-tuple-element.27) | copy-start | bytes 4718596
  419.1 54.3 %copy-start.4 = (bf16[1024,768]{1,0:T(8,128)(2,1)S(1)}, bf16[1024,768]{1,0:T(8,128)(2,1)}, u32[]{:S(2)}) copy-start(bf16[1024,768]{1,0:T(8,128)(2,1)} %get-tuple-element.113) | copy-start | bytes 4718596
  469.0 5.6 %copy-start.7 = (bf16[1024,768]{1,0:T(8,128)(2,1)S(1)}, bf16[1024,768]{1,0:T(8,128)(2,1)}, u32[]{:S(2)}) copy-start(bf16[1024,768]{1,0:T(8,128)(2,1)} %get-tuple-element.114) | copy-start | bytes 4718596
  469.0 6.7 %copy-start.10 = (f32[24,768]{1,0:T(8,128)S(1)}, f32[24,768]{1,0:T(8,128)}, u32[]{:S(2)}) copy-start(f32[24,768]{1,0:T(8,128)} %get-tuple-element.116) | copy-start | bytes 221188
  472.7 4.3 copy-start.8
  473.4 2.9 copy-start.9

commit v2 on v1

--- a/solution.py
+++ b/solution.py
@@ -282,6 +282,11 @@
                 n += 1
         pl.semaphore_wait(barrier, n)
 
+    def go(self, *makers):
+        for make in makers:
+            make().start()
+            self.drains.append(lambda make=make: make().wait_send())
+
     def drain(self):
         for d in self.drains:
             d()
@@ -305,7 +310,7 @@
     fr = [None] + [L.new() for _ in range(3)]
     fl = [None] + [L.new() for _ in range(3)]
     ax, by, ay, bx0, bx1, c0, c1, c2 = [L.new() for _ in range(8)]
-    first = L.copy(i0, shard.at[:, other], half_buf, L.dp, L.sib)
+    first = lambda: L.copy(i0, shard.at[:, other], half_buf, L.dp, L.sib)
 
     def right(d, z0):
         return L.copy(fr[d], full.at[chip(z0), mine], full.at[chip(z0), mine], L.dp, L.sq + 2)
@@ -345,11 +350,10 @@
         return L.copy(i, ref, ref, dp, sq)
 
     def s0():
-        first.start()
-        L.drains.append(first.wait_send)
+        L.go(first)
 
     def s1():
-        first.wait_recv()
+        first().wait_recv()
         own, got = shard[:, mine], half_buf[...]
 
         @pl.when(L.core == 0)
@@ -372,28 +376,24 @@
         send_line(3)
         L.drains.append(functools.partial(drain_line, 3))
 
-    def go(cs):
-        for c in cs:
-            c.start()
-            L.drains.append(c.wait_send)
-
     def s4():
         recv_line(3)
-        q = quarter(L.dp)
-        go([same(ax, q, cols_a, L.dp_x, L.sq), same(by, q, cols_b, L.dp_y, L.sq), same(c0, q, mine, L.dp, L.sib)])
+        q = lambda: quarter(L.dp)
+        L.go(lambda: same(ax, q(), cols_a, L.dp_x, L.sq), lambda: same(by, q(), cols_b, L.dp_y, L.sq),
+             lambda: same(c0, q(), mine, L.dp, L.sib))
 
     def s5():
         same(ax, quarter(L.dp_x), cols_a, L.dp_x, L.sq).wait_recv()
-        go([same(ay, quarter(2 * L.y, 2), cols_a, L.dp_y, L.sq)])
+        L.go(lambda: same(ay, quarter(2 * L.y, 2), cols_a, L.dp_y, L.sq))
         same(by, quarter(L.dp_y), cols_b, L.dp_y, L.sq).wait_recv()
-        go([same(bx0, quarter(L.dp), cols_b, L.dp_x, L.sq), same(bx1, quarter(L.dp_y), cols_b, L.dp_x, L.sq)])
+        L.go(lambda: same(bx0, quarter(L.dp), cols_b, L.dp_x, L.sq), lambda: same(bx1, quarter(L.dp_y), cols_b, L.dp_x, L.sq))
 
     def s6():
         same(bx0, quarter(L.dp_x), cols_b, L.dp_x, L.sq).wait_recv()
-        go([same(c1, quarter(L.dp_x), mine, L.dp, L.sib)])
+        L.go(lambda: same(c1, quarter(L.dp_x), mine, L.dp, L.sib))
         same(ay, quarter(2 * (1 - L.y), 2), cols_a, L.dp_y, L.sq).wait_recv()
         same(bx1, quarter(3 - L.dp), cols_b, L.dp_x, L.sq).wait_recv()
-        go([same(c2, quarter(2 * (1 - L.y), 2), mine, L.dp, L.sib)])
+        L.go(lambda: same(c2, quarter(2 * (1 - L.y), 2), mine, L.dp, L.sib))
 
     def s7():
         same(c0, quarter(L.dp), other, L.dp, L.sib).wait_recv()
@@ -413,9 +413,7 @@
     def begin():
         keep.start()
         for j in range(1, 2 * NZ):
-            c = move(j, lax.rem(L.sq + j, 2 * NZ), L.sq)
-            c.start()
-            L.drains.append(c.wait_send)
+            L.go(lambda j=j: move(j, lax.rem(L.sq + j, 2 * NZ), L.sq))
 
     def finish():
         keep.wait()
@@ -461,23 +459,18 @@
     q = lambda dp: dp * NZ * big
     other_y = quarter(2 * (1 - L.y), 2)
 
-    def go(*cs):
-        for c in cs:
-            c.start()
-            L.drains.append(c.wait_send)
-
-    core_copy = L.copy(i0, part.at[:, other], acc, L.dp, L.sib)
-    a1_copy = L.copy(ia1, acc.at[other_y, ca], a1, L.dp_y, L.sq)
-    bx_copy = L.copy(ibx, acc.at[quarter(L.dp_x), cb], b1x, L.dp_x, L.sq)
-    by_copy = L.copy(iby, acc.at[quarter(3 - L.dp), cb], b1y, L.dp_x, L.sq)
-    a2_copy = L.copy(ia2, acc.at[quarter(L.dp_x), ca], a2, L.dp_x, L.sq)
-    b2_copy = L.copy(ib2, acc.at[quarter(L.dp_y), cb], b2, L.dp_y, L.sq)
+    core_copy = lambda: L.copy(i0, part.at[:, other], acc, L.dp, L.sib)
+    a1_copy = lambda: L.copy(ia1, acc.at[other_y, ca], a1, L.dp_y, L.sq)
+    bx_copy = lambda: L.copy(ibx, acc.at[quarter(L.dp_x), cb], b1x, L.dp_x, L.sq)
+    by_copy = lambda: L.copy(iby, acc.at[quarter(3 - L.dp), cb], b1y, L.dp_x, L.sq)
+    a2_copy = lambda: L.copy(ia2, acc.at[quarter(L.dp_x), ca], a2, L.dp_x, L.sq)
+    b2_copy = lambda: L.copy(ib2, acc.at[quarter(L.dp_y), cb], b2, L.dp_y, L.sq)
 
     def s0():
-        go(core_copy)
+        L.go(core_copy)
 
     def s1():
-        core_copy.wait_recv()
+        core_copy().wait_recv()
         step = 48
 
         def one(i, _):
@@ -485,22 +478,22 @@
             acc[here, :] = (acc[here, :].astype(jnp.float32) + part[here, mine].astype(jnp.float32)).astype(jnp.bfloat16)
             return 0
         lax.fori_loop(0, acc.shape[0] // step, one, 0)
-        go(a1_copy, bx_copy, by_copy)
+        L.go(a1_copy, bx_copy, by_copy)
 
     def s2():
-        a1_copy.wait_recv()
+        a1_copy().wait_recv()
         add_into(acc, q(2 * L.y), ca, a1, 8 * big)
-        go(a2_copy)
-        bx_copy.wait_recv()
-        by_copy.wait_recv()
+        L.go(a2_copy)
+        bx_copy().wait_recv()
+        by_copy().wait_recv()
         add_into(acc, q(L.dp_y), cb, b1y, 4 * big)
-        go(b2_copy)
+        L.go(b2_copy)
         add_into(acc, q(L.dp), cb, b1x, 4 * big)
 
     def s3():
-        a2_copy.wait_recv()
+        a2_copy().wait_recv()
         add_into(acc, q(L.dp), ca, a2, 4 * big)
-        b2_copy.wait_recv()
+        b2_copy().wait_recv()
         add_into(acc, q(L.dp), cb, b2, 4 * big)
 
     full_cols = pl.ds(0, half)
@@ -547,7 +540,7 @@
                     hop_l(t, from_r.at[t]).wait_send()
         L.drains.append(drain)
 
-    fin_copy = L.copy(ifin, fin.at[1 - L.core], got, L.dp, L.sib)
+    fin_copy = lambda: L.copy(ifin, fin.at[1 - L.core], got, L.dp, L.sib)
 
     def s7():
         for z in range(NZ):
@@ -561,11 +554,11 @@
                     hop_l(z, from_r.at[z]).wait_recv()
                     total = total + from_r[z].astype(jnp.float32)
                 fin[...] = total.reshape(2, r, half)
-        go(fin_copy)
+        L.go(fin_copy)
 
     def s8():
         out[:, mine] = fin[L.core]
-        fin_copy.wait_recv()
+        fin_copy().wait_recv()
         out[:, other] = got[...]
     return [s0, s1, s2, s3] + [functools.partial(line, s) for s in range(3)] + [s7, s8]
 
@@ -583,6 +576,13 @@
 
 def dot(a, b, ca, cb):
     return lax.dot_general(a, b, (((ca,), (cb,)), ((), ())), preferred_element_type=jnp.float32)
+
+
+def bdot(a, b, ca, cb):
+    return lax.dot_general(a, b, (((ca,), (cb,)), ((0,), (0,))), preferred_element_type=jnp.float32)
+
+
+BATCH = 8
 
 
 def attend_fwd(scale, q_ref, k_ref, v_ref, perm_ref, mixed_ref, slot_ref, prob_ref, head_ref):
@@ -596,13 +596,14 @@
         moved = jnp.where(keep, dot(table, packed, 0, 0), 0.0).astype(jnp.bfloat16)
         slot_ref[0, :, :, pl.ds(k * share, share), :] = moved.reshape(2, nblk, share, 384)
     for h in range(2):
-        for c in range(nblk):
-            q, kk, v = slot_ref[0, h, c, :, 0:128], slot_ref[0, h, c, :, 128:256], slot_ref[0, h, c, :, 256:384]
-            scores = dot(q, kk, 1, 1) * scale
+        for c in range(0, nblk, BATCH):
+            cs = pl.ds(c, BATCH)
+            q, kk, v = slot_ref[0, h, cs, :, 0:128], slot_ref[0, h, cs, :, 128:256], slot_ref[0, h, cs, :, 256:384]
+            scores = bdot(q, kk, 2, 2) * scale
             e = jnp.exp(scores - jnp.max(scores, axis=-1, keepdims=True))
-            probs = (e / jnp.sum(e, axis=-1, keepdims=True)).astype(jnp.bfloat16)
-            prob_ref[0, h, c] = probs
-            head_ref[h, c] = dot(probs, v, 1, 0).astype(jnp.bfloat16)
+            probs = (e * (1.0 / jnp.sum(e, axis=-1, keepdims=True))).astype(jnp.bfloat16)
+            prob_ref[0, h, cs] = probs
+            head_ref[h, cs] = bdot(probs, v, 2, 1).astype(jnp.bfloat16)
     for k in range(nblk):
         table = one_hot(perm_ref[0, k:k + 1, :], BLK)
         back = head_ref[:, :, pl.ds(k * share, share), :].reshape(2 * BLK, BLK)
@@ -618,16 +619,17 @@
         moved = jnp.where(keep, dot(table, dm_ref[pl.ds(k * BLK, BLK), :], 0, 0), 0.0).astype(jnp.bfloat16)
         up_ref[:, :, pl.ds(k * share, share), :] = moved.reshape(2, nblk, share, 128)
     for h in range(2):
-        for c in range(nblk):
-            q, kk, v = slot_ref[0, h, c, :, 0:128], slot_ref[0, h, c, :, 128:256], slot_ref[0, h, c, :, 256:384]
-            probs, up = prob_ref[0, h, c], up_ref[h, c]
-            dprobs = dot(up, v, 1, 1)
+        for c in range(0, nblk, BATCH):
+            cs = pl.ds(c, BATCH)
+            q, kk, v = slot_ref[0, h, cs, :, 0:128], slot_ref[0, h, cs, :, 128:256], slot_ref[0, h, cs, :, 256:384]
+            probs, up = prob_ref[0, h, cs], up_ref[h, cs]
+            dprobs = bdot(up, v, 2, 2)
             p32 = probs.astype(jnp.float32)
-            inner = jnp.sum(p32 * dprobs, axis=-1, keepdims=True)
-            dscores = (p32 * (dprobs - inner)).astype(jnp.bfloat16)
-            grad_ref[h, c, :, 0:128] = (dot(dscores, kk, 1, 0) * scale).astype(jnp.bfloat16)
-            grad_ref[h, c, :, 128:256] = (dot(dscores, q, 0, 0) * scale).astype(jnp.bfloat16)
-            grad_ref[h, c, :, 256:384] = dot(probs, up, 0, 0).astype(jnp.bfloat16)
+            pd = p32 * dprobs
+            dscores = (pd - p32 * jnp.sum(pd, axis=-1, keepdims=True)).astype(jnp.bfloat16)
+            grad_ref[h, cs, :, 0:128] = (bdot(dscores, kk, 2, 1) * scale).astype(jnp.bfloat16)
+            grad_ref[h, cs, :, 128:256] = (bdot(dscores, q, 1, 1) * scale).astype(jnp.bfloat16)
+            grad_ref[h, cs, :, 256:384] = bdot(probs, up, 1, 1).astype(jnp.bfloat16)
     total = jnp.zeros((1, 384), jnp.float32)
     for k in range(nblk):
         table = one_hot(perm_ref[0, k:k + 1, :], BLK)
@@ -659,7 +661,7 @@
     for k in range(8):
         for p in progs:
             p[k]()
-        if k == 3:
+        if k == 5:
             for b, _ in sp:
                 b()
     for _, f in sp:
@@ -710,6 +712,172 @@
     )(*parts, *rows)
 
 
+def loop(n, body, hooks=()):
+    def one(i, _):
+        body(i)
+        for at, stage in hooks:
+            pl.when(i == at)(stage)
+        return 0
+    lax.fori_loop(0, n, one, 0)
+
+
+def moments(v):
+    mean = jnp.mean(v, axis=-1, keepdims=True)
+    centred = v - mean
+    inv = lax.rsqrt(jnp.mean(centred * centred, axis=-1, keepdims=True) + epsilon)
+    return centred * inv, inv
+
+
+TB = 256
+FB = 512
+
+
+def dense_kernel(mixed, x, w_out, w_up, down_shard, up_rows, vec, ub,
+                 d_res, d_mixed, g_up, g_out, sums, ubsum, out_rows, r_down,
+                 w_down, half_buf, n1, s1, low, act, gp, up, outb, dn, da, gd, *rest):
+    red, (ss, rs, ls, cs) = rest[:10], rest[10:]
+    rows_here, width = x.shape
+    ff = w_up.shape[1]
+    L = Links(ss, rs)
+    L.enter()
+    ga = gather(L, down_shard, w_down, half_buf, SIZES["down"][0], SIZES["down"][2])
+    up_begin, up_finish = spread(L, up_rows, up, ls.at[0])
+    out_begin, out_finish = spread(L, outb, out_rows, ls.at[1])
+    rd = reduce(L, gd, r_down, red, SIZES["down"][0], SIZES["down"][2])
+    sums[...] = jnp.zeros_like(sums)
+    ubsum[...] = jnp.zeros_like(ubsum)
+    row = lambda i: vec[i:i + 1, :]
+    ga[0]()
+    ga[1]()
+
+    def first_half(m):
+        here = pl.ds(mult(m * TB, TB), TB)
+        r1 = x[here, :].astype(jnp.float32) + dot(mixed[here, :], w_out[...], 1, 0) + row(2)
+        norm, inv = moments(r1)
+        n1[here, :] = norm
+        s1[here, :] = inv
+        lo = (norm * row(4) + row(5)).astype(jnp.bfloat16)
+        low[here, :] = lo
+        for f in range(0, ff, FB):
+            c = pl.ds(f, FB)
+            wide = dot(lo, w_up[:, c], 1, 0) + ub[:, c]
+            cdf = 0.5 + 0.5 * lax.erf(wide * 0.7071067811865476)
+            act[here, c] = (wide * cdf).astype(jnp.bfloat16)
+            gp[here, c] = (cdf + wide * (0.3989422804014327 * jnp.exp(-0.5 * wide * wide))).astype(jnp.bfloat16)
+
+    loop(rows_here // TB, first_half, HOOK_A(ga, up_begin))
+    for stage in REST_A(ga):
+        stage()
+    up_finish()
+
+    def second_half(m):
+        here = pl.ds(mult(m * TB, TB), TB)
+        first = n1[here, :] * row(4) + row(5)
+        r2 = first + dot(act[here, :], w_down[...], 1, 0) + row(3)
+        n2, s2 = moments(r2)
+        outb[here, :] = (n2 * row(6) + row(7)).astype(jnp.bfloat16)
+        g = up[here, :].astype(jnp.float32)
+        sums[4:5, :] += jnp.sum(g * n2, axis=0, keepdims=True)
+        sums[5:6, :] += jnp.sum(g, axis=0, keepdims=True)
+        d = norm_back(g, n2, s2, row(6))
+        d_res[here, :] = d
+        lo = d.astype(jnp.bfloat16)
+        dn[here, :] = lo
+        sums[1:2, :] += jnp.sum(lo.astype(jnp.float32), axis=0, keepdims=True)
+
+    loop(rows_here // TB, second_half)
+    out_begin()
+
+    def grad_down(i):
+        c = pl.ds(mult(i * FB, FB), FB)
+        gd[c, :] = dot(act[:, c], dn[...], 0, 0).astype(jnp.bfloat16)
+
+    loop(ff // FB, grad_down)
+    rd[0]()
+
+    def third(m):
+        here = pl.ds(mult(m * TB, TB), TB)
+        total = d_res[here, :]
+        lo = dn[here, :]
+        for f in range(0, ff, FB):
+            c = pl.ds(f, FB)
+            dw = (dot(lo, w_down[c, :], 1, 1) * gp[here, c].astype(jnp.float32)).astype(jnp.bfloat16)
+            gp[here, c] = dw
+            ubsum[0:1, c] += jnp.sum(dw.astype(jnp.float32), axis=0, keepdims=True)
+            total = total + dot(dw, w_up[:, c], 1, 1)
+        norm = n1[here, :]
+        sums[2:3, :] += jnp.sum(total * norm, axis=0, keepdims=True)
+        sums[3:4, :] += jnp.sum(total, axis=0, keepdims=True)
+        d = norm_back(total, norm, s1[here, :], row(4))
+        d_res[here, :] = d
+        lo = d.astype(jnp.bfloat16)
+        da[here, :] = lo
+        sums[0:1, :] += jnp.sum(lo.astype(jnp.float32), axis=0, keepdims=True)
+        d_mixed[here, :] = dot(lo, w_out[...], 1, 1).astype(jnp.bfloat16)
+
+    loop(rows_here // TB, third, HOOK_C(rd))
+
+    def grad_up(i):
+        c = pl.ds(mult(i * FB, FB), FB)
+        act[pl.ds(0, width), c] = dot(low[...], gp[:, c], 0, 0).astype(jnp.bfloat16)
+
+    loop(ff // FB, grad_up, HOOK_D(rd))
+    flush = pltpu.make_async_copy(act.at[pl.ds(0, width), :], g_up, cs.at[0])
+    flush.start()
+    g_out[...] = dot(mixed[...], da[...], 0, 0).astype(jnp.bfloat16)
+    for stage in REST_D(rd):
+        stage()
+    out_finish()
+    flush.wait()
+    L.drain()
+
+
+def HOOK_A(ga, up_begin):
+    return [(0, ga[2]), (1, ga[3]), (2, ga[4]), (2, up_begin), (3, ga[5])]
+
+
+def REST_A(ga):
+    return ga[6:]
+
+
+def HOOK_C(rd):
+    return [(0, rd[1]), (1, rd[2]), (2, rd[3]), (3, rd[4])]
+
+
+def HOOK_D(rd):
+    return [(0, rd[5]), (2, rd[6]), (4, rd[7])]
+
+
+def REST_D(rd):
+    return rd[8:]
+
+
+def dense_call(mixed, x, w_out, w_up, w_down, upstream, vec, ub):
+    rows_here, width = x.shape
+    ff = w_up.shape[1]
+    r, cols, split = SIZES["down"]
+    count = 15 + 14 + N_REDUCE
+    f32 = lambda *s: jax.ShapeDtypeStruct(s, jnp.float32)
+    bf = lambda *s: jax.ShapeDtypeStruct(s, BF)
+    vbf = lambda *s: pltpu.VMEM(s, BF)
+    vf = lambda *s: pltpu.VMEM(s, jnp.float32)
+    hbm = pl.BlockSpec(memory_space=pl.ANY)
+    return pl.pallas_call(
+        dense_kernel,
+        out_shape=[f32(rows_here, width), bf(rows_here, width), bf(width, ff), bf(width, width), f32(8, width), f32(8, ff),
+                   bf(rows_here, width), f32(r, cols)],
+        in_specs=[VM] * 5 + [hbm] + [VM] * 2,
+        out_specs=[VM, VM, hbm] + [VM] * 5,
+        scratch_shapes=[vbf(ff, width), vbf(r, cols // 2), vf(rows_here, width), vf(rows_here, 1), vbf(rows_here, width),
+                        vbf(rows_here, ff), vbf(rows_here, ff), vbf(rows_here, width), vbf(rows_here, width),
+                        vbf(rows_here, width), vbf(rows_here, width), vbf(ff, width)]
+        + reduce_scratch(r, cols, split)
+        + [pltpu.SemaphoreType.DMA((count,)), pltpu.SemaphoreType.DMA((count,)), pltpu.SemaphoreType.DMA((2,)),
+           pltpu.SemaphoreType.DMA((1,))],
+        compiler_params=pltpu.CompilerParams(collective_id=1, has_side_effects=True, vmem_limit_bytes=62 * 2**20),
+    )(mixed, x, w_out, w_up, w_down, upstream, vec, ub)
+
+
 def slot_rows(route, me):
     heads, n = route.shape[0], 2 * NZ
     per = route.reshape(heads, n, -1)
@@ -727,8 +895,8 @@
     pairs = H // 2
     scale = (width // H) ** -0.5
     aux = jnp.pad(vectors.T, ((0, 0), (0, 248))) + jnp.pad(up_bias[None, :], ((0, 23), (8, 152)))
-    full_qkv, full_out, full_up, full_down, x, g = gather_call(
-        ("qkv", "out", "up", "down"), [jnp.concatenate([w_qkv, aux], axis=1), w_out, w_up, w_down], [tokens, upstream])
+    full_qkv, full_out, full_up, x = gather_call(
+        ("qkv", "out", "up"), [jnp.concatenate([w_qkv, aux], axis=1), w_out, w_up], [tokens])
     perm = slot_rows(cluster_route[0], me)
     vec = full_qkv[:, 2304:2312].T.astype(jnp.float32)
     ub = full_qkv[::24, 2312:2408].reshape(-1).astype(jnp.float32)
@@ -747,30 +915,7 @@
         scratch_shapes=[pltpu.VMEM((2, 8, BLK, BLK), BF)],
         compiler_params=pltpu.CompilerParams(vmem_limit_bytes=LIMIT),
     )(qkv, qkv, qkv, perm)
-    attention = jnp.dot(mixed, full_out, preferred_element_type=jnp.float32) + vec[2]
-    first, n1, s1 = normalize(x.astype(jnp.float32) + attention, vec[4], vec[5])
-    low = first.astype(BF)
-    wide = jnp.dot(low, full_up, preferred_element_type=jnp.float32) + ub
-    act, pull = jax.vjp(exact_gelu, wide)
-    act = act.astype(BF)
-    narrow = jnp.dot(act, full_down, preferred_element_type=jnp.float32) + vec[3]
-    out, n2, s2 = normalize(first + narrow, vec[6], vec[7])
-    gf = g.astype(jnp.float32)
-    gain2, shift2 = jnp.sum(gf * n2, axis=0), jnp.sum(gf, axis=0)
-    d_second = norm_back(gf, n2, s2, vec[6])
-    d_narrow = d_second.astype(BF)
-    g_down = jnp.einsum("tf,td->fd", act, d_narrow, preferred_element_type=jnp.float32).astype(BF)
-    down_bias = jnp.sum(d_narrow.astype(jnp.float32), axis=0)
-    d_wide = pull(jnp.einsum("td,fd->tf", d_narrow, full_down, preferred_element_type=jnp.float32))[0].astype(BF)
-    g_up = jnp.einsum("td,tf->df", low, d_wide, preferred_element_type=jnp.float32).astype(BF)
-    g_ub = jnp.sum(d_wide.astype(jnp.float32), axis=0)
-    d_first = d_second + jnp.einsum("tf,df->td", d_wide, full_up, preferred_element_type=jnp.float32)
-    gain1, shift1 = jnp.sum(d_first * n1, axis=0), jnp.sum(d_first, axis=0)
-    d_res = norm_back(d_first, n1, s1, vec[4])
-    d_attn = d_res.astype(BF)
-    g_out = jnp.einsum("td,te->de", mixed, d_attn, preferred_element_type=jnp.float32).astype(BF)
-    out_bias = jnp.sum(d_attn.astype(jnp.float32), axis=0)
-    d_mixed = jnp.einsum("te,de->td", d_attn, full_out, preferred_element_type=jnp.float32).astype(BF)
+    d_res, d_mixed, g_up, g_out, sums1, ubsum, out_rows, r_down = dense_call(mixed, x, full_out, full_up, w_down, upstream, vec, ub[None])
     dq, dk, dv, sums = pl.pallas_call(
         functools.partial(attend_bwd, scale), grid=(pairs,),
         out_shape=[jax.ShapeDtypeStruct((rows_here, width), BF)] * 3 + [jax.ShapeDtypeStruct((8 * pairs, 384), jnp.float32)],
@@ -782,12 +927,11 @@
     d_proj = jnp.concatenate([dq, dk, dv], axis=1)
     g_qkv = jnp.einsum("td,tf->df", x, d_proj, preferred_element_type=jnp.float32).astype(BF)
     gx = (jnp.einsum("tf,df->td", d_proj, w, preferred_element_type=jnp.float32) + d_res).astype(BF)
-    g_vec = jnp.stack([sums[:, 0].reshape(-1), sums[:, 2].reshape(-1), out_bias, down_bias, gain1, shift1, gain2, shift2])
+    g_vec = jnp.concatenate([sums[:, 0].reshape(1, -1), sums[:, 2].reshape(1, -1), sums1[:6]])
     g_aux = jnp.pad(g_vec.T, ((0, 0), (0, 248)))
-    g_aux = g_aux.reshape(32, 24, 256) + jnp.pad(g_ub.reshape(32, 1, 96), ((0, 0), (0, 23), (8, 152)))
+    g_aux = g_aux.reshape(32, 24, 256) + jnp.pad(ubsum[0].reshape(32, 1, 96), ((0, 0), (0, 23), (8, 152)))
     part = jnp.concatenate([g_qkv, g_aux.reshape(768, 256).astype(BF)], axis=1)
-    r_out, r_up, r_down, out_rows = reduce_call(("out", "up", "down"), [g_out, g_up, g_down], [out.astype(BF)], 1)
-    r_qkv, gx_rows = reduce_call(("qkv",), [part], [gx], 2)
+    r_out, r_up, r_qkv, gx_rows = reduce_call(("out", "up", "qkv"), [g_out, g_up, part], [gx], 2)
     return (out_rows, gx_rows, r_qkv[:, :2304], r_out, r_up, r_down, r_qkv[:, 2304:2312].T, r_qkv[0, 2312:2408])
 
 

time: 487 us -> 374 us (0.77); the launches traced: 478 us -> 373 us
  matrix products: 118 us -> 18.5 us
  other arithmetic: 18.8 us -> 11.1 us
    pallas_call x0 -> x1, Pallas kernels: none -> 130 us  [dense_call(): pl.pallas_call(dense_kernel, out_shape=[f32(rows_here, width), bf(rows_he...]
    dot_general x9 -> x0, matrix products: 99.2 us -> none  [the longest x1 37.9 us: homes(): wide = jnp.dot(low, full_up, preferred_element_type=jnp.float32) + ub]
    pallas_call x2 -> x1, Pallas kernels: 138 us -> 84.4 us  [reduce_call(): pl.pallas_call(functools.partial(reduce_kernel, names, na), out_shape=out...]
    pallas_call x1, Pallas kernels: 110 us -> 75 us  [gather_call(): pl.pallas_call(functools.partial(gather_kernel, names, na), out_shape=out...]
    pallas_call x1, Pallas kernels: 36.9 us -> 14 us  [homes(): pl.pallas_call(functools.partial(attend_fwd, scale), grid=(pairs,), out_s...]
    pallas_call x1, Pallas kernels: 34.9 us -> 14.3 us  [homes(): pl.pallas_call(functools.partial(attend_bwd, scale), grid=(pairs,), out_s...]
    reduce_sum x5 -> x0, other arithmetic: 7.32 us -> none  [the longest x1 2.78 us: homes(): gain2, shift2 = (jnp.sum(gf * n2, axis=0), jnp.sum(gf, axis=0))]
    pallas_call x0 -> x1, local copies, waits for them, and re-layouts: none -> 6.38 us  [gather_call(): pl.pallas_call(functools.partial(gather_kernel, names, na), out_shape=out...]
where the time goes in v2:
time: 374 us; the launch traced here: 373 us
  Pallas kernels  318 us (85%)
  local copies, waits for them, and re-layouts  24.6 us (7%)
  matrix products  18.5 us (5%)
  other arithmetic  11.1 us (3%)
    pallas_call x1, Pallas kernels, dense_call(): pl.pallas_call(dense_kernel, out_shape=[f32(rows_here, width), bf(rows_he...  130 us
    pallas_call x1, Pallas kernels, reduce_call(): pl.pallas_call(functools.partial(reduce_kernel, names, na), out_shape=out...  84.4 us
    pallas_call x1, Pallas kernels, gather_call(): pl.pallas_call(functools.partial(gather_kernel, names, na), out_shape=out...  75 us
    pallas_call x1, Pallas kernels, homes(): pl.pallas_call(functools.partial(attend_bwd, scale), grid=(pairs,), out_s...  14.3 us
    pallas_call x1, Pallas kernels, homes(): pl.pallas_call(functools.partial(attend_fwd, scale), grid=(pairs,), out_s...  14 us
    unnamed x40, local copies, waits for them, and re-layouts  10.2 us
    dot_general x1, matrix products, homes(): jnp.dot(x, w, preferred_element_type=jnp.float32) + shifts  7.54 us

profile of v2, /device:TPU:1, one launch (start us, length us, event | category | flops | bytes accessed | tf_op | source)
XLA Modules:
  0.0 372.9 jit_solution(7244989401460821348)
XLA Ops:
  0.6 0.8 copy.32
  1.4 0.7 pad_add_fusion
  2.1 1.6 pad_maximum_fusion.1.refs_0_
  3.7 1.9 reduce.2
  6.0 3.4 reduce-window.6
  10.2 1.9 fusion.10
  12.1 75.0 %shard_map.152 = (bf16[768,2560]{1,0:T(8,128)(2,1)}, bf16[768,768]{1,0:T(8,128)(2,1)}, bf16[768,3072]{1,0:T(8,128)(2,1)}, bf16[1024,768]{1,0:T(8,128)(2,1)}) custom-call(bf16[24,2560]{1,0:T(8,128)(2,1)} %pad_maximum_fusion.1.refs_0_, bf16[24,768]{1,0:T(8,128)(2,1)} %refs_1_.1, bf16[24,3072]{1,0:T(8,128)(2,1)} %refs_2_.1, bf16[1024,768]{1,0:T(8,128)(2,1)} %refs_3_.1), custom_call_target="tpu_custom_call" | custom-call | tf_op jit(solution)/shard_map/pallas_call | solution.py:677
  87.1 1.0 slice.55
  88.2 0.7 reshape.78.ub
  88.9 6.4 %copy.33 = bf16[768,2560]{0,1:T(8,128)(2,1)} copy(bf16[768,2560]{1,0:T(8,128)(2,1)} %get-tuple-element.32) | data formatting | bytes 7864320 | tf_op jit(solution)/shard_map/pallas_call | solution.py:677
  95.3 0.7 convert_bitcast_fusion.vec
  96.0 7.5 %add_convert_fusion.q_ref.k_ref.v_ref = bf16[1024,2304]{1,0:T(8,128)(2,1)} fusion(bf16[1024,768]{1,0:T(8,128)(2,1)S(1)} %copy-done.1, f32[2304]{0:T(1024)S(1)} %pad_maximum_fusion.2, bf16[768,2560]{1,0:T(8,128)(2,1)} %get-tuple-element.32), kind=kOutput, calls=%fused_computation | convolution fusion | flops 3628597248 | bytes 9839616 | tf_op jit(solution)/shard_map/dot_general | solution.py:905
  103.6 14.0 %shard_map.153 = (bf16[1024,768]{1,0:T(8,128)(2,1)}, bf16[6,2,8,128,384]{4,3,2,1,0:T(8,128)(2,1)}, bf16[6,2,8,128,128]{4,3,2,1,0:T(8,128)(2,1)}) custom-call(bf16[1024,2304]{1,0:T(8,128)(2,1)} %add_convert_fusion.q_ref.k_ref.v_ref, bf16[1024,2304]{1,0:T(8,128)(2,1)} %add_convert_fusion.q_ref.k_ref.v_ref, ...), custom_call_target="tpu_custom_call" | custom-call | tf_op jit(solution)/shard_map/pallas_call | solution.py:910
  117.6 130.1 %shard_map.154 = (f32[1024,768]{1,0:T(8,128)}, bf16[1024,768]{1,0:T(8,128)(2,1)}, bf16[768,3072]{1,0:T(8,128)(2,1)}, bf16[768,768]{1,0:T(8,128)(2,1)}, f32[8,768...) custom-call(bf16[1024,768]{1,0:T(8,128)(2,1)} %get-tuple-element.33.mixed, ...), custom_call_target="tpu_custom_call" | custom-call | tf_op jit(solution)/shard_map/pallas_call | solution.py:865
  247.6 14.3 %shard_map.155 = (bf16[1024,768]{1,0:T(8,128)(2,1)}, bf16[1024,768]{1,0:T(8,128)(2,1)}, bf16[1024,768]{1,0:T(8,128)(2,1)}, f32[48,384]{1,0:T(8,128)}) custom-call(bf16[1024,768]{1,0:T(8,128)(2,1)} %get-tuple-element.39.dm_ref, s32[6,8,256]{2,1,0:T(8,128)} %bitcast.47, bf16[6,2,8,128,384]{4,3,2,1,0:T(8,128)(2,1)} %get-tuple-element.40.slot_ref, ...), custom_call_target="tpu_custom_call" | custom-call | tf_op jit(solution)/shard_map/pallas_call | solution.py:919
  261.9 1.0 slice.56
  263.0 0.9 slice_reduce_fusion
  264.4 1.7 constant_dynamic-update-slice_fusion.2
  266.3 0.8 copy-done.12
  267.1 1.4 copy-done
  268.5 4.9 %add_convert_fusion.1.refs_3_ = bf16[1024,768]{1,0:T(8,128)(2,1)} fusion(f32[1024,768]{1,0:T(8,128)S(1)} %copy-done.12, bf16[1024,2304]{1,0:T(8,128)(2,1)S(1)} %constant_dynamic-update-slice_fusion, bf16[768,2560]{1,0:T(8,128)(2,1)S(1)} %copy-done), kind=kOutput, calls=%fused_computation.6 | convolution fusion | flops 3625451520 | bytes 12976128 | tf_op jit(solution)/shard_map/tf,df->td/dot_general | solution.py:929
  273.4 4.1 %convolution_convert_fusion = bf16[768,2304]{1,0:T(8,128)(2,1)S(1)} fusion(bf16[1024,768]{1,0:T(8,128)(2,1)S(1)} %copy-done.2, bf16[1024,2304]{1,0:T(8,128)(2,1)S(1)} %constant_dynamic-update-slice_fusion), kind=kOutput, calls=%fused_computation.4 | convolution fusion | flops 3625648128 | bytes 9830400 | tf_op jit(solution)/shard_map/td,tf->df/dot_general | solution.py:928
  277.5 2.2 pad_maximum_fusion.refs_2_
  279.7 84.4 %shard_map.156 = (f32[24,768]{1,0:T(8,128)}, f32[24,3072]{1,0:T(8,128)}, f32[24,2560]{1,0:T(8,128)}, bf16[1024,768]{1,0:T(8,128)(2,1)}) custom-call(bf16[768,768]{1,0:T(8,128)(2,1)} %get-tuple-element.37.refs_0_, bf16[768,3072]{1,0:T(8,128)(2,1)} %get-tuple-element.38.refs_1_, bf16[768,2560]{1,0:T(8,128)(2,1)} %pad_maximum_fusion.refs_2_, ...), custom_call_target="tpu_custom_call" | custom-call | tf_op jit(solution)/shard_map/pallas_call | solution.py:707
  364.1 1.4 slice_bitcast_fusion.3
  365.5 0.7 slice_bitcast_fusion
  366.2 1.6 slice.61
  367.9 0.7 copy.38
  368.5 1.1 copy.52
  369.7 1.1 copy.53
  371.5 0.7 copy.55
  372.2 0.7 copy.56
  (51 shorter events, 2.5 us)
Async XLA Ops:
  88.9 7.2 %copy-start.1 = (bf16[1024,768]{1,0:T(8,128)(2,1)S(1)}, bf16[1024,768]{1,0:T(8,128)(2,1)}, u32[]{:S(2)}) copy-start(bf16[1024,768]{1,0:T(8,128)(2,1)} %get-tuple-element.31.x) | copy-start | bytes 4718596
  96.0 7.6 %copy-start.9 = (f32[8,768]{1,0:T(8,128)}, f32[8,768]{1,0:T(8,128)S(1)}, u32[]{:S(2)}) copy-start(f32[8,768]{1,0:T(8,128)S(1)} %convert_bitcast_fusion.vec) | copy-start | bytes 73732
  247.6 15.3 %copy-start.11 = (f32[8,768]{1,0:T(8,128)S(1)}, f32[8,768]{1,0:T(8,128)}, u32[]{:S(2)}) copy-start(f32[8,768]{1,0:T(8,128)} %get-tuple-element.46) | copy-start | bytes 73732
  261.9 4.1 %copy-start.5 = (bf16[1024,768]{1,0:T(8,128)(2,1)S(1)}, bf16[1024,768]{1,0:T(8,128)(2,1)}, u32[]{:S(2)}) copy-start(bf16[1024,768]{1,0:T(8,128)(2,1)} %get-tuple-element.43) | copy-start | bytes 4718596
  264.2 2.0 copy-start.4
  264.4 2.7 copy-start.12
  266.1 2.4 copy-start
  268.5 4.9 %copy-start.2 = (bf16[1024,768]{1,0:T(8,128)(2,1)S(1)}, bf16[1024,768]{1,0:T(8,128)(2,1)}, u32[]{:S(2)}) copy-start(bf16[1024,768]{1,0:T(8,128)(2,1)} %get-tuple-element.31.x) | copy-start | bytes 4718596
  279.7 88.8 %copy-start.3 = (bf16[1024,768]{1,0:T(8,128)(2,1)S(1)}, bf16[1024,768]{1,0:T(8,128)(2,1)}, u32[]{:S(2)}) copy-start(bf16[1024,768]{1,0:T(8,128)(2,1)} %get-tuple-element.90) | copy-start | bytes 4718596
  364.1 5.5 %copy-start.6 = (bf16[1024,768]{1,0:T(8,128)(2,1)S(1)}, bf16[1024,768]{1,0:T(8,128)(2,1)}, u32[]{:S(2)}) copy-start(bf16[1024,768]{1,0:T(8,128)(2,1)} %get-tuple-element.91) | copy-start | bytes 4718596
  364.1 6.7 %copy-start.10 = (f32[24,768]{1,0:T(8,128)S(1)}, f32[24,768]{1,0:T(8,128)}, u32[]{:S(2)}) copy-start(f32[24,768]{1,0:T(8,128)} %get-tuple-element.93) | copy-start | bytes 221188
  367.9 4.3 %copy-start.7 = (f32[96,768]{1,0:T(8,128)S(1)}, f32[96,768]{1,0:T(8,128)}, u32[]{:S(2)}) copy-start(f32[96,768]{1,0:T(8,128)} %get-tuple-element.95) | copy-start | bytes 884740
  368.5 2.9 copy-start.8

commit v3 on v2

--- a/solution.py
+++ b/solution.py
@@ -252,7 +252,7 @@
 
 class Links:
     def __init__(self, send_sems, recv_sems):
-        self.send_sems, self.recv_sems, self.count, self.drains = send_sems, recv_sems, 0, []
+        self.send_sems, self.recv_sems, self.count, self.drains, self.key = send_sems, recv_sems, 0, {}, None
         self.dp, self.sq = lax.axis_index("dp"), lax.axis_index("seq")
         self.x, self.y = lax.rem(self.dp, 2), self.dp // 2
         self.core, self.z = lax.rem(self.sq, 2), self.sq // 2
@@ -285,11 +285,22 @@
     def go(self, *makers):
         for make in makers:
             make().start()
-            self.drains.append(lambda make=make: make().wait_send())
-
-    def drain(self):
-        for d in self.drains:
-            d()
+            self.add(lambda make=make: make().wait_send())
+
+    def drain(self, keys=None):
+        for key in list(self.drains) if keys is None else keys:
+            for d in self.drains.pop(key, []):
+                d()
+
+    def add(self, d):
+        self.drains.setdefault(self.key, []).append(d)
+
+    def under(self, key, stages):
+        def run(stage):
+            before, self.key = self.key, key
+            stage()
+            self.key = before
+        return [functools.partial(run, stage) for stage in stages]
 
 
 def mult(v, m):
@@ -364,17 +375,17 @@
         def _():
             full[chip(L.z), mine] = jnp.concatenate([got, own], axis=0)
         send_line(1)
-        L.drains.append(functools.partial(drain_line, 1))
+        L.add(functools.partial(drain_line, 1))
 
     def s2():
         recv_line(1)
         send_line(2)
-        L.drains.append(functools.partial(drain_line, 2))
+        L.add(functools.partial(drain_line, 2))
 
     def s3():
         recv_line(2)
         send_line(3)
-        L.drains.append(functools.partial(drain_line, 3))
+        L.add(functools.partial(drain_line, 3))
 
     def s4():
         recv_line(3)
@@ -443,7 +454,7 @@
 N_REDUCE = 14
 
 
-def reduce(L, part, out, scratch, r, split):
+def reduce(L, part, out, scratch, r, split, own=None, sem=None):
     acc, a1, b1x, b1y, a2, b2, from_l, from_r, fin, got = scratch
     half = part.shape[1] // 2
     a, b = split
@@ -466,16 +477,23 @@
     a2_copy = lambda: L.copy(ia2, acc.at[quarter(L.dp_x), ca], a2, L.dp_x, L.sq)
     b2_copy = lambda: L.copy(ib2, acc.at[quarter(L.dp_y), cb], b2, L.dp_y, L.sq)
 
+    mine_copy = lambda: pltpu.make_async_copy(part.at[:, mine], own, sem)
+
     def s0():
         L.go(core_copy)
+        if own is not None:
+            mine_copy().start()
 
     def s1():
         core_copy().wait_recv()
+        if own is not None:
+            mine_copy().wait()
         step = 48
 
         def one(i, _):
             here = pl.ds(mult(i * step, 16), step)
-            acc[here, :] = (acc[here, :].astype(jnp.float32) + part[here, mine].astype(jnp.float32)).astype(jnp.bfloat16)
+            add = part[here, mine] if own is None else own[here, :]
+            acc[here, :] = (acc[here, :].astype(jnp.float32) + add.astype(jnp.float32)).astype(jnp.bfloat16)
             return 0
         lax.fori_loop(0, acc.shape[0] // step, one, 0)
         L.go(a1_copy, bx_copy, by_copy)
@@ -538,7 +556,7 @@
             def _():
                 for t in range(0, NZ - 1 - s):
                     hop_l(t, from_r.at[t]).wait_send()
-        L.drains.append(drain)
+        L.add(drain)
 
     fin_copy = lambda: L.copy(ifin, fin.at[1 - L.core], got, L.dp, L.sib)
 
@@ -585,65 +603,6 @@
 BATCH = 8
 
 
-def attend_fwd(scale, q_ref, k_ref, v_ref, perm_ref, mixed_ref, slot_ref, prob_ref, head_ref):
-    nblk = q_ref.shape[0] // BLK
-    share = BLK // nblk
-    keep = head_lanes(384)
-    for k in range(nblk):
-        here = pl.ds(k * BLK, BLK)
-        packed = jnp.concatenate([q_ref[here, :], k_ref[here, :], v_ref[here, :]], axis=1)
-        table = one_hot(perm_ref[0, k:k + 1, :], BLK)
-        moved = jnp.where(keep, dot(table, packed, 0, 0), 0.0).astype(jnp.bfloat16)
-        slot_ref[0, :, :, pl.ds(k * share, share), :] = moved.reshape(2, nblk, share, 384)
-    for h in range(2):
-        for c in range(0, nblk, BATCH):
-            cs = pl.ds(c, BATCH)
-            q, kk, v = slot_ref[0, h, cs, :, 0:128], slot_ref[0, h, cs, :, 128:256], slot_ref[0, h, cs, :, 256:384]
-            scores = bdot(q, kk, 2, 2) * scale
-            e = jnp.exp(scores - jnp.max(scores, axis=-1, keepdims=True))
-            probs = (e * (1.0 / jnp.sum(e, axis=-1, keepdims=True))).astype(jnp.bfloat16)
-            prob_ref[0, h, cs] = probs
-            head_ref[h, cs] = bdot(probs, v, 2, 1).astype(jnp.bfloat16)
-    for k in range(nblk):
-        table = one_hot(perm_ref[0, k:k + 1, :], BLK)
-        back = head_ref[:, :, pl.ds(k * share, share), :].reshape(2 * BLK, BLK)
-        mixed_ref[pl.ds(k * BLK, BLK), :] = dot(table, back, 1, 0).astype(jnp.bfloat16)
-
-
-def attend_bwd(scale, dm_ref, perm_ref, slot_ref, prob_ref, dq_ref, dk_ref, dv_ref, sums_ref, up_ref, grad_ref):
-    nblk = dm_ref.shape[0] // BLK
-    share = BLK // nblk
-    keep = head_lanes(128)
-    for k in range(nblk):
-        table = one_hot(perm_ref[0, k:k + 1, :], BLK)
-        moved = jnp.where(keep, dot(table, dm_ref[pl.ds(k * BLK, BLK), :], 0, 0), 0.0).astype(jnp.bfloat16)
-        up_ref[:, :, pl.ds(k * share, share), :] = moved.reshape(2, nblk, share, 128)
-    for h in range(2):
-        for c in range(0, nblk, BATCH):
-            cs = pl.ds(c, BATCH)
-            q, kk, v = slot_ref[0, h, cs, :, 0:128], slot_ref[0, h, cs, :, 128:256], slot_ref[0, h, cs, :, 256:384]
-            probs, up = prob_ref[0, h, cs], up_ref[h, cs]
-            dprobs = bdot(up, v, 2, 2)
-            p32 = probs.astype(jnp.float32)
-            pd = p32 * dprobs
-            dscores = (pd - p32 * jnp.sum(pd, axis=-1, keepdims=True)).astype(jnp.bfloat16)
-            grad_ref[h, cs, :, 0:128] = (bdot(dscores, kk, 2, 1) * scale).astype(jnp.bfloat16)
-            grad_ref[h, cs, :, 128:256] = (bdot(dscores, q, 1, 1) * scale).astype(jnp.bfloat16)
-            grad_ref[h, cs, :, 256:384] = bdot(probs, up, 1, 1).astype(jnp.bfloat16)
-    total = jnp.zeros((1, 384), jnp.float32)
-    for k in range(nblk):
-        table = one_hot(perm_ref[0, k:k + 1, :], BLK)
-        back = grad_ref[:, :, pl.ds(k * share, share), :].reshape(2 * BLK, 384)
-        here = pl.ds(k * BLK, BLK)
-        moved = dot(table, back, 1, 0)
-        total = total + jnp.sum(moved, axis=0, keepdims=True)
-        moved = moved.astype(jnp.bfloat16)
-        dq_ref[here, :] = moved[:, 0:128]
-        dk_ref[here, :] = moved[:, 128:256]
-        dv_ref[here, :] = moved[:, 256:384]
-    sums_ref[...] = jnp.broadcast_to(total, (8, 384))
-
-
 SIZES = {"qkv": (24, 2560, (640, 640)), "out": (24, 768, (256, 128)), "up": (24, 3072, (768, 768)), "down": (96, 768, (128, 256))}
 ALL = ("dp", "seq")
 VM = pl.BlockSpec(memory_space=pltpu.VMEM)
@@ -651,65 +610,52 @@
 LIMIT = 60 * 2**20
 
 
-def gather_kernel(names, na, *refs):
-    n = len(names)
-    ins, outs, sc = refs[:n + na], refs[n + na:2 * (n + na)], refs[2 * (n + na):]
-    L = Links(sc[n], sc[n + 1])
-    L.enter()
-    progs = [gather(L, ins[i], outs[i], sc[i], SIZES[nm][0], SIZES[nm][2]) for i, nm in enumerate(names)]
-    sp = [spread(L, ins[n + i], outs[n + i], sc[n + 2].at[i]) for i in range(na)]
-    for k in range(8):
-        for p in progs:
-            p[k]()
-        if k == 5:
-            for b, _ in sp:
-                b()
-    for _, f in sp:
-        f()
-    L.drain()
-
-
-def gather_call(names, shards, rows):
-    na, n = len(rows), len(names)
-    count = 15 * n + 7 * na
-    outs = [jax.ShapeDtypeStruct((32 * SIZES[nm][0], SIZES[nm][1]), BF) for nm in names]
-    outs += [jax.ShapeDtypeStruct(a.shape, BF) for a in rows]
-    return pl.pallas_call(
-        functools.partial(gather_kernel, names, na), out_shape=outs, in_specs=[VM] * (n + na), out_specs=[VM] * (n + na),
-        scratch_shapes=[pltpu.VMEM((SIZES[nm][0], SIZES[nm][1] // 2), BF) for nm in names]
-        + [pltpu.SemaphoreType.DMA((count,)), pltpu.SemaphoreType.DMA((count,)), pltpu.SemaphoreType.DMA((max(na, 1),))],
-        compiler_params=pltpu.CompilerParams(collective_id=0, has_side_effects=True, vmem_limit_bytes=LIMIT),
-    )(*shards, *rows)
-
-
-def reduce_kernel(names, na, *refs):
-    n = len(names)
-    ins, outs, sc = refs[:n + na], refs[n + na:2 * (n + na)], refs[2 * (n + na):]
-    L = Links(sc[10 * n], sc[10 * n + 1])
-    L.enter()
-    progs = [reduce(L, ins[i], outs[i], sc[10 * i:10 * i + 10], SIZES[nm][0], SIZES[nm][2]) for i, nm in enumerate(names)]
-    sp = [spread(L, ins[n + i], outs[n + i], sc[10 * n + 2].at[i]) for i in range(na)]
-    for b, _ in sp:
-        b()
-    for k in range(9):
-        for p in progs:
-            p[k]()
-    for _, f in sp:
-        f()
-    L.drain()
-
-
-def reduce_call(names, parts, rows, cid):
-    na, n = len(rows), len(names)
-    count = N_REDUCE * n + 7 * na
-    outs = [jax.ShapeDtypeStruct(SIZES[nm][:2], jnp.float32) for nm in names]
-    outs += [jax.ShapeDtypeStruct(a.shape, BF) for a in rows]
-    return pl.pallas_call(
-        functools.partial(reduce_kernel, names, na), out_shape=outs, in_specs=[VM] * (n + na), out_specs=[VM] * (n + na),
-        scratch_shapes=sum([reduce_scratch(*SIZES[nm]) for nm in names], [])
-        + [pltpu.SemaphoreType.DMA((count,)), pltpu.SemaphoreType.DMA((count,)), pltpu.SemaphoreType.DMA((max(na, 1),))],
-        compiler_params=pltpu.CompilerParams(collective_id=cid, has_side_effects=True, vmem_limit_bytes=LIMIT),
-    )(*parts, *rows)
+def place_rows(route, perm, me):
+    heads, n, size = route.shape
+    base = me * BLK
+    head_row = jnp.concatenate([route[h, 0:1, :] for h in range(heads)] + [jnp.full((16 - heads, size), -1, jnp.int32)], axis=0)
+    mine = (head_row >= base) & (head_row < base + BLK)
+    flags = jnp.where(mine, 1.0, 0.0).astype(jnp.bfloat16)
+    before = []
+    for c in range(0, size, 128):
+        row = lax.broadcasted_iota(jnp.int32, (size, 128), 0)
+        col = lax.broadcasted_iota(jnp.int32, (size, 128), 1) + c
+        before.append(dot(flags, jnp.where(row < col, 1.0, 0.0).astype(jnp.bfloat16), 1, 0))
+    slot = jnp.where(mine, jnp.concatenate(before, axis=1).astype(jnp.int32), -1)
+    for h in range(heads):
+        per = route[h]
+        local = jnp.where((per >= base) & (per < base + BLK), per - base, 0).astype(jnp.float32).astype(jnp.bfloat16)
+        pick = jnp.where(slot[h:h + 1, :] == lax.broadcasted_iota(jnp.int32, (BLK, size), 0), 1.0, 0.0).astype(jnp.bfloat16)
+        perm[h // 2, :, pl.ds((h % 2) * BLK, BLK)] = dot(local, pick, 1, 1).astype(jnp.int32)
+
+
+def front_pair(scale, qkv, width, perm, mixed, pool, head_ref, p, par):
+    nblk = qkv.shape[0] // BLK
+    share = BLK // nblk
+    keep = head_lanes(384)
+    cols = pl.ds(mult(par * 384, 128), 384)
+    lane = lambda o: pl.ds(mult(par * 384 + o, 128), 128)
+    col = lambda o: pl.ds(mult(p * 128 + o * width, 128), 128)
+    half = nblk * BLK
+    for k in range(nblk):
+        here = pl.ds(k * BLK, BLK)
+        packed = jnp.concatenate([qkv[here, col(0)], qkv[here, col(1)], qkv[here, col(2)]], axis=1)
+        table = one_hot(perm[p, k:k + 1, :], BLK)
+        moved = jnp.where(keep, dot(table, packed, 0, 0), 0.0).astype(jnp.bfloat16)
+        for c in range(2 * nblk):
+            pool[pl.ds(c * BLK + k * share, share), cols] = moved[c * share:(c + 1) * share]
+    for h in range(2):
+        rows = pl.ds(h * half, half)
+        q, kk, v = [pool[rows, lane(o)].reshape(nblk, BLK, 128) for o in (0, 128, 256)]
+        scores = bdot(q, kk, 2, 2) * scale
+        e = jnp.exp(scores - jnp.max(scores, axis=-1, keepdims=True))
+        probs = (e * (1.0 / jnp.sum(e, axis=-1, keepdims=True))).astype(jnp.bfloat16)
+        pool[pl.ds(2 * half, half), pl.ds(mult((2 * par + h) * 128, 128), 128)] = probs.reshape(half, BLK)
+        head_ref[rows, :] = bdot(probs, v, 2, 1).reshape(half, BLK).astype(jnp.bfloat16)
+    for k in range(nblk):
+        table = one_hot(perm[p, k:k + 1, :], BLK)
+        back = jnp.concatenate([head_ref[pl.ds(c * BLK + k * share, share), :] for c in range(2 * nblk)], axis=0)
+        mixed[pl.ds(k * BLK, BLK), col(0)] = dot(table, back, 1, 0).astype(jnp.bfloat16)
 
 
 def loop(n, body, hooks=()):
@@ -729,26 +675,84 @@
 
 
 TB = 256
-FB = 512
-
-
-def dense_kernel(mixed, x, w_out, w_up, down_shard, up_rows, vec, ub,
-                 d_res, d_mixed, g_up, g_out, sums, ubsum, out_rows, r_down,
-                 w_down, half_buf, n1, s1, low, act, gp, up, outb, dn, da, gd, *rest):
+FB = 768
+
+
+def front_kernel(scale, qkv_shard, out_shard, up_shard, down_shard, route, x_rows, up_rows,
+                 x_home, w_home, slots, probs, perm, d_res, d_mixed, g_up, g_out, sums, ubsum, out_rows, r_down,
+                 w_out, w_up, w_down, act, gp, x, mixed, n1, s1, low, up, outb, dn, gd, head_ref, vec, ub, auxf,
+                 bq, bo, bu, bd, *rest):
     red, (ss, rs, ls, cs) = rest[:10], rest[10:]
     rows_here, width = x.shape
     ff = w_up.shape[1]
+    pairs = perm.shape[0]
+    w = gp.at[pl.ds(0, width), pl.ds(0, qkv_shard.shape[1])]
+    da = up
     L = Links(ss, rs)
     L.enter()
-    ga = gather(L, down_shard, w_down, half_buf, SIZES["down"][0], SIZES["down"][2])
-    up_begin, up_finish = spread(L, up_rows, up, ls.at[0])
-    out_begin, out_finish = spread(L, outb, out_rows, ls.at[1])
-    rd = reduce(L, gd, r_down, red, SIZES["down"][0], SIZES["down"][2])
+    Q = L.under("qkv", gather(L, qkv_shard, w, bq, *SIZES["qkv"][::2]))
+    O = L.under("out", gather(L, out_shard, w_out, bo, *SIZES["out"][::2]))
+    U = gather(L, up_shard, w_up, bu, *SIZES["up"][::2])
+    D = gather(L, down_shard, w_down, bd, *SIZES["down"][::2])
+    x_begin, x_finish = spread(L, x_rows, x, ls.at[0])
+    up_begin, up_finish = spread(L, up_rows, up, ls.at[1])
+    out_begin, out_finish = spread(L, outb, out_rows, ls.at[2])
+    R = reduce(L, gd, r_down, red, *SIZES["down"][::2])
+    plan = PLAN(Q, O, U, D, x_begin, up_begin, R)
+    row = lambda i: vec[i:i + 1, :]
+
+    def run(stages):
+        for stage in stages:
+            stage()
+
+    run(plan["start"])
     sums[...] = jnp.zeros_like(sums)
     ubsum[...] = jnp.zeros_like(ubsum)
-    row = lambda i: vec[i:i + 1, :]
-    ga[0]()
-    ga[1]()
+    place_rows(route, perm, L.sq)
+    run(plan["placed"])
+    vec[...] = w[:, 2304:2432].astype(jnp.float32).T[0:8, :]
+    auxf[...] = w[:, 2432:2560].astype(jnp.float32)
+    step = ff // 32
+    for i in range(32):
+        ub[:, i * step:(i + 1) * step] = auxf[i * 24:i * 24 + 1, 0:step]
+    w_flush = pltpu.make_async_copy(w, w_home, cs.at[0])
+    w_flush.start()
+    run(plan["weights"])
+    x_finish()
+    x_flush = pltpu.make_async_copy(x, x_home, cs.at[1])
+    x_flush.start()
+
+    def project(m):
+        here = pl.ds(mult(m * TB, TB), TB)
+        for j in range(3):
+            c = pl.ds(j * width, width)
+            r = dot(x[here, :], w[:, c], 1, 0)
+            if j != 1:
+                r = r + row(j // 2)
+            act[here, c] = r.astype(jnp.bfloat16)
+
+    loop(rows_here // TB, project, plan["project"])
+
+    def kept(p, par):
+        half = rows_here
+        return [pltpu.make_async_copy(gd.at[pl.ds(0, 2 * half), pl.ds(mult(par * 384, 128), 384)], slots.at[p], cs.at[2 + 3 * par])] + [
+            pltpu.make_async_copy(gd.at[pl.ds(2 * half, half), pl.ds(mult((2 * par + h) * 128, 128), 128)], probs.at[p, h],
+                                  cs.at[3 + 3 * par + h]) for h in range(2)]
+
+    def attend(p):
+        par = lax.rem(p, 2)
+
+        @pl.when(p >= 2)
+        def _():
+            for c in kept(p - 2, par):
+                c.wait()
+        front_pair(scale, act, width, perm, mixed, gd, head_ref, p, par)
+        for c in kept(p, par):
+            c.start()
+
+    loop(pairs, attend, plan["attend"])
+    w_flush.wait()
+    L.drain(["qkv", "out"])
 
     def first_half(m):
         here = pl.ds(mult(m * TB, TB), TB)
@@ -765,10 +769,13 @@
             act[here, c] = (wide * cdf).astype(jnp.bfloat16)
             gp[here, c] = (cdf + wide * (0.3989422804014327 * jnp.exp(-0.5 * wide * wide))).astype(jnp.bfloat16)
 
-    loop(rows_here // TB, first_half, HOOK_A(ga, up_begin))
-    for stage in REST_A(ga):
-        stage()
+    loop(rows_here // TB, first_half, plan["first"])
+    run(plan["firsts"])
     up_finish()
+    for p in range(pairs - 2, pairs):
+        for c in kept(p, p % 2):
+            c.wait()
+    x_flush.wait()
 
     def second_half(m):
         here = pl.ds(mult(m * TB, TB), TB)
@@ -793,7 +800,7 @@
         gd[c, :] = dot(act[:, c], dn[...], 0, 0).astype(jnp.bfloat16)
 
     loop(ff // FB, grad_down)
-    rd[0]()
+    R[0]()
 
     def third(m):
         here = pl.ds(mult(m * TB, TB), TB)
@@ -813,126 +820,232 @@
         lo = d.astype(jnp.bfloat16)
         da[here, :] = lo
         sums[0:1, :] += jnp.sum(lo.astype(jnp.float32), axis=0, keepdims=True)
-        d_mixed[here, :] = dot(lo, w_out[...], 1, 1).astype(jnp.bfloat16)
-
-    loop(rows_here // TB, third, HOOK_C(rd))
+        x[here, :] = dot(lo, w_out[...], 1, 1).astype(jnp.bfloat16)
+
+    loop(rows_here // TB, third, plan["third"])
+    flush = [pltpu.make_async_copy(x, d_mixed, cs.at[0])]
+    flush[0].start()
 
     def grad_up(i):
         c = pl.ds(mult(i * FB, FB), FB)
         act[pl.ds(0, width), c] = dot(low[...], gp[:, c], 0, 0).astype(jnp.bfloat16)
 
-    loop(ff // FB, grad_up, HOOK_D(rd))
-    flush = pltpu.make_async_copy(act.at[pl.ds(0, width), :], g_up, cs.at[0])
-    flush.start()
-    g_out[...] = dot(mixed[...], da[...], 0, 0).astype(jnp.bfloat16)
-    for stage in REST_D(rd):
-        stage()
+    loop(ff // FB, grad_up, plan["grad_up"])
+    flush.append(pltpu.make_async_copy(act.at[pl.ds(0, width), :], g_up, cs.at[1]))
+    flush[1].start()
+    w_out[...] = dot(mixed[...], da[...], 0, 0).astype(jnp.bfloat16)
+    flush.append(pltpu.make_async_copy(w_out, g_out, cs.at[2]))
+    flush[2].start()
+    run(plan["end"])
     out_finish()
-    flush.wait()
+    for f in flush:
+        f.wait()
     L.drain()
 
 
-def HOOK_A(ga, up_begin):
-    return [(0, ga[2]), (1, ga[3]), (2, ga[4]), (2, up_begin), (3, ga[5])]
-
-
-def REST_A(ga):
-    return ga[6:]
-
-
-def HOOK_C(rd):
-    return [(0, rd[1]), (1, rd[2]), (2, rd[3]), (3, rd[4])]
-
-
-def HOOK_D(rd):
-    return [(0, rd[5]), (2, rd[6]), (4, rd[7])]
-
-
-def REST_D(rd):
-    return rd[8:]
-
-
-def dense_call(mixed, x, w_out, w_up, w_down, upstream, vec, ub):
-    rows_here, width = x.shape
+def PLAN(Q, O, U, D, x_begin, up_begin, R):
+    return {
+        "start": [Q[0], O[0], U[0], D[0], Q[1], O[1], U[1], Q[2], O[2], U[2], Q[3], O[3], U[3], x_begin, Q[4], D[1]],
+        "placed": [Q[5], O[4], U[4], Q[6], O[5], U[5], Q[7]],
+        "weights": [O[6], U[6]],
+        "project": [(3, D[2])],
+        "attend": [(0, O[7]), (0, U[7]), (1, D[3]), (1, up_begin), (3, D[4])],
+        "first": [(0, D[5]), (3, D[6])],
+        "firsts": [D[7]],
+        "third": [(0, R[1]), (3, R[2])],
+        "grad_up": [(1, R[3]), (1, R[4])],
+        "end": [R[5], R[6], R[7], R[8]],
+    }
+
+
+def front_call(scale, pairs, qkv_shard, w_out, w_up, w_down, route, tokens, upstream):
+    rows_here, width = tokens.shape
     ff = w_up.shape[1]
     r, cols, split = SIZES["down"]
-    count = 15 + 14 + N_REDUCE
+    count = 4 * 15 + 3 * 7 + N_REDUCE
     f32 = lambda *s: jax.ShapeDtypeStruct(s, jnp.float32)
     bf = lambda *s: jax.ShapeDtypeStruct(s, BF)
     vbf = lambda *s: pltpu.VMEM(s, BF)
     vf = lambda *s: pltpu.VMEM(s, jnp.float32)
     hbm = pl.BlockSpec(memory_space=pl.ANY)
+    wq = qkv_shard.shape[1]
     return pl.pallas_call(
-        dense_kernel,
-        out_shape=[f32(rows_here, width), bf(rows_here, width), bf(width, ff), bf(width, width), f32(8, width), f32(8, ff),
-                   bf(rows_here, width), f32(r, cols)],
-        in_specs=[VM] * 5 + [hbm] + [VM] * 2,
-        out_specs=[VM, VM, hbm] + [VM] * 5,
-        scratch_shapes=[vbf(ff, width), vbf(r, cols // 2), vf(rows_here, width), vf(rows_here, 1), vbf(rows_here, width),
-                        vbf(rows_here, ff), vbf(rows_here, ff), vbf(rows_here, width), vbf(rows_here, width),
-                        vbf(rows_here, width), vbf(rows_here, width), vbf(ff, width)]
+        functools.partial(front_kernel, scale),
+        out_shape=[bf(rows_here, width), bf(width, wq), bf(pairs, 2 * rows_here, 384), bf(pairs, 2, rows_here, BLK),
+                   jax.ShapeDtypeStruct((pairs, 2 * NZ, 2 * BLK), jnp.int32), f32(rows_here, width), bf(rows_here, width),
+                   bf(width, ff), bf(width, width), f32(8, width), f32(8, ff), bf(rows_here, width), f32(r, cols)],
+        in_specs=[VM] * 5 + [hbm] * 2,
+        out_specs=[hbm] * 4 + [VM] * 2 + [hbm] * 3 + [VM] * 2 + [hbm, VM],
+        scratch_shapes=[vbf(width, width), vbf(width, ff), vbf(ff, width), vbf(rows_here, ff), vbf(rows_here, ff),
+                        vbf(rows_here, width), vbf(rows_here, width), vf(rows_here, width), vf(rows_here, 1)]
+        + [vbf(rows_here, width)] * 4
+        + [vbf(ff, width), vbf(2 * rows_here, BLK), vf(8, width), vf(1, ff), vf(width, BLK)]
+        + [vbf(SIZES[n][0], SIZES[n][1] // 2) for n in ("qkv", "out", "up", "down")]
         + reduce_scratch(r, cols, split)
-        + [pltpu.SemaphoreType.DMA((count,)), pltpu.SemaphoreType.DMA((count,)), pltpu.SemaphoreType.DMA((2,)),
-           pltpu.SemaphoreType.DMA((1,))],
-        compiler_params=pltpu.CompilerParams(collective_id=1, has_side_effects=True, vmem_limit_bytes=62 * 2**20),
-    )(mixed, x, w_out, w_up, w_down, upstream, vec, ub)
-
-
-def slot_rows(route, me):
-    heads, n = route.shape[0], 2 * NZ
-    per = route.reshape(heads, n, -1)
-    mine = (per[:, 0] // BLK) == me
-    place = jnp.cumsum(mine.astype(jnp.int32), axis=1) - 1
-    pick = (mine[:, None, :] & (place[:, None, :] == jnp.arange(BLK)[None, :, None])).astype(BF)
-    local = jnp.where(mine[:, None, :], per - me * BLK, 0).astype(BF)
-    rows = jnp.einsum("hke,hse->hks", local, pick, preferred_element_type=jnp.float32).astype(jnp.int32)
-    return rows.reshape(heads // 2, 2, n, BLK).transpose(0, 2, 1, 3).reshape(heads // 2, n, 2 * BLK)
+        + [pltpu.SemaphoreType.DMA((count,)), pltpu.SemaphoreType.DMA((count,)), pltpu.SemaphoreType.DMA((3,)),
+           pltpu.SemaphoreType.DMA((8,))],
+        compiler_params=pltpu.CompilerParams(collective_id=0, has_side_effects=True, vmem_limit_bytes=62 * 2**20),
+    )(qkv_shard, w_out, w_up, w_down, route, tokens, upstream)
+
+
+def back_pair(scale, dm_ref, perm_ref, slot_ref, prob_ref, up_ref, grad_ref, dp_ref):
+    nblk = dm_ref.shape[0] // BLK
+    share = BLK // nblk
+    keep = head_lanes(128)
+    for k in range(nblk):
+        table = one_hot(perm_ref[0, k:k + 1, :], BLK)
+        moved = jnp.where(keep, dot(table, dm_ref[pl.ds(k * BLK, BLK), :], 0, 0), 0.0).astype(jnp.bfloat16)
+        up_ref[:, :, pl.ds(k * share, share), :] = moved.reshape(2, nblk, share, 128)
+    for h in range(2):
+        for c in range(0, nblk, BATCH):
+            cs = pl.ds(c, BATCH)
+            rows = pl.ds((h * nblk + c) * BLK, BATCH * BLK)
+            q, kk, v = [slot_ref[0, rows, o:o + 128].reshape(BATCH, BLK, 128) for o in (0, 128, 256)]
+            probs, up = prob_ref[0, h, pl.ds(c * BLK, BATCH * BLK), :].reshape(BATCH, BLK, BLK), up_ref[h, cs]
+            dprobs = bdot(up, v, 2, 2)
+            p32 = probs.astype(jnp.float32)
+            pd = p32 * dprobs
+            dscores = (pd - p32 * jnp.sum(pd, axis=-1, keepdims=True)).astype(jnp.bfloat16)
+            grad_ref[h, cs, :, 0:128] = (bdot(dscores, kk, 2, 1) * scale).astype(jnp.bfloat16)
+            grad_ref[h, cs, :, 128:256] = (bdot(dscores, q, 1, 1) * scale).astype(jnp.bfloat16)
+            grad_ref[h, cs, :, 256:384] = bdot(probs, up, 1, 1).astype(jnp.bfloat16)
+    total = jnp.zeros((1, 384), jnp.float32)
+    for k in range(nblk):
+        table = one_hot(perm_ref[0, k:k + 1, :], BLK)
+        back = grad_ref[:, :, pl.ds(k * share, share), :].reshape(2 * BLK, 384)
+        moved = dot(table, back, 1, 0)
+        total = total + jnp.sum(moved, axis=0, keepdims=True)
+        dp_ref[pl.ds(k * BLK, BLK), :] = moved.astype(jnp.bfloat16)
+    return total
+
+
+A_PAIRS = 4
+
+
+def back_kernel(scale, pairs, dm_ref, perm_ref, slot_ref, prob_ref, x_hbm, w_hbm, dres_hbm, gup_hbm, gout_hbm, sums1, ubsum,
+                r_qkv, r_up, r_out, gx_rows,
+                up_ref, grad_ref, dp_ref, x, xt, w, gx, gxb, part_a, part_b, own_up, own_out, vsum, ubs, ra, rb, *rest):
+    red = [rest[10 * i:10 * i + 10] for i in range(4)]
+    ss, rs, ls, cs = rest[40:]
+    width = x.shape[1]
+    p = pl.program_id(0)
+    L = Links(ss, rs)
+    up = reduce(L, gup_hbm, r_up, red[0], *SIZES["up"][::2], own=own_up, sem=cs.at[0])
+    ou = reduce(L, gout_hbm, r_out, red[1], *SIZES["out"][::2], own=own_out, sem=cs.at[1])
+    qa = reduce(L, part_a, ra, red[2], 24, (384, 384))
+    qb = reduce(L, part_b, rb, red[3], 24, (256, 256))
+    begin, finish = spread(L, gxb, gx_rows, ls.at[0])
+    loads = [(x_hbm, x, 2), (w_hbm, w, 3), (dres_hbm, gx, 4)]
+
+    @pl.when(p == 0)
+    def _():
+        for a, b, i in loads:
+            pltpu.make_async_copy(a, b, cs.at[i]).start()
+        vsum[...] = jnp.zeros_like(vsum)
+        vsum[2:8, :] = sums1[0:6, :]
+        L.enter()
+        ou[0]()
+        up[0]()
+
+    total = back_pair(scale, dm_ref, perm_ref, slot_ref, prob_ref, up_ref, grad_ref, dp_ref)
+    col = lambda o: pl.ds(mult(p * 128 + o * width, 128), 128)
+    vsum[0:1, col(0)] = total[:, 0:128]
+    vsum[1:2, col(0)] = total[:, 256:384]
+
+    @pl.when(p == 0)
+    def _():
+        for a, b, i in loads:
+            pltpu.make_async_copy(a, b, cs.at[i]).wait()
+        xt[...] = x[...].T
+
+    dp = dp_ref[...]
+    wp = jnp.concatenate([w[:, col(0)], w[:, col(1)], w[:, col(2)]], axis=1)
+    for m in range(0, x.shape[0], 256):
+        gx[m:m + 256, :] += dot(dp[m:m + 256], wp, 1, 1)
+    g = dot(xt[...], dp, 1, 0).astype(jnp.bfloat16)
+
+    @pl.when(p < A_PAIRS)
+    def _():
+        part_a[:, pl.ds(mult(p * 384, 128), 384)] = g
+
+    @pl.when(p >= A_PAIRS)
+    def _():
+        part_b[:, pl.ds(mult((p - A_PAIRS) * 384, 128), 384)] = g
+
+    for at, stage in BACK_PLAN(up, ou, qa):
+        pl.when(p == at)(stage)
+
+    @pl.when(p == pairs - 1)
+    def _():
+        gxb[...] = gx[...].astype(jnp.bfloat16)
+        ubs[...] = jnp.zeros_like(ubs)
+        step = ubsum.shape[1] // 32
+        for i in range(32):
+            ubs[i, 0:1, 0:step] = ubsum[0:1, i * step:(i + 1) * step]
+        wide = jnp.concatenate([vsum[...], jnp.zeros((120, width), jnp.float32)], axis=0)
+        part_b[:, 768:896] = wide.T.astype(jnp.bfloat16)
+        part_b[:, 896:1024] = ubs[...].reshape(width, 128).astype(jnp.bfloat16)
+        for stage in BACK_TAIL(up, ou, qa, qb, begin):
+            stage()
+        finish()
+        for b in range(20):
+            src = ra[:, b * 128:(b + 1) * 128] if b < 12 else rb[:, (b - 12) * 128:(b - 11) * 128]
+            dst = (b // 3 + (b % 3) * pairs) if b < 18 else b
+            r_qkv[:, dst * 128:(dst + 1) * 128] = src
+        L.drain()
+
+
+def BACK_PLAN(up, ou, qa):
+    return [(0, ou[1]), (0, up[1]), (1, ou[2]), (1, up[2]), (2, ou[3]), (2, up[3]), (2, ou[4]), (2, up[4]),
+            (3, qa[0]), (3, ou[5]), (3, up[5]), (4, ou[6]), (4, up[6]), (4, qa[1])]
+
+
+def BACK_TAIL(up, ou, qa, qb, begin):
+    return [qb[0], begin, qa[2], qb[1], ou[7], up[7], qa[3], qb[2], qa[4], qb[3], ou[8], up[8], qb[4], qa[5], qb[5],
+            qa[6], qb[6], qa[7], qb[7], qa[8], qb[8]]
+
+
+def back_call(scale, d_mixed, perm, slots, probs, x, w, d_res, g_up, g_out, sums1, ubsum):
+    pairs = perm.shape[0]
+    rows_here, width = x.shape
+    count = 4 * N_REDUCE + 7
+    hbm = pl.BlockSpec(memory_space=pl.ANY)
+    vbf = lambda *s: pltpu.VMEM(s, BF)
+    vf = lambda *s: pltpu.VMEM(s, jnp.float32)
+    f32 = lambda *s: jax.ShapeDtypeStruct(s, jnp.float32)
+    whole = lambda *s: pl.BlockSpec(s, lambda p: (0,) * len(s))
+    r, cu = SIZES["up"][:2]
+    co = SIZES["out"][1]
+    return pl.pallas_call(
+        functools.partial(back_kernel, scale, pairs), grid=(pairs,),
+        out_shape=[f32(r, 2560), f32(r, cu), f32(r, co), jax.ShapeDtypeStruct((rows_here, width), BF)],
+        in_specs=[pl.BlockSpec((rows_here, 128), lambda p: (0, p)), pl.BlockSpec((1, 8, 256), lambda p: (p, 0, 0)),
+                  pl.BlockSpec((1, 2 * rows_here, 384), lambda p: (p, 0, 0)),
+                  pl.BlockSpec((1, 2, rows_here, BLK), lambda p: (p, 0, 0, 0))] + [hbm] * 5
+        + [whole(*sums1.shape), whole(*ubsum.shape)],
+        out_specs=[whole(r, 2560), whole(r, cu), whole(r, co), hbm],
+        scratch_shapes=[vbf(2, 8, BLK, BLK), vbf(2, 8, BLK, 384), vbf(rows_here, 384), vbf(rows_here, width),
+                        vbf(width, rows_here), vbf(*w.shape), vf(rows_here, width), vbf(rows_here, width),
+                        vbf(width, 1536), vbf(width, 1024), vbf(32 * r, cu // 2), vbf(32 * r, co // 2),
+                        vf(8, width), vf(32, r, 128), vf(r, 1536), vf(r, 1024)]
+        + reduce_scratch(*SIZES["up"]) + reduce_scratch(*SIZES["out"]) + reduce_scratch(r, 1536, (384, 384))
+        + reduce_scratch(r, 1024, (256, 256))
+        + [pltpu.SemaphoreType.DMA((count,)), pltpu.SemaphoreType.DMA((count,)), pltpu.SemaphoreType.DMA((1,)),
+           pltpu.SemaphoreType.DMA((5,))],
+        compiler_params=pltpu.CompilerParams(collective_id=1, has_side_effects=True, vmem_limit_bytes=LIMIT),
+    )(d_mixed, perm, slots, probs, x, w, d_res, g_up, g_out, sums1, ubsum)
 
 
 def homes(tokens, w_qkv, w_out, w_up, w_down, vectors, up_bias, cluster_route, upstream):
-    me = lax.axis_index("seq")
-    rows_here, width = tokens.shape
     pairs = H // 2
-    scale = (width // H) ** -0.5
-    aux = jnp.pad(vectors.T, ((0, 0), (0, 248))) + jnp.pad(up_bias[None, :], ((0, 23), (8, 152)))
-    full_qkv, full_out, full_up, x = gather_call(
-        ("qkv", "out", "up"), [jnp.concatenate([w_qkv, aux], axis=1), w_out, w_up], [tokens])
-    perm = slot_rows(cluster_route[0], me)
-    vec = full_qkv[:, 2304:2312].T.astype(jnp.float32)
-    ub = full_qkv[::24, 2312:2408].reshape(-1).astype(jnp.float32)
-    w = full_qkv[:, :2304]
-    shifts = jnp.concatenate([vec[0], jnp.zeros((width,), jnp.float32), vec[1]])
-    qkv = (jnp.dot(x, w, preferred_element_type=jnp.float32) + shifts).astype(BF)
-    col = lambda o: pl.BlockSpec((rows_here, 128), lambda p, o=o: (0, p + o))
-    perm_spec = pl.BlockSpec((1, 8, 256), lambda p: (p, 0, 0))
-    slot_spec = pl.BlockSpec((1, 2, 8, BLK, 384), lambda p: (p, 0, 0, 0, 0))
-    prob_spec = pl.BlockSpec((1, 2, 8, BLK, BLK), lambda p: (p, 0, 0, 0, 0))
-    mixed, slots, probs = pl.pallas_call(
-        functools.partial(attend_fwd, scale), grid=(pairs,),
-        out_shape=[jax.ShapeDtypeStruct((rows_here, width), BF), jax.ShapeDtypeStruct((pairs, 2, 8, BLK, 384), BF),
-                   jax.ShapeDtypeStruct((pairs, 2, 8, BLK, BLK), BF)],
-        in_specs=[col(0), col(pairs), col(2 * pairs), perm_spec], out_specs=[col(0), slot_spec, prob_spec],
-        scratch_shapes=[pltpu.VMEM((2, 8, BLK, BLK), BF)],
-        compiler_params=pltpu.CompilerParams(vmem_limit_bytes=LIMIT),
-    )(qkv, qkv, qkv, perm)
-    d_res, d_mixed, g_up, g_out, sums1, ubsum, out_rows, r_down = dense_call(mixed, x, full_out, full_up, w_down, upstream, vec, ub[None])
-    dq, dk, dv, sums = pl.pallas_call(
-        functools.partial(attend_bwd, scale), grid=(pairs,),
-        out_shape=[jax.ShapeDtypeStruct((rows_here, width), BF)] * 3 + [jax.ShapeDtypeStruct((8 * pairs, 384), jnp.float32)],
-        in_specs=[col(0), perm_spec, slot_spec, prob_spec], out_specs=[col(0)] * 3 + [pl.BlockSpec((8, 384), lambda p: (p, 0))],
-        scratch_shapes=[pltpu.VMEM((2, 8, BLK, BLK), BF), pltpu.VMEM((2, 8, BLK, 384), BF)],
-        compiler_params=pltpu.CompilerParams(vmem_limit_bytes=LIMIT),
-    )(d_mixed, perm, slots, probs)
-    sums = sums[::8].reshape(pairs, 3, 128)
-    d_proj = jnp.concatenate([dq, dk, dv], axis=1)
-    g_qkv = jnp.einsum("td,tf->df", x, d_proj, preferred_element_type=jnp.float32).astype(BF)
-    gx = (jnp.einsum("tf,df->td", d_proj, w, preferred_element_type=jnp.float32) + d_res).astype(BF)
-    g_vec = jnp.concatenate([sums[:, 0].reshape(1, -1), sums[:, 2].reshape(1, -1), sums1[:6]])
-    g_aux = jnp.pad(g_vec.T, ((0, 0), (0, 248)))
-    g_aux = g_aux.reshape(32, 24, 256) + jnp.pad(ubsum[0].reshape(32, 1, 96), ((0, 0), (0, 23), (8, 152)))
-    part = jnp.concatenate([g_qkv, g_aux.reshape(768, 256).astype(BF)], axis=1)
-    r_out, r_up, r_qkv, gx_rows = reduce_call(("out", "up", "qkv"), [g_out, g_up, part], [gx], 2)
-    return (out_rows, gx_rows, r_qkv[:, :2304], r_out, r_up, r_down, r_qkv[:, 2304:2312].T, r_qkv[0, 2312:2408])
+    scale = (tokens.shape[1] // H) ** -0.5
+    step = up_bias.shape[0]
+    aux = jnp.pad(vectors.T, ((0, 0), (0, 248))) + jnp.pad(up_bias[None, :], ((0, 23), (128, 128 - step)))
+    x, w, slots, probs, perm, d_res, d_mixed, g_up, g_out, sums, ubsum, out_rows, r_down = front_call(
+        scale, pairs, jnp.concatenate([w_qkv, aux], axis=1), w_out, w_up, w_down,
+        cluster_route[0].reshape(H, 2 * NZ, -1), tokens, upstream)
+    r_qkv, r_up, r_out, gx_rows = back_call(scale, d_mixed, perm, slots, probs, x, w, d_res, g_up, g_out, sums, ubsum)
+    return (out_rows, gx_rows, r_qkv[:, :2304], r_out, r_up, r_down, r_qkv[:, 2304:2312].T, r_qkv[0, 2432:2432 + step])
 
 
 def solution(mesh):

time: 374 us -> 291 us (0.78)
  Pallas kernels: 318 us -> 274 us
  matrix products: 18.5 us -> 0 us
  local copies, waits for them, and re-layouts: 24.6 us -> 11.2 us
  other arithmetic: 11.1 us -> 4.15 us
    pallas_call x5 -> x2, Pallas kernels: 318 us -> 274 us  [the longest x1 176 us: front_call(): pl.pallas_call(functools.partial(front_kernel, scale), out_shape=[bf(rows...]
    dot_general x4 -> x0, matrix products: 18.5 us -> none  [the longest x1 7.54 us: homes(): jnp.dot(x, w, preferred_element_type=jnp.float32) + shifts]
    pallas_call x1 -> x0, local copies, waits for them, and re-layouts: 6.38 us -> none  [gather_call(): pl.pallas_call(functools.partial(gather_kernel, names, na), out_shape=out...]
    unnamed x40 -> x18, local copies, waits for them, and re-layouts: 10.2 us -> 6.92 us
where the time goes in v3:
time: 291 us; the launch traced here: 290 us
  Pallas kernels  274 us (94%)
  local copies, waits for them, and re-layouts  11.2 us (4%)
  other arithmetic  4.15 us (1%)
    pallas_call x1, Pallas kernels, front_call(): pl.pallas_call(functools.partial(front_kernel, scale), out_shape=[bf(rows...  176 us
    pallas_call x1, Pallas kernels, back_call(): pl.pallas_call(functools.partial(back_kernel, scale, pairs), grid=(pairs,...  98.3 us
    unnamed x18, local copies, waits for them, and re-layouts  6.92 us

profile of v3, /device:TPU:1, one launch (start us, length us, event | category | flops | bytes accessed | tf_op | source)
XLA Modules:
  0.0 290.5 jit_solution(5659716510524118080)
XLA Ops:
  0.6 0.8 copy.17
  1.4 0.7 pad_add_fusion
  2.1 1.6 pad_maximum_fusion.qkv_shard
  3.6 1.9 reduce
  5.6 0.3 copy.19
  5.9 0.8 slice.12.route
  6.6 176.2 %shard_map.152 = (bf16[1024,768]{1,0:T(8,128)(2,1)}, bf16[768,2560]{1,0:T(8,128)(2,1)}, bf16[6,2048,384]{2,1,0:T(8,128)(2,1)}, bf16[6,2,1024,128]{3,2,1,0:T(8,12...) custom-call(bf16[24,2560]{1,0:T(8,128)(2,1)} %pad_maximum_fusion.qkv, ...), custom_call_target="tpu_custom_call" | custom-call | tf_op jit(solution)/shard_map/pallas_call | solution.py:872
  182.8 0.0 copy-start
  182.8 98.3 %shard_map.153 = (f32[24,2560]{1,0:T(8,128)}, f32[24,3072]{1,0:T(8,128)}, f32[24,768]{1,0:T(8,128)}, bf16[1024,768]{1,0:T(8,128)(2,1)}) custom-call(bf16[1024,768]{1,0:T(8,128)(2,1)} %get-tuple-element.26.dm_ref, s32[6,8,256]{2,1,0:T(8,128)} %get-tuple-element.27.perm_ref, bf16[6,2048,384]{2,1,0:T(8,128)(2,1)} %get-tuple-element.28.slot_ref, ...), custom_call_target="tpu_custom_call" | custom-call | tf_op jit(solution)/shard_map/pallas_call | solution.py:1019
  281.1 1.2 slice_bitcast_fusion.1
  282.3 0.7 slice_bitcast_fusion
  283.0 1.6 slice.9
  284.6 0.7 copy.18
  285.3 0.0 copy-done
  285.3 0.0 copy-start.1
  285.3 1.1 copy.25
  286.4 0.8 copy-done.1
  287.3 0.0 copy-start.4
  287.3 0.0 copy-start.3
  287.3 0.0 copy-start.2
  287.3 1.1 copy.26
  288.4 0.0 copy-done.4
  288.4 0.6 copy.27
  289.1 0.0 copy-done.3
  289.1 0.7 copy.28
  289.8 0.0 copy-done.2
  289.8 0.7 copy.29
Async XLA Ops:
  182.8 102.5 %copy-start = (bf16[1024,768]{1,0:T(8,128)(2,1)S(1)}, bf16[1024,768]{1,0:T(8,128)(2,1)}, u32[]{:S(2)}) copy-start(bf16[1024,768]{1,0:T(8,128)(2,1)} %get-tuple-element.58) | copy-start | bytes 4718596
  285.3 2.0 copy-start.1
  287.3 1.2 copy-start.4
  287.3 1.8 copy-start.3
  287.3 2.5 copy-start.2

commit v4 on v3

--- a/solution.py
+++ b/solution.py
@@ -260,6 +260,9 @@
         self.dp_x = self.dp + 1 - 2 * self.x
         self.dp_y = self.dp + 2 - 4 * self.y
 
+    def peers(self):
+        return jnp.where(self.core == 0, self.dp_x, self.dp_y), jnp.where(self.core == 0, self.dp_y, self.dp_x)
+
     def new(self):
         self.count += 1
         return self.count - 1
@@ -320,7 +323,9 @@
     i0 = L.new()
     fr = [None] + [L.new() for _ in range(3)]
     fl = [None] + [L.new() for _ in range(3)]
-    ax, by, ay, bx0, bx1, c0, c1, c2 = [L.new() for _ in range(8)]
+    a1, b1, a2, a3, b2, b3, c0, c1, c2 = [L.new() for _ in range(9)]
+    fa, fb = L.peers()
+    opposite = 3 - L.dp
     first = lambda: L.copy(i0, shard.at[:, other], half_buf, L.dp, L.sib)
 
     def right(d, z0):
@@ -390,20 +395,21 @@
     def s4():
         recv_line(3)
         q = lambda: quarter(L.dp)
-        L.go(lambda: same(ax, q(), cols_a, L.dp_x, L.sq), lambda: same(by, q(), cols_b, L.dp_y, L.sq),
+        L.go(lambda: same(a1, q(), cols_a, fa, L.sq), lambda: same(b1, q(), cols_b, fb, L.sq),
              lambda: same(c0, q(), mine, L.dp, L.sib))
 
     def s5():
-        same(ax, quarter(L.dp_x), cols_a, L.dp_x, L.sq).wait_recv()
-        L.go(lambda: same(ay, quarter(2 * L.y, 2), cols_a, L.dp_y, L.sq))
-        same(by, quarter(L.dp_y), cols_b, L.dp_y, L.sq).wait_recv()
-        L.go(lambda: same(bx0, quarter(L.dp), cols_b, L.dp_x, L.sq), lambda: same(bx1, quarter(L.dp_y), cols_b, L.dp_x, L.sq))
+        same(a1, quarter(fa), cols_a, fa, L.sq).wait_recv()
+        L.go(lambda: same(a2, quarter(L.dp), cols_a, fb, L.sq), lambda: same(a3, quarter(fa), cols_a, fb, L.sq))
+        same(b1, quarter(fb), cols_b, fb, L.sq).wait_recv()
+        L.go(lambda: same(b2, quarter(L.dp), cols_b, fa, L.sq), lambda: same(b3, quarter(fb), cols_b, fa, L.sq))
 
     def s6():
-        same(bx0, quarter(L.dp_x), cols_b, L.dp_x, L.sq).wait_recv()
+        same(a2, quarter(fb), cols_a, fb, L.sq).wait_recv()
+        same(b2, quarter(fa), cols_b, fa, L.sq).wait_recv()
         L.go(lambda: same(c1, quarter(L.dp_x), mine, L.dp, L.sib))
-        same(ay, quarter(2 * (1 - L.y), 2), cols_a, L.dp_y, L.sq).wait_recv()
-        same(bx1, quarter(3 - L.dp), cols_b, L.dp_x, L.sq).wait_recv()
+        same(a3, quarter(opposite), cols_a, fb, L.sq).wait_recv()
+        same(b3, quarter(opposite), cols_b, fa, L.sq).wait_recv()
         L.go(lambda: same(c2, quarter(2 * (1 - L.y), 2), mine, L.dp, L.sib))
 
     def s7():
@@ -413,23 +419,27 @@
     return [s0, s1, s2, s3, s4, s5, s6, s7]
 
 
-def spread(L, src, dst, local_sem):
-    ids = [None] + [L.new() for _ in range(2 * NZ - 1)]
-    block = lambda s: pl.ds(mult(s * BLK, BLK), BLK)
-    keep = pltpu.make_async_copy(src.at[block(L.sq)], dst.at[block(L.sq)], local_sem)
-
-    def move(j, to, frm):
-        return L.copy(ids[j], src.at[block(to)], dst.at[block(frm)], L.dp, to)
-
-    def begin():
-        keep.start()
+def spread(L, src, dst, local_sem, parts=1):
+    ids = [[L.new() for _ in range(2 * NZ - 1)] for _ in range(parts)]
+    n = BLK // parts
+    rows = lambda s, i: pl.ds(mult(s * BLK + i * n, n), n)
+
+    def keep(i):
+        return pltpu.make_async_copy(src.at[rows(L.sq, i)], dst.at[rows(L.sq, i)], local_sem.at[i])
+
+    def move(i, j, to, frm):
+        return L.copy(ids[i][j - 1], src.at[rows(to, i)], dst.at[rows(frm, i)], L.dp, to)
+
+    def begin(i=0):
+        keep(i).start()
         for j in range(1, 2 * NZ):
-            L.go(lambda j=j: move(j, lax.rem(L.sq + j, 2 * NZ), L.sq))
+            L.go(lambda j=j: move(i, j, lax.rem(L.sq + j, 2 * NZ), L.sq))
 
     def finish():
-        keep.wait()
-        for j in range(1, 2 * NZ):
-            move(j, L.sq, lax.rem(L.sq + 2 * NZ - j, 2 * NZ)).wait_recv()
+        for i in range(parts):
+            keep(i).wait()
+            for j in range(1, 2 * NZ):
+                move(i, j, L.sq, lax.rem(L.sq + 2 * NZ - j, 2 * NZ)).wait_recv()
     return begin, finish
 
 
@@ -447,15 +457,17 @@
 def reduce_scratch(r, c, split):
     half, (a, b), big = c // 2, split, 2 * r
     bf = lambda *s: pltpu.VMEM(s, jnp.bfloat16)
-    return [bf(32 * r, half), bf(8 * big, a), bf(4 * big, b), bf(4 * big, b), bf(4 * big, a), bf(4 * big, b),
+    return [bf(32 * r, half), bf(2, 4 * big, a), bf(2, 4 * big, b), bf(4 * big, a), bf(4 * big, b),
             bf(3, big, half), bf(3, big, half), pltpu.VMEM((2, r, half), jnp.float32), pltpu.VMEM((r, half), jnp.float32)]
 
 
-N_REDUCE = 14
+N_REDUCE = 15
+N_GATHER = 16
+N_SCRATCH = 9
 
 
 def reduce(L, part, out, scratch, r, split, own=None, sem=None):
-    acc, a1, b1x, b1y, a2, b2, from_l, from_r, fin, got = scratch
+    acc, a1, b1, a2, b2, from_l, from_r, fin, got = scratch
     half = part.shape[1] // 2
     a, b = split
     big = 2 * r
@@ -464,19 +476,21 @@
     ca, cb = pl.ds(0, a), pl.ds(a, b)
     quarter = lambda dp, n=1: pl.ds(mult(dp * NZ * big, 16), n * NZ * big)
     chip = lambda z: pl.ds(mult((L.dp * NZ + z) * big, 16), big)
-    i0, ia1, ibx, iby, ia2, ib2, ifin = [L.new() for _ in range(7)]
+    i0, ia0, ia1, ib0, ib1, ia2, ib2, ifin = [L.new() for _ in range(8)]
+    fb, fa = L.peers()
+    opposite = 3 - L.dp
     ir = [None] + [L.new() for _ in range(3)]
     il = [L.new() for _ in range(3)]
     q = lambda dp: dp * NZ * big
-    other_y = quarter(2 * (1 - L.y), 2)
 
     core_copy = lambda: L.copy(i0, part.at[:, other], acc, L.dp, L.sib)
-    a1_copy = lambda: L.copy(ia1, acc.at[other_y, ca], a1, L.dp_y, L.sq)
-    bx_copy = lambda: L.copy(ibx, acc.at[quarter(L.dp_x), cb], b1x, L.dp_x, L.sq)
-    by_copy = lambda: L.copy(iby, acc.at[quarter(3 - L.dp), cb], b1y, L.dp_x, L.sq)
-    a2_copy = lambda: L.copy(ia2, acc.at[quarter(L.dp_x), ca], a2, L.dp_x, L.sq)
-    b2_copy = lambda: L.copy(ib2, acc.at[quarter(L.dp_y), cb], b2, L.dp_y, L.sq)
-
+    def part_copy(i, dp, cols, to, peer):
+        return L.copy(i, acc.at[quarter(dp), cols], to, peer, L.sq)
+
+    a_copies = [lambda: part_copy(ia0, opposite, ca, a1.at[0], fa), lambda: part_copy(ia1, fa, ca, a1.at[1], fa)]
+    b_copies = [lambda: part_copy(ib0, opposite, cb, b1.at[0], fb), lambda: part_copy(ib1, fb, cb, b1.at[1], fb)]
+    a2_copy = lambda: part_copy(ia2, fb, ca, a2, fb)
+    b2_copy = lambda: part_copy(ib2, fa, cb, b2, fa)
     mine_copy = lambda: pltpu.make_async_copy(part.at[:, mine], own, sem)
 
     def s0():
@@ -496,17 +510,19 @@
             acc[here, :] = (acc[here, :].astype(jnp.float32) + add.astype(jnp.float32)).astype(jnp.bfloat16)
             return 0
         lax.fori_loop(0, acc.shape[0] // step, one, 0)
-        L.go(a1_copy, bx_copy, by_copy)
+        L.go(a_copies[0], b_copies[0], a_copies[1], b_copies[1])
 
     def s2():
-        a1_copy().wait_recv()
-        add_into(acc, q(2 * L.y), ca, a1, 8 * big)
+        a_copies[0]().wait_recv()
+        add_into(acc, q(fb), ca, a1.at[0], 4 * big)
         L.go(a2_copy)
-        bx_copy().wait_recv()
-        by_copy().wait_recv()
-        add_into(acc, q(L.dp_y), cb, b1y, 4 * big)
+        b_copies[0]().wait_recv()
+        add_into(acc, q(fa), cb, b1.at[0], 4 * big)
         L.go(b2_copy)
-        add_into(acc, q(L.dp), cb, b1x, 4 * big)
+        a_copies[1]().wait_recv()
+        add_into(acc, q(L.dp), ca, a1.at[1], 4 * big)
+        b_copies[1]().wait_recv()
+        add_into(acc, q(L.dp), cb, b1.at[1], 4 * big)
 
     def s3():
         a2_copy().wait_recv()
@@ -611,9 +627,10 @@
 
 
 def place_rows(route, perm, me):
-    heads, n, size = route.shape
+    heads, n = route.shape[1], 2 * NZ
+    size = route.shape[2] // n
     base = me * BLK
-    head_row = jnp.concatenate([route[h, 0:1, :] for h in range(heads)] + [jnp.full((16 - heads, size), -1, jnp.int32)], axis=0)
+    head_row = jnp.concatenate([route[0, :, 0:size], jnp.full((16 - heads, size), -1, jnp.int32)], axis=0)
     mine = (head_row >= base) & (head_row < base + BLK)
     flags = jnp.where(mine, 1.0, 0.0).astype(jnp.bfloat16)
     before = []
@@ -623,7 +640,7 @@
         before.append(dot(flags, jnp.where(row < col, 1.0, 0.0).astype(jnp.bfloat16), 1, 0))
     slot = jnp.where(mine, jnp.concatenate(before, axis=1).astype(jnp.int32), -1)
     for h in range(heads):
-        per = route[h]
+        per = jnp.concatenate([route[0, h:h + 1, k * size:(k + 1) * size] for k in range(n)], axis=0)
         local = jnp.where((per >= base) & (per < base + BLK), per - base, 0).astype(jnp.float32).astype(jnp.bfloat16)
         pick = jnp.where(slot[h:h + 1, :] == lax.broadcasted_iota(jnp.int32, (BLK, size), 0), 1.0, 0.0).astype(jnp.bfloat16)
         perm[h // 2, :, pl.ds((h % 2) * BLK, BLK)] = dot(local, pick, 1, 1).astype(jnp.int32)
@@ -678,26 +695,36 @@
 FB = 768
 
 
-def front_kernel(scale, qkv_shard, out_shard, up_shard, down_shard, route, x_rows, up_rows,
-                 x_home, w_home, slots, probs, perm, d_res, d_mixed, g_up, g_out, sums, ubsum, out_rows, r_down,
+def front_kernel(scale, w_shard, out_shard, up_shard, down_shard, vec_shard, ub_shard, route, x_rows, up_rows,
+                 x_home, w_home, slots, probs, d_proj, gx, g_up, g_out, sums, ubsum, out_rows, r_down,
                  w_out, w_up, w_down, act, gp, x, mixed, n1, s1, low, up, outb, dn, gd, head_ref, vec, ub, auxf,
-                 bq, bo, bu, bd, *rest):
-    red, (ss, rs, ls, cs) = rest[:10], rest[10:]
+                 bq, bo, bu, bd, qkv_shard, perm, d_res, *rest):
+    red, (ss, rs, ls, cs) = rest[:N_SCRATCH], rest[N_SCRATCH:]
     rows_here, width = x.shape
     ff = w_up.shape[1]
     pairs = perm.shape[0]
     w = gp.at[pl.ds(0, width), pl.ds(0, qkv_shard.shape[1])]
     da = up
     L = Links(ss, rs)
+    r = w_shard.shape[0]
+    nv, step = vec_shard.shape[0], ub_shard.shape[1]
+    qkv_shard[:, 0:3 * width] = w_shard[...]
+    auxf[...] = jnp.zeros_like(auxf)
+    auxf[0:nv, 0:r] = vec_shard[...].astype(jnp.float32)
+    qkv_shard[:, 3 * width:3 * width + 128] = auxf[0:128, :].T[0:r, :].astype(jnp.bfloat16)
+    auxf[0:nv, :] = jnp.zeros((nv, 128), jnp.float32)
+    auxf[0:1, 0:step] = ub_shard[...].astype(jnp.float32)
+    qkv_shard[:, 3 * width + 128:3 * width + 256] = auxf[0:r, :].astype(jnp.bfloat16)
     L.enter()
     Q = L.under("qkv", gather(L, qkv_shard, w, bq, *SIZES["qkv"][::2]))
     O = L.under("out", gather(L, out_shard, w_out, bo, *SIZES["out"][::2]))
     U = gather(L, up_shard, w_up, bu, *SIZES["up"][::2])
-    D = gather(L, down_shard, w_down, bd, *SIZES["down"][::2])
+    D = L.under("down", gather(L, down_shard, w_down, bd, *SIZES["down"][::2]))
     x_begin, x_finish = spread(L, x_rows, x, ls.at[0])
     up_begin, up_finish = spread(L, up_rows, up, ls.at[1])
     out_begin, out_finish = spread(L, outb, out_rows, ls.at[2])
     R = reduce(L, gd, r_down, red, *SIZES["down"][::2])
+    R = L.under("sum", R[:1]) + R[1:]
     plan = PLAN(Q, O, U, D, x_begin, up_begin, R)
     row = lambda i: vec[i:i + 1, :]
 
@@ -712,9 +739,8 @@
     run(plan["placed"])
     vec[...] = w[:, 2304:2432].astype(jnp.float32).T[0:8, :]
     auxf[...] = w[:, 2432:2560].astype(jnp.float32)
-    step = ff // 32
-    for i in range(32):
-        ub[:, i * step:(i + 1) * step] = auxf[i * 24:i * 24 + 1, 0:step]
+    for i in range(ff // step):
+        ub[:, i * step:(i + 1) * step] = auxf[i * r:i * r + 1, 0:step]
     w_flush = pltpu.make_async_copy(w, w_home, cs.at[0])
     w_flush.start()
     run(plan["weights"])
@@ -737,6 +763,12 @@
         half = rows_here
         return [pltpu.make_async_copy(gd.at[pl.ds(0, 2 * half), pl.ds(mult(par * 384, 128), 384)], slots.at[p], cs.at[2 + 3 * par])] + [
             pltpu.make_async_copy(gd.at[pl.ds(2 * half, half), pl.ds(mult((2 * par + h) * 128, 128), 128)], probs.at[p, h],
+                                  cs.at[3 + 3 * par + h]) for h in range(2)]
+
+    def back_in(p, par):
+        half = rows_here
+        return [pltpu.make_async_copy(slots.at[p], w_down.at[pl.ds(0, 2 * half), pl.ds(mult(par * 384, 128), 384)], cs.at[2 + 3 * par])] + [
+            pltpu.make_async_copy(probs.at[p, h], w_down.at[pl.ds(2 * half, half), pl.ds(mult((2 * par + h) * 128, 128), 128)],
                                   cs.at[3 + 3 * par + h]) for h in range(2)]
 
     def attend(p):
@@ -823,19 +855,56 @@
         x[here, :] = dot(lo, w_out[...], 1, 1).astype(jnp.bfloat16)
 
     loop(rows_here // TB, third, plan["third"])
-    flush = [pltpu.make_async_copy(x, d_mixed, cs.at[0])]
-    flush[0].start()
+    flush = []
+    L.drain(["down"])
+    for p in range(2):
+        for c in back_in(p, p):
+            c.start()
 
     def grad_up(i):
         c = pl.ds(mult(i * FB, FB), FB)
         act[pl.ds(0, width), c] = dot(low[...], gp[:, c], 0, 0).astype(jnp.bfloat16)
 
     loop(ff // FB, grad_up, plan["grad_up"])
-    flush.append(pltpu.make_async_copy(act.at[pl.ds(0, width), :], g_up, cs.at[1]))
-    flush[1].start()
+    flush.append(pltpu.make_async_copy(act.at[pl.ds(0, width), :], g_up, cs.at[8]))
+    flush[-1].start()
     w_out[...] = dot(mixed[...], da[...], 0, 0).astype(jnp.bfloat16)
-    flush.append(pltpu.make_async_copy(w_out, g_out, cs.at[2]))
-    flush[2].start()
+    flush.append(pltpu.make_async_copy(w_out, g_out, cs.at[9]))
+    flush[-1].start()
+    run(plan["grads"])
+    L.drain(["sum"])
+    reload = [pltpu.make_async_copy(w_home.at[:, pl.ds(j * width, width)], gd.at[pl.ds(j * width, width), :], cs.at[10 + j])
+              for j in range(3)]
+    for c in reload:
+        c.start()
+
+    def back(p):
+        par = lax.rem(p, 2)
+        for c in back_in(p, par):
+            c.wait()
+        back_pair(scale, x, perm, w_down, head_ref, gp, sums, p, par)
+
+        @pl.when(p < pairs - 2)
+        def _():
+            for c in back_in(p + 2, par):
+                c.start()
+
+    loop(pairs, back, plan["back"])
+    flush.append(pltpu.make_async_copy(gp.at[:, pl.ds(0, 3 * width)], d_proj, cs.at[0]))
+    flush[-1].start()
+    for c in reload:
+        c.wait()
+
+    def grad_x(m):
+        here = pl.ds(mult(m * TB, TB), TB)
+        total = d_res[here, :]
+        for j in range(3):
+            total = total + dot(gp[here, pl.ds(j * width, width)], gd[pl.ds(j * width, width), :], 1, 1)
+        dn[here, :] = total.astype(jnp.bfloat16)
+
+    loop(rows_here // TB, grad_x)
+    flush.append(pltpu.make_async_copy(dn, gx, cs.at[1]))
+    flush[-1].start()
     run(plan["end"])
     out_finish()
     for f in flush:
@@ -845,207 +914,168 @@
 
 def PLAN(Q, O, U, D, x_begin, up_begin, R):
     return {
-        "start": [Q[0], O[0], U[0], D[0], Q[1], O[1], U[1], Q[2], O[2], U[2], Q[3], O[3], U[3], x_begin, Q[4], D[1]],
-        "placed": [Q[5], O[4], U[4], Q[6], O[5], U[5], Q[7]],
-        "weights": [O[6], U[6]],
-        "project": [(3, D[2])],
-        "attend": [(0, O[7]), (0, U[7]), (1, D[3]), (1, up_begin), (3, D[4])],
-        "first": [(0, D[5]), (3, D[6])],
+        "start": [Q[0],O[0],U[0],D[0],Q[1],O[1],U[1],Q[2],O[2],U[2],Q[3],O[3],U[3],Q[4],x_begin,D[1],Q[5],O[4],U[4]],
+        "placed": [Q[6],Q[7]],
+        "weights": [O[5],U[5]],
+        "project": [(0,D[2]),(3,O[6]),(3,U[6])],
+        "attend": [(0,O[7]),(0,U[7]),(0,D[3]),(0,up_begin),(2,D[4])],
+        "first": [(0,D[5]),(3,D[6])],
         "firsts": [D[7]],
-        "third": [(0, R[1]), (3, R[2])],
-        "grad_up": [(1, R[3]), (1, R[4])],
-        "end": [R[5], R[6], R[7], R[8]],
+        "third": [(0, R[1])],
+        "grad_up": [],
+        "grads": [R[2]],
+        "back": [(1, R[3]), (1, R[4]), (3, R[5]), (4, R[6])],
+        "end": [R[7], R[8]],
     }
 
 
-def front_call(scale, pairs, qkv_shard, w_out, w_up, w_down, route, tokens, upstream):
+def front_call(scale, pairs, w_qkv, w_out, w_up, w_down, vectors, up_bias, route, tokens, upstream):
     rows_here, width = tokens.shape
     ff = w_up.shape[1]
     r, cols, split = SIZES["down"]
-    count = 4 * 15 + 3 * 7 + N_REDUCE
+    wq = SIZES["qkv"][1]
+    count = 4 * N_GATHER + 3 * 7 + N_REDUCE
     f32 = lambda *s: jax.ShapeDtypeStruct(s, jnp.float32)
     bf = lambda *s: jax.ShapeDtypeStruct(s, BF)
     vbf = lambda *s: pltpu.VMEM(s, BF)
     vf = lambda *s: pltpu.VMEM(s, jnp.float32)
     hbm = pl.BlockSpec(memory_space=pl.ANY)
-    wq = qkv_shard.shape[1]
     return pl.pallas_call(
         functools.partial(front_kernel, scale),
         out_shape=[bf(rows_here, width), bf(width, wq), bf(pairs, 2 * rows_here, 384), bf(pairs, 2, rows_here, BLK),
-                   jax.ShapeDtypeStruct((pairs, 2 * NZ, 2 * BLK), jnp.int32), f32(rows_here, width), bf(rows_here, width),
-                   bf(width, ff), bf(width, width), f32(8, width), f32(8, ff), bf(rows_here, width), f32(r, cols)],
-        in_specs=[VM] * 5 + [hbm] * 2,
-        out_specs=[hbm] * 4 + [VM] * 2 + [hbm] * 3 + [VM] * 2 + [hbm, VM],
+                   bf(rows_here, 3 * width), bf(rows_here, width), bf(width, ff), bf(width, width), f32(8, width), f32(8, ff),
+                   bf(rows_here, width), f32(r, cols)],
+        in_specs=[VM] * 7 + [hbm] * 2,
+        out_specs=[hbm] * 8 + [VM] * 2 + [hbm, VM],
         scratch_shapes=[vbf(width, width), vbf(width, ff), vbf(ff, width), vbf(rows_here, ff), vbf(rows_here, ff),
                         vbf(rows_here, width), vbf(rows_here, width), vf(rows_here, width), vf(rows_here, 1)]
         + [vbf(rows_here, width)] * 4
         + [vbf(ff, width), vbf(2 * rows_here, BLK), vf(8, width), vf(1, ff), vf(width, BLK)]
         + [vbf(SIZES[n][0], SIZES[n][1] // 2) for n in ("qkv", "out", "up", "down")]
+        + [vbf(SIZES["qkv"][0], wq), pltpu.VMEM((pairs, 2 * NZ, 2 * BLK), jnp.int32), vf(rows_here, width)]
         + reduce_scratch(r, cols, split)
-        + [pltpu.SemaphoreType.DMA((count,)), pltpu.SemaphoreType.DMA((count,)), pltpu.SemaphoreType.DMA((3,)),
-           pltpu.SemaphoreType.DMA((8,))],
+        + [pltpu.SemaphoreType.DMA((count,)), pltpu.SemaphoreType.DMA((count,)), pltpu.SemaphoreType.DMA((3, 1)),
+           pltpu.SemaphoreType.DMA((13,))],
         compiler_params=pltpu.CompilerParams(collective_id=0, has_side_effects=True, vmem_limit_bytes=62 * 2**20),
-    )(qkv_shard, w_out, w_up, w_down, route, tokens, upstream)
-
-
-def back_pair(scale, dm_ref, perm_ref, slot_ref, prob_ref, up_ref, grad_ref, dp_ref):
-    nblk = dm_ref.shape[0] // BLK
+    )(w_qkv, w_out, w_up, w_down, vectors, up_bias, route, tokens, upstream)
+
+
+def back_pair(scale, dm, perm, pool, up_ref, gp, sums, p, par):
+    nblk = dm.shape[0] // BLK
     share = BLK // nblk
+    half = nblk * BLK
+    width = dm.shape[1]
     keep = head_lanes(128)
+    lane = lambda o: pl.ds(mult(par * 384 + o, 128), 128)
+    col = lambda o: pl.ds(mult(p * 128 + o * width, 128), 128)
     for k in range(nblk):
-        table = one_hot(perm_ref[0, k:k + 1, :], BLK)
-        moved = jnp.where(keep, dot(table, dm_ref[pl.ds(k * BLK, BLK), :], 0, 0), 0.0).astype(jnp.bfloat16)
-        up_ref[:, :, pl.ds(k * share, share), :] = moved.reshape(2, nblk, share, 128)
+        table = one_hot(perm[p, k:k + 1, :], BLK)
+        moved = jnp.where(keep, dot(table, dm[pl.ds(k * BLK, BLK), col(0)], 0, 0), 0.0).astype(jnp.bfloat16)
+        for c in range(2 * nblk):
+            up_ref[pl.ds(c * BLK + k * share, share), :] = moved[c * share:(c + 1) * share]
     for h in range(2):
-        for c in range(0, nblk, BATCH):
-            cs = pl.ds(c, BATCH)
-            rows = pl.ds((h * nblk + c) * BLK, BATCH * BLK)
-            q, kk, v = [slot_ref[0, rows, o:o + 128].reshape(BATCH, BLK, 128) for o in (0, 128, 256)]
-            probs, up = prob_ref[0, h, pl.ds(c * BLK, BATCH * BLK), :].reshape(BATCH, BLK, BLK), up_ref[h, cs]
-            dprobs = bdot(up, v, 2, 2)
-            p32 = probs.astype(jnp.float32)
-            pd = p32 * dprobs
-            dscores = (pd - p32 * jnp.sum(pd, axis=-1, keepdims=True)).astype(jnp.bfloat16)
-            grad_ref[h, cs, :, 0:128] = (bdot(dscores, kk, 2, 1) * scale).astype(jnp.bfloat16)
-            grad_ref[h, cs, :, 128:256] = (bdot(dscores, q, 1, 1) * scale).astype(jnp.bfloat16)
-            grad_ref[h, cs, :, 256:384] = bdot(probs, up, 1, 1).astype(jnp.bfloat16)
+        rows = pl.ds(h * half, half)
+        q, kk, v = [pool[rows, lane(o)].reshape(nblk, BLK, 128) for o in (0, 128, 256)]
+        probs = pool[pl.ds(2 * half, half), pl.ds(mult((2 * par + h) * 128, 128), 128)].reshape(nblk, BLK, BLK)
+        up = up_ref[rows, :].reshape(nblk, BLK, 128)
+        dprobs = bdot(up, v, 2, 2)
+        p32 = probs.astype(jnp.float32)
+        pd = p32 * dprobs
+        dscores = (pd - p32 * jnp.sum(pd, axis=-1, keepdims=True)).astype(jnp.bfloat16)
+        parts = (bdot(dscores, kk, 2, 1) * scale, bdot(dscores, q, 1, 1) * scale, bdot(probs, up, 1, 1))
+        for j, g in enumerate(parts):
+            gp[:, pl.ds(3 * width + h * 384 + j * 128, 128)] = g.reshape(half, 128).astype(jnp.bfloat16)
     total = jnp.zeros((1, 384), jnp.float32)
     for k in range(nblk):
-        table = one_hot(perm_ref[0, k:k + 1, :], BLK)
-        back = grad_ref[:, :, pl.ds(k * share, share), :].reshape(2 * BLK, 384)
+        table = one_hot(perm[p, k:k + 1, :], BLK)
+        back = jnp.concatenate(
+            [gp[pl.ds(c * BLK + k * share, share), pl.ds(3 * width + h * 384, 384)] for h in range(2) for c in range(nblk)], axis=0)
         moved = dot(table, back, 1, 0)
         total = total + jnp.sum(moved, axis=0, keepdims=True)
-        dp_ref[pl.ds(k * BLK, BLK), :] = moved.astype(jnp.bfloat16)
-    return total
-
-
-A_PAIRS = 4
-
-
-def back_kernel(scale, pairs, dm_ref, perm_ref, slot_ref, prob_ref, x_hbm, w_hbm, dres_hbm, gup_hbm, gout_hbm, sums1, ubsum,
-                r_qkv, r_up, r_out, gx_rows,
-                up_ref, grad_ref, dp_ref, x, xt, w, gx, gxb, part_a, part_b, own_up, own_out, vsum, ubs, ra, rb, *rest):
-    red = [rest[10 * i:10 * i + 10] for i in range(4)]
-    ss, rs, ls, cs = rest[40:]
+        for j in range(3):
+            gp[pl.ds(k * BLK, BLK), col(j)] = moved[:, j * 128:(j + 1) * 128].astype(jnp.bfloat16)
+    sums[6:7, col(0)] = total[:, 0:128]
+    sums[7:8, col(0)] = total[:, 256:384]
+
+
+PARTS = 4
+
+
+def back_kernel(x_hbm, dp_hbm, gx_hbm, gup_hbm, gout_hbm, sums, ubsum, r_qkv, r_aux, r_up, r_out, gx_rows,
+                x, dp, part, own_up, own_out, vsum, ubs, ra, *rest):
+    red = [rest[N_SCRATCH * i:N_SCRATCH * (i + 1)] for i in range(3)]
+    ss, rs, ls, cs = rest[3 * N_SCRATCH:]
     width = x.shape[1]
-    p = pl.program_id(0)
     L = Links(ss, rs)
-    up = reduce(L, gup_hbm, r_up, red[0], *SIZES["up"][::2], own=own_up, sem=cs.at[0])
-    ou = reduce(L, gout_hbm, r_out, red[1], *SIZES["out"][::2], own=own_out, sem=cs.at[1])
-    qa = reduce(L, part_a, ra, red[2], 24, (384, 384))
-    qb = reduce(L, part_b, rb, red[3], 24, (256, 256))
-    begin, finish = spread(L, gxb, gx_rows, ls.at[0])
-    loads = [(x_hbm, x, 2), (w_hbm, w, 3), (dres_hbm, gx, 4)]
-
-    @pl.when(p == 0)
-    def _():
-        for a, b, i in loads:
-            pltpu.make_async_copy(a, b, cs.at[i]).start()
-        vsum[...] = jnp.zeros_like(vsum)
-        vsum[2:8, :] = sums1[0:6, :]
-        L.enter()
-        ou[0]()
-        up[0]()
-
-    total = back_pair(scale, dm_ref, perm_ref, slot_ref, prob_ref, up_ref, grad_ref, dp_ref)
-    col = lambda o: pl.ds(mult(p * 128 + o * width, 128), 128)
-    vsum[0:1, col(0)] = total[:, 0:128]
-    vsum[1:2, col(0)] = total[:, 256:384]
-
-    @pl.when(p == 0)
-    def _():
-        for a, b, i in loads:
-            pltpu.make_async_copy(a, b, cs.at[i]).wait()
-        xt[...] = x[...].T
-
-    dp = dp_ref[...]
-    wp = jnp.concatenate([w[:, col(0)], w[:, col(1)], w[:, col(2)]], axis=1)
-    for m in range(0, x.shape[0], 256):
-        gx[m:m + 256, :] += dot(dp[m:m + 256], wp, 1, 1)
-    g = dot(xt[...], dp, 1, 0).astype(jnp.bfloat16)
-
-    @pl.when(p < A_PAIRS)
-    def _():
-        part_a[:, pl.ds(mult(p * 384, 128), 384)] = g
-
-    @pl.when(p >= A_PAIRS)
-    def _():
-        part_b[:, pl.ds(mult((p - A_PAIRS) * 384, 128), 384)] = g
-
-    for at, stage in BACK_PLAN(up, ou, qa):
-        pl.when(p == at)(stage)
-
-    @pl.when(p == pairs - 1)
-    def _():
-        gxb[...] = gx[...].astype(jnp.bfloat16)
-        ubs[...] = jnp.zeros_like(ubs)
-        step = ubsum.shape[1] // 32
-        for i in range(32):
-            ubs[i, 0:1, 0:step] = ubsum[0:1, i * step:(i + 1) * step]
-        wide = jnp.concatenate([vsum[...], jnp.zeros((120, width), jnp.float32)], axis=0)
-        part_b[:, 768:896] = wide.T.astype(jnp.bfloat16)
-        part_b[:, 896:1024] = ubs[...].reshape(width, 128).astype(jnp.bfloat16)
-        for stage in BACK_TAIL(up, ou, qa, qb, begin):
-            stage()
-        finish()
-        for b in range(20):
-            src = ra[:, b * 128:(b + 1) * 128] if b < 12 else rb[:, (b - 12) * 128:(b - 11) * 128]
-            dst = (b // 3 + (b % 3) * pairs) if b < 18 else b
-            r_qkv[:, dst * 128:(dst + 1) * 128] = src
-        L.drain()
-
-
-def BACK_PLAN(up, ou, qa):
-    return [(0, ou[1]), (0, up[1]), (1, ou[2]), (1, up[2]), (2, ou[3]), (2, up[3]), (2, ou[4]), (2, up[4]),
-            (3, qa[0]), (3, ou[5]), (3, up[5]), (4, ou[6]), (4, up[6]), (4, qa[1])]
-
-
-def BACK_TAIL(up, ou, qa, qb, begin):
-    return [qb[0], begin, qa[2], qb[1], ou[7], up[7], qa[3], qb[2], qa[4], qb[3], ou[8], up[8], qb[4], qa[5], qb[5],
-            qa[6], qb[6], qa[7], qb[7], qa[8], qb[8]]
-
-
-def back_call(scale, d_mixed, perm, slots, probs, x, w, d_res, g_up, g_out, sums1, ubsum):
-    pairs = perm.shape[0]
+    U = reduce(L, gup_hbm, r_up, red[0], *SIZES["up"][::2], own=own_up, sem=cs.at[0])
+    O = reduce(L, gout_hbm, r_out, red[1], *SIZES["out"][::2], own=own_out, sem=cs.at[1])
+    Q = reduce(L, part, ra, red[2], *SIZES["qkv"][::2])
+    begin, finish = spread(L, gx_hbm, gx_rows, ls, PARTS)
+    loads = [pltpu.make_async_copy(x_hbm, x, cs.at[2]), pltpu.make_async_copy(dp_hbm, dp, cs.at[3])]
+    for c in loads:
+        c.start()
+    L.enter()
+    G = [functools.partial(begin, i) for i in range(PARTS)]
+    plan = BACK_PLAN(U, O, Q, G)
+    for stage in plan[0]:
+        stage()
+    for c in loads:
+        c.wait()
+    for j in range(0, 3 * width, FB):
+        part[:, j:j + FB] = dot(x[...], dp[:, j:j + FB], 0, 0).astype(jnp.bfloat16)
+    ubs[...] = jnp.zeros_like(ubs)
+    step = ubsum.shape[1] // ubs.shape[0]
+    for i in range(ubs.shape[0]):
+        ubs[i, 0:1, 0:step] = ubsum[0:1, i * step:(i + 1) * step]
+    vsum[...] = jnp.zeros_like(vsum)
+    vsum[0:2, :] = sums[6:8, :]
+    vsum[2:8, :] = sums[0:6, :]
+    part[:, 3 * width:3 * width + 128] = vsum[...].T.astype(jnp.bfloat16)
+    part[:, 3 * width + 128:3 * width + 256] = ubs[...].reshape(width, 128).astype(jnp.bfloat16)
+    for stage in plan[1]:
+        stage()
+    r_qkv[...] = ra[:, 0:3 * width]
+    r_aux[...] = ra[:, 3 * width:3 * width + 256]
+    finish()
+    L.drain()
+
+
+def BACK_PLAN(U, O, Q, G):
+    return ([O[0], U[0], G[0]],
+            [Q[0], O[1], U[1], G[1], Q[1], O[2], U[2], G[2], Q[2], O[3], U[3], O[4], U[4], Q[3], Q[4], G[3],
+             O[5], U[5], Q[5], O[6], U[6], Q[6], O[7], U[7], Q[7], O[8], U[8], Q[8]])
+
+
+def back_call(x, d_proj, gx, g_up, g_out, sums, ubsum):
     rows_here, width = x.shape
-    count = 4 * N_REDUCE + 7
+    count = 3 * N_REDUCE + 7 * PARTS
     hbm = pl.BlockSpec(memory_space=pl.ANY)
     vbf = lambda *s: pltpu.VMEM(s, BF)
     vf = lambda *s: pltpu.VMEM(s, jnp.float32)
     f32 = lambda *s: jax.ShapeDtypeStruct(s, jnp.float32)
-    whole = lambda *s: pl.BlockSpec(s, lambda p: (0,) * len(s))
     r, cu = SIZES["up"][:2]
-    co = SIZES["out"][1]
+    co, cq = SIZES["out"][1], SIZES["qkv"][1]
     return pl.pallas_call(
-        functools.partial(back_kernel, scale, pairs), grid=(pairs,),
-        out_shape=[f32(r, 2560), f32(r, cu), f32(r, co), jax.ShapeDtypeStruct((rows_here, width), BF)],
-        in_specs=[pl.BlockSpec((rows_here, 128), lambda p: (0, p)), pl.BlockSpec((1, 8, 256), lambda p: (p, 0, 0)),
-                  pl.BlockSpec((1, 2 * rows_here, 384), lambda p: (p, 0, 0)),
-                  pl.BlockSpec((1, 2, rows_here, BLK), lambda p: (p, 0, 0, 0))] + [hbm] * 5
-        + [whole(*sums1.shape), whole(*ubsum.shape)],
-        out_specs=[whole(r, 2560), whole(r, cu), whole(r, co), hbm],
-        scratch_shapes=[vbf(2, 8, BLK, BLK), vbf(2, 8, BLK, 384), vbf(rows_here, 384), vbf(rows_here, width),
-                        vbf(width, rows_here), vbf(*w.shape), vf(rows_here, width), vbf(rows_here, width),
-                        vbf(width, 1536), vbf(width, 1024), vbf(32 * r, cu // 2), vbf(32 * r, co // 2),
-                        vf(8, width), vf(32, r, 128), vf(r, 1536), vf(r, 1024)]
-        + reduce_scratch(*SIZES["up"]) + reduce_scratch(*SIZES["out"]) + reduce_scratch(r, 1536, (384, 384))
-        + reduce_scratch(r, 1024, (256, 256))
-        + [pltpu.SemaphoreType.DMA((count,)), pltpu.SemaphoreType.DMA((count,)), pltpu.SemaphoreType.DMA((1,)),
-           pltpu.SemaphoreType.DMA((5,))],
+        back_kernel,
+        out_shape=[f32(r, 3 * width), f32(r, 256), f32(r, cu), f32(r, co), jax.ShapeDtypeStruct((rows_here, width), BF)],
+        in_specs=[hbm] * 5 + [VM] * 2, out_specs=[VM] * 4 + [hbm],
+        scratch_shapes=[vbf(rows_here, width), vbf(rows_here, 3 * width), vbf(width, cq), vbf(32 * r, cu // 2),
+                        vbf(32 * r, co // 2), vf(BLK, width), vf(32, r, BLK), vf(r, cq)]
+        + reduce_scratch(*SIZES["up"]) + reduce_scratch(*SIZES["out"]) + reduce_scratch(*SIZES["qkv"])
+        + [pltpu.SemaphoreType.DMA((count,)), pltpu.SemaphoreType.DMA((count,)), pltpu.SemaphoreType.DMA((PARTS,)),
+           pltpu.SemaphoreType.DMA((4,))],
         compiler_params=pltpu.CompilerParams(collective_id=1, has_side_effects=True, vmem_limit_bytes=LIMIT),
-    )(d_mixed, perm, slots, probs, x, w, d_res, g_up, g_out, sums1, ubsum)
+    )(x, d_proj, gx, g_up, g_out, sums, ubsum)
 
 
 def homes(tokens, w_qkv, w_out, w_up, w_down, vectors, up_bias, cluster_route, upstream):
     pairs = H // 2
     scale = (tokens.shape[1] // H) ** -0.5
     step = up_bias.shape[0]
-    aux = jnp.pad(vectors.T, ((0, 0), (0, 248))) + jnp.pad(up_bias[None, :], ((0, 23), (128, 128 - step)))
-    x, w, slots, probs, perm, d_res, d_mixed, g_up, g_out, sums, ubsum, out_rows, r_down = front_call(
-        scale, pairs, jnp.concatenate([w_qkv, aux], axis=1), w_out, w_up, w_down,
-        cluster_route[0].reshape(H, 2 * NZ, -1), tokens, upstream)
-    r_qkv, r_up, r_out, gx_rows = back_call(scale, d_mixed, perm, slots, probs, x, w, d_res, g_up, g_out, sums, ubsum)
-    return (out_rows, gx_rows, r_qkv[:, :2304], r_out, r_up, r_down, r_qkv[:, 2304:2312].T, r_qkv[0, 2432:2432 + step])
+    x, w, slots, probs, d_proj, gx, g_up, g_out, sums, ubsum, out_rows, r_down = front_call(
+        scale, pairs, w_qkv, w_out, w_up, w_down, vectors, up_bias[None], cluster_route, tokens, upstream)
+    r_qkv, r_aux, r_up, r_out, gx_rows = back_call(x, d_proj, gx, g_up, g_out, sums, ubsum)
+    return (out_rows, gx_rows, r_qkv, r_out, r_up, r_down, r_aux[:, 0:8].T, r_aux[0, 128:128 + step])
 
 
 def solution(mesh):

time: 291 us -> 269 us (0.924)
  Pallas kernels: 274 us -> 258 us
  other arithmetic: 4.15 us -> 0 us
    pallas_call x1, Pallas kernels: 98.3 us -> 80 us  [back_call(): pl.pallas_call(back_kernel, out_shape=[f32(r, 3 * width), f32(r, 256), f3...]
    unnamed x18 -> x20, local copies, waits for them, and re-layouts: 6.92 us -> 8.58 us
where the time goes in v4:
time: 269 us
  Pallas kernels  258 us (96%)
  local copies, waits for them, and re-layouts  10.5 us (4%)
    pallas_call x1, Pallas kernels, front_call(): pl.pallas_call(functools.partial(front_kernel, scale), out_shape=[bf(rows...  178 us
    pallas_call x1, Pallas kernels, back_call(): pl.pallas_call(back_kernel, out_shape=[f32(r, 3 * width), f32(r, 256), f3...  80 us
    unnamed x20, local copies, waits for them, and re-layouts  8.58 us

profile of v4, /device:TPU:1, one launch (start us, length us, event | category | flops | bytes accessed | tf_op | source)
XLA Modules:
  0.0 268.8 jit_solution(1136333966264430297)
XLA Ops:
  0.6 2.0 copy.17.route
  2.7 177.6 %shard_map.152 = (bf16[1024,768]{1,0:T(8,128)(2,1)}, bf16[768,2560]{1,0:T(8,128)(2,1)}, bf16[6,2048,384]{2,1,0:T(8,128)(2,1)}, bf16[6,2,1024,128]{3,2,1,0:T(8,12...) custom-call(bf16[24,2304]{1,0:T(8,128)(2,1)} %w_shard.1, ...), custom_call_target="tpu_custom_call" | custom-call | tf_op jit(solution)/shard_map/pallas_call | solution.py:943
  180.3 0.0 copy-start
  180.3 80.0 %shard_map.153 = (f32[24,2304]{1,0:T(8,128)}, f32[24,256]{1,0:T(8,128)}, f32[24,3072]{1,0:T(8,128)}, f32[24,768]{1,0:T(8,128)}, bf16[1024,768]{1,0:T(8,128)(2,1)}) custom-call(bf16[1024,768]{1,0:T(8,128)(2,1)} %get-tuple-element.23.x_hbm, bf16[1024,2304]{1,0:T(8,128)(2,1)} %get-tuple-element.24.dp_hbm, bf16[1024,768]{1,0:T(8,128)(2,1)} %get-tuple-element.25.gx_hbm, ...), custom_call_target="tpu_custom_call" | custom-call | tf_op jit(solution)/shard_map/pallas_call | solution.py:1058
  260.3 1.2 slice_bitcast_fusion.1
  261.5 0.7 slice_bitcast_fusion
  262.2 0.7 copy.18
  262.9 0.0 copy-done
  262.9 0.0 copy-start.1
  262.9 1.1 copy.25
  264.0 0.8 copy-done.1
  264.9 0.0 copy-start.4
  264.9 0.0 copy-start.5
  264.9 0.0 copy-start.3
  264.9 0.0 copy-start.2
  264.9 1.1 copy.26
  266.0 0.0 copy-done.4
  266.0 0.7 copy.27
  266.7 0.0 copy-done.5
  266.7 0.6 copy.28
  267.3 0.0 copy-done.3
  267.3 0.7 copy.29
  268.1 0.0 copy-done.2
  268.1 0.7 copy.30
Async XLA Ops:
  180.3 82.6 %copy-start = (bf16[1024,768]{1,0:T(8,128)(2,1)S(1)}, bf16[1024,768]{1,0:T(8,128)(2,1)}, u32[]{:S(2)}) copy-start(bf16[1024,768]{1,0:T(8,128)(2,1)} %get-tuple-element.52) | copy-start | bytes 4718596
  262.9 2.0 copy-start.1
  264.9 1.2 copy-start.4
  264.9 1.8 copy-start.5
  264.9 2.5 copy-start.3
  264.9 3.2 %copy-start.2 = (f32[96,768]{1,0:T(8,128)S(1)}, f32[96,768]{1,0:T(8,128)}, u32[]{:S(2)}) copy-start(f32[96,768]{1,0:T(8,128)} %get-tuple-element.57) | copy-start | bytes 884740

commit v5 on v4

--- a/solution.py
+++ b/solution.py
@@ -454,20 +454,28 @@
     lax.fori_loop(0, n // step, one, 0)
 
 
+def landing(r, c, split):
+    half, (a, b), big = c // 2, split, 2 * r
+    return [(32 * r, half), (4 * big, a), (4 * big, a), (4 * big, b), (4 * big, b), (4 * big, a), (4 * big, b)]
+
+
+def line_scratch(r, c):
+    half, big = c // 2, 2 * r
+    return [pltpu.VMEM((3, big, half), jnp.bfloat16)] * 2 + [pltpu.VMEM((2, r, half), jnp.float32), pltpu.VMEM((r, half), jnp.float32)]
+
+
 def reduce_scratch(r, c, split):
-    half, (a, b), big = c // 2, split, 2 * r
-    bf = lambda *s: pltpu.VMEM(s, jnp.bfloat16)
-    return [bf(32 * r, half), bf(2, 4 * big, a), bf(2, 4 * big, b), bf(4 * big, a), bf(4 * big, b),
-            bf(3, big, half), bf(3, big, half), pltpu.VMEM((2, r, half), jnp.float32), pltpu.VMEM((r, half), jnp.float32)]
+    return [pltpu.VMEM(shape, jnp.bfloat16) for shape in landing(r, c, split)] + line_scratch(r, c)
 
 
 N_REDUCE = 15
 N_GATHER = 16
-N_SCRATCH = 9
-
-
-def reduce(L, part, out, scratch, r, split, own=None, sem=None):
-    acc, a1, b1, a2, b2, from_l, from_r, fin, got = scratch
+N_SCRATCH = 11
+N_LINE = 4
+
+
+def reduce(L, part, out, scratch, r, split):
+    acc, a10, a11, b10, b11, a2, b2, from_l, from_r, fin, got = scratch
     half = part.shape[1] // 2
     a, b = split
     big = 2 * r
@@ -487,42 +495,35 @@
     def part_copy(i, dp, cols, to, peer):
         return L.copy(i, acc.at[quarter(dp), cols], to, peer, L.sq)
 
-    a_copies = [lambda: part_copy(ia0, opposite, ca, a1.at[0], fa), lambda: part_copy(ia1, fa, ca, a1.at[1], fa)]
-    b_copies = [lambda: part_copy(ib0, opposite, cb, b1.at[0], fb), lambda: part_copy(ib1, fb, cb, b1.at[1], fb)]
+    a_copies = [lambda: part_copy(ia0, opposite, ca, a10, fa), lambda: part_copy(ia1, fa, ca, a11, fa)]
+    b_copies = [lambda: part_copy(ib0, opposite, cb, b10, fb), lambda: part_copy(ib1, fb, cb, b11, fb)]
     a2_copy = lambda: part_copy(ia2, fb, ca, a2, fb)
     b2_copy = lambda: part_copy(ib2, fa, cb, b2, fa)
-    mine_copy = lambda: pltpu.make_async_copy(part.at[:, mine], own, sem)
-
     def s0():
         L.go(core_copy)
-        if own is not None:
-            mine_copy().start()
 
     def s1():
         core_copy().wait_recv()
-        if own is not None:
-            mine_copy().wait()
         step = 48
 
         def one(i, _):
             here = pl.ds(mult(i * step, 16), step)
-            add = part[here, mine] if own is None else own[here, :]
-            acc[here, :] = (acc[here, :].astype(jnp.float32) + add.astype(jnp.float32)).astype(jnp.bfloat16)
+            acc[here, :] = (acc[here, :].astype(jnp.float32) + part[here, mine].astype(jnp.float32)).astype(jnp.bfloat16)
             return 0
-        lax.fori_loop(0, acc.shape[0] // step, one, 0)
+        lax.fori_loop(0, 32 * r // step, one, 0)
         L.go(a_copies[0], b_copies[0], a_copies[1], b_copies[1])
 
     def s2():
         a_copies[0]().wait_recv()
-        add_into(acc, q(fb), ca, a1.at[0], 4 * big)
+        add_into(acc, q(fb), ca, a10, 4 * big)
         L.go(a2_copy)
         b_copies[0]().wait_recv()
-        add_into(acc, q(fa), cb, b1.at[0], 4 * big)
+        add_into(acc, q(fa), cb, b10, 4 * big)
         L.go(b2_copy)
         a_copies[1]().wait_recv()
-        add_into(acc, q(L.dp), ca, a1.at[1], 4 * big)
+        add_into(acc, q(L.dp), ca, a11, 4 * big)
         b_copies[1]().wait_recv()
-        add_into(acc, q(L.dp), cb, b1.at[1], 4 * big)
+        add_into(acc, q(L.dp), cb, b11, 4 * big)
 
     def s3():
         a2_copy().wait_recv()
@@ -695,11 +696,13 @@
 FB = 768
 
 
-def front_kernel(scale, w_shard, out_shard, up_shard, down_shard, vec_shard, ub_shard, route, x_rows, up_rows,
-                 x_home, w_home, slots, probs, d_proj, gx, g_up, g_out, sums, ubsum, out_rows, r_down,
+def layer_kernel(scale, w_shard, out_shard, up_shard, down_shard, vec_shard, ub_shard, route, x_rows, up_rows,
+                 x_home, w_home, slots, probs, out_rows, gx_rows, r_qkv, r_aux, r_out, r_up, r_down,
                  w_out, w_up, w_down, act, gp, x, mixed, n1, s1, low, up, outb, dn, gd, head_ref, vec, ub, auxf,
-                 bq, bo, bu, bd, qkv_shard, perm, d_res, *rest):
-    red, (ss, rs, ls, cs) = rest[:N_SCRATCH], rest[N_SCRATCH:]
+                 bq, bo, bu, bd, qkv_shard, perm, d_res, s2, sums, ubsum, ra, *rest):
+    own = [rest[i:i + N_SCRATCH] for i in (0, N_SCRATCH)]
+    late = rest[2 * N_SCRATCH:2 * N_SCRATCH + 3 + 2 * N_LINE]
+    ss, rs, ls, cs = rest[2 * N_SCRATCH + 3 + 2 * N_LINE:]
     rows_here, width = x.shape
     ff = w_up.shape[1]
     pairs = perm.shape[0]
@@ -718,14 +721,25 @@
     L.enter()
     Q = L.under("qkv", gather(L, qkv_shard, w, bq, *SIZES["qkv"][::2]))
     O = L.under("out", gather(L, out_shard, w_out, bo, *SIZES["out"][::2]))
-    U = gather(L, up_shard, w_up, bu, *SIZES["up"][::2])
+    U = L.under("up", gather(L, up_shard, w_up, bu, *SIZES["up"][::2]))
     D = L.under("down", gather(L, down_shard, w_down, bd, *SIZES["down"][::2]))
     x_begin, x_finish = spread(L, x_rows, x, ls.at[0])
     up_begin, up_finish = spread(L, up_rows, up, ls.at[1])
     out_begin, out_finish = spread(L, outb, out_rows, ls.at[2])
-    R = reduce(L, gd, r_down, red, *SIZES["down"][::2])
+    gx_begin, gx_finish = spread(L, dn, gx_rows, ls.at[3], PARTS)
+    g_up, part = act.at[pl.ds(0, width), :], act.at[pl.ds(0, width), pl.ds(0, SIZES["qkv"][1])]
+    spare = [act.at[pl.ds(width, r * 8), pl.ds(i * width, width)] for i in range(4)]
+    hq = SIZES["qkv"][1] // 2
+    spare_q = [w_up.at[:, pl.ds(0, hq)]] + [w_up.at[pl.ds(i * r * 8, r * 8), pl.ds(hq + j * hq // 2, hq // 2)]
+                                          for j in range(2) for i in range(3)]
+    R = reduce(L, gd, r_down, own[0], *SIZES["down"][::2])
     R = L.under("sum", R[:1]) + R[1:]
+    SO = reduce(L, w_out, r_out, own[1], *SIZES["out"][::2])
+    SU = reduce(L, g_up, r_up, [late[0], *spare, *late[1:3 + N_LINE]], *SIZES["up"][::2])
+    SU = L.under("sum_up", SU[:1]) + SU[1:]
+    SQ = reduce(L, part, ra, [*spare_q, *late[3 + N_LINE:]], *SIZES["qkv"][::2])
     plan = PLAN(Q, O, U, D, x_begin, up_begin, R)
+    plan.update(LATE(R, SO, SU, SQ, [functools.partial(gx_begin, i) for i in range(PARTS)]))
     row = lambda i: vec[i:i + 1, :]
 
     def run(stages):
@@ -803,29 +817,37 @@
 
     loop(rows_here // TB, first_half, plan["first"])
     run(plan["firsts"])
-    up_finish()
     for p in range(pairs - 2, pairs):
         for c in kept(p, p % 2):
             c.wait()
     x_flush.wait()
 
-    def second_half(m):
+    def second(m):
         here = pl.ds(mult(m * TB, TB), TB)
         first = n1[here, :] * row(4) + row(5)
         r2 = first + dot(act[here, :], w_down[...], 1, 0) + row(3)
-        n2, s2 = moments(r2)
+        n2, inv = moments(r2)
         outb[here, :] = (n2 * row(6) + row(7)).astype(jnp.bfloat16)
+        d_res[here, :] = n2
+        s2[here, :] = inv
+
+    loop(rows_here // TB, second)
+    out_begin()
+    up_finish()
+
+    def second_back(m):
+        here = pl.ds(mult(m * TB, TB), TB)
+        n2 = d_res[here, :]
         g = up[here, :].astype(jnp.float32)
         sums[4:5, :] += jnp.sum(g * n2, axis=0, keepdims=True)
         sums[5:6, :] += jnp.sum(g, axis=0, keepdims=True)
-        d = norm_back(g, n2, s2, row(6))
+        d = norm_back(g, n2, s2[here, :], row(6))
         d_res[here, :] = d
         lo = d.astype(jnp.bfloat16)
         dn[here, :] = lo
         sums[1:2, :] += jnp.sum(lo.astype(jnp.float32), axis=0, keepdims=True)
 
-    loop(rows_here // TB, second_half)
-    out_begin()
+    loop(rows_here // TB, second_back)
 
     def grad_down(i):
         c = pl.ds(mult(i * FB, FB), FB)
@@ -855,7 +877,6 @@
         x[here, :] = dot(lo, w_out[...], 1, 1).astype(jnp.bfloat16)
 
     loop(rows_here // TB, third, plan["third"])
-    flush = []
     L.drain(["down"])
     for p in range(2):
         for c in back_in(p, p):
@@ -866,12 +887,10 @@
         act[pl.ds(0, width), c] = dot(low[...], gp[:, c], 0, 0).astype(jnp.bfloat16)
 
     loop(ff // FB, grad_up, plan["grad_up"])
-    flush.append(pltpu.make_async_copy(act.at[pl.ds(0, width), :], g_up, cs.at[8]))
-    flush[-1].start()
+    L.drain(["up"])
+    run(plan["up_ready"])
     w_out[...] = dot(mixed[...], da[...], 0, 0).astype(jnp.bfloat16)
-    flush.append(pltpu.make_async_copy(w_out, g_out, cs.at[9]))
-    flush[-1].start()
-    run(plan["grads"])
+    run(plan["out_ready"])
     L.drain(["sum"])
     reload = [pltpu.make_async_copy(w_home.at[:, pl.ds(j * width, width)], gd.at[pl.ds(j * width, width), :], cs.at[10 + j])
               for j in range(3)]
@@ -890,8 +909,8 @@
                 c.start()
 
     loop(pairs, back, plan["back"])
-    flush.append(pltpu.make_async_copy(gp.at[:, pl.ds(0, 3 * width)], d_proj, cs.at[0]))
-    flush[-1].start()
+    x_again = pltpu.make_async_copy(x_home, x, cs.at[0])
+    x_again.start()
     for c in reload:
         c.wait()
 
@@ -903,12 +922,28 @@
         dn[here, :] = total.astype(jnp.bfloat16)
 
     loop(rows_here // TB, grad_x)
-    flush.append(pltpu.make_async_copy(dn, gx, cs.at[1]))
-    flush[-1].start()
+    run(plan["x_ready"])
+    x_again.wait()
+    L.drain(["sum_up"])
+
+    def grad_qkv(i):
+        c = pl.ds(mult(i * FB, FB), FB)
+        part[:, c] = dot(x[...], gp[:, c], 0, 0).astype(jnp.bfloat16)
+
+    loop(3 * width // FB, grad_qkv)
+    d_res[0:BLK, :] = jnp.zeros((BLK, width), jnp.float32)
+    d_res[0:2, :] = sums[6:8, :]
+    d_res[2:8, :] = sums[0:6, :]
+    part[:, 3 * width:3 * width + 128] = d_res[0:BLK, :].T.astype(jnp.bfloat16)
+    auxf[...] = jnp.zeros_like(auxf)
+    for i in range(ff // step):
+        auxf[i * r:i * r + 1, 0:step] = ubsum[0:1, i * step:(i + 1) * step]
+    part[:, 3 * width + 128:3 * width + 256] = auxf[...].astype(jnp.bfloat16)
     run(plan["end"])
+    r_qkv[...] = ra[:, 0:3 * width]
+    r_aux[...] = ra[:, 3 * width:3 * width + 256]
     out_finish()
-    for f in flush:
-        f.wait()
+    gx_finish()
     L.drain()
 
 
@@ -917,44 +952,59 @@
         "start": [Q[0],O[0],U[0],D[0],Q[1],O[1],U[1],Q[2],O[2],U[2],Q[3],O[3],U[3],Q[4],x_begin,D[1],Q[5],O[4],U[4]],
         "placed": [Q[6],Q[7]],
         "weights": [O[5],U[5]],
-        "project": [(0,D[2]),(3,O[6]),(3,U[6])],
-        "attend": [(0,O[7]),(0,U[7]),(0,D[3]),(0,up_begin),(2,D[4])],
+        "project": [(1,D[2])],
+        "attend": [(0,D[3]),(0,up_begin),(0,O[6]),(0,U[6]),(2,O[7]),(2,U[7]),(3,D[4])],
         "first": [(0,D[5]),(3,D[6])],
         "firsts": [D[7]],
+    }
+
+
+def LATE(R, O, U, Q, G):
+    return {
         "third": [(0, R[1])],
         "grad_up": [],
-        "grads": [R[2]],
-        "back": [(1, R[3]), (1, R[4]), (3, R[5]), (4, R[6])],
-        "end": [R[7], R[8]],
+        "up_ready": [U[0]],
+        "out_ready": [O[0], R[2]],
+        "back": [(0, U[1]), (1, R[3]), (1, R[4]), (2, O[1]), (3, R[5]), (4, R[6]), (5, R[7])],
+        "x_ready": [G[0], G[1], U[2], O[2]],
+        "end": [Q[0], R[8], U[3], U[4], G[2], Q[1], O[3], O[4], U[5], G[3], Q[2], U[6], O[5], Q[3], Q[4], O[6], Q[5], U[7], O[7],
+                Q[6], Q[7], U[8], O[8], Q[8]],
     }
 
 
-def front_call(scale, pairs, w_qkv, w_out, w_up, w_down, vectors, up_bias, route, tokens, upstream):
+PARTS = 4
+
+
+def layer_call(scale, pairs, w_qkv, w_out, w_up, w_down, vectors, up_bias, route, tokens, upstream):
     rows_here, width = tokens.shape
     ff = w_up.shape[1]
     r, cols, split = SIZES["down"]
     wq = SIZES["qkv"][1]
-    count = 4 * N_GATHER + 3 * 7 + N_REDUCE
+    count = 4 * (N_GATHER + N_REDUCE) + 7 * (3 + PARTS)
     f32 = lambda *s: jax.ShapeDtypeStruct(s, jnp.float32)
     bf = lambda *s: jax.ShapeDtypeStruct(s, BF)
     vbf = lambda *s: pltpu.VMEM(s, BF)
     vf = lambda *s: pltpu.VMEM(s, jnp.float32)
     hbm = pl.BlockSpec(memory_space=pl.ANY)
+    ru = landing(*SIZES["up"])
+    rq = SIZES["qkv"][0]
     return pl.pallas_call(
-        functools.partial(front_kernel, scale),
+        functools.partial(layer_kernel, scale),
         out_shape=[bf(rows_here, width), bf(width, wq), bf(pairs, 2 * rows_here, 384), bf(pairs, 2, rows_here, BLK),
-                   bf(rows_here, 3 * width), bf(rows_here, width), bf(width, ff), bf(width, width), f32(8, width), f32(8, ff),
-                   bf(rows_here, width), f32(r, cols)],
+                   bf(rows_here, width), bf(rows_here, width), f32(rq, 3 * width), f32(rq, 256), f32(*SIZES["out"][:2]),
+                   f32(*SIZES["up"][:2]), f32(r, cols)],
         in_specs=[VM] * 7 + [hbm] * 2,
-        out_specs=[hbm] * 8 + [VM] * 2 + [hbm, VM],
+        out_specs=[hbm] * 6 + [VM] * 5,
         scratch_shapes=[vbf(width, width), vbf(width, ff), vbf(ff, width), vbf(rows_here, ff), vbf(rows_here, ff),
                         vbf(rows_here, width), vbf(rows_here, width), vf(rows_here, width), vf(rows_here, 1)]
         + [vbf(rows_here, width)] * 4
         + [vbf(ff, width), vbf(2 * rows_here, BLK), vf(8, width), vf(1, ff), vf(width, BLK)]
         + [vbf(SIZES[n][0], SIZES[n][1] // 2) for n in ("qkv", "out", "up", "down")]
-        + [vbf(SIZES["qkv"][0], wq), pltpu.VMEM((pairs, 2 * NZ, 2 * BLK), jnp.int32), vf(rows_here, width)]
-        + reduce_scratch(r, cols, split)
-        + [pltpu.SemaphoreType.DMA((count,)), pltpu.SemaphoreType.DMA((count,)), pltpu.SemaphoreType.DMA((3, 1)),
+        + [vbf(rq, wq), pltpu.VMEM((pairs, 2 * NZ, 2 * BLK), jnp.int32), vf(rows_here, width), vf(rows_here, 1), vf(8, width),
+           vf(8, ff), vf(rq, wq)]
+        + reduce_scratch(r, cols, split) + reduce_scratch(*SIZES["out"])
+        + [vbf(*ru[0]), vbf(*ru[5]), vbf(*ru[6])] + line_scratch(*SIZES["up"][:2]) + line_scratch(rq, wq)
+        + [pltpu.SemaphoreType.DMA((count,)), pltpu.SemaphoreType.DMA((count,)), pltpu.SemaphoreType.DMA((4, PARTS)),
            pltpu.SemaphoreType.DMA((13,))],
         compiler_params=pltpu.CompilerParams(collective_id=0, has_side_effects=True, vmem_limit_bytes=62 * 2**20),
     )(w_qkv, w_out, w_up, w_down, vectors, up_bias, route, tokens, upstream)
@@ -998,83 +1048,12 @@
     sums[7:8, col(0)] = total[:, 256:384]
 
 
-PARTS = 4
-
-
-def back_kernel(x_hbm, dp_hbm, gx_hbm, gup_hbm, gout_hbm, sums, ubsum, r_qkv, r_aux, r_up, r_out, gx_rows,
-                x, dp, part, own_up, own_out, vsum, ubs, ra, *rest):
-    red = [rest[N_SCRATCH * i:N_SCRATCH * (i + 1)] for i in range(3)]
-    ss, rs, ls, cs = rest[3 * N_SCRATCH:]
-    width = x.shape[1]
-    L = Links(ss, rs)
-    U = reduce(L, gup_hbm, r_up, red[0], *SIZES["up"][::2], own=own_up, sem=cs.at[0])
-    O = reduce(L, gout_hbm, r_out, red[1], *SIZES["out"][::2], own=own_out, sem=cs.at[1])
-    Q = reduce(L, part, ra, red[2], *SIZES["qkv"][::2])
-    begin, finish = spread(L, gx_hbm, gx_rows, ls, PARTS)
-    loads = [pltpu.make_async_copy(x_hbm, x, cs.at[2]), pltpu.make_async_copy(dp_hbm, dp, cs.at[3])]
-    for c in loads:
-        c.start()
-    L.enter()
-    G = [functools.partial(begin, i) for i in range(PARTS)]
-    plan = BACK_PLAN(U, O, Q, G)
-    for stage in plan[0]:
-        stage()
-    for c in loads:
-        c.wait()
-    for j in range(0, 3 * width, FB):
-        part[:, j:j + FB] = dot(x[...], dp[:, j:j + FB], 0, 0).astype(jnp.bfloat16)
-    ubs[...] = jnp.zeros_like(ubs)
-    step = ubsum.shape[1] // ubs.shape[0]
-    for i in range(ubs.shape[0]):
-        ubs[i, 0:1, 0:step] = ubsum[0:1, i * step:(i + 1) * step]
-    vsum[...] = jnp.zeros_like(vsum)
-    vsum[0:2, :] = sums[6:8, :]
-    vsum[2:8, :] = sums[0:6, :]
-    part[:, 3 * width:3 * width + 128] = vsum[...].T.astype(jnp.bfloat16)
-    part[:, 3 * width + 128:3 * width + 256] = ubs[...].reshape(width, 128).astype(jnp.bfloat16)
-    for stage in plan[1]:
-        stage()
-    r_qkv[...] = ra[:, 0:3 * width]
-    r_aux[...] = ra[:, 3 * width:3 * width + 256]
-    finish()
-    L.drain()
-
-
-def BACK_PLAN(U, O, Q, G):
-    return ([O[0], U[0], G[0]],
-            [Q[0], O[1], U[1], G[1], Q[1], O[2], U[2], G[2], Q[2], O[3], U[3], O[4], U[4], Q[3], Q[4], G[3],
-             O[5], U[5], Q[5], O[6], U[6], Q[6], O[7], U[7], Q[7], O[8], U[8], Q[8]])
-
-
-def back_call(x, d_proj, gx, g_up, g_out, sums, ubsum):
-    rows_here, width = x.shape
-    count = 3 * N_REDUCE + 7 * PARTS
-    hbm = pl.BlockSpec(memory_space=pl.ANY)
-    vbf = lambda *s: pltpu.VMEM(s, BF)
-    vf = lambda *s: pltpu.VMEM(s, jnp.float32)
-    f32 = lambda *s: jax.ShapeDtypeStruct(s, jnp.float32)
-    r, cu = SIZES["up"][:2]
-    co, cq = SIZES["out"][1], SIZES["qkv"][1]
-    return pl.pallas_call(
-        back_kernel,
-        out_shape=[f32(r, 3 * width), f32(r, 256), f32(r, cu), f32(r, co), jax.ShapeDtypeStruct((rows_here, width), BF)],
-        in_specs=[hbm] * 5 + [VM] * 2, out_specs=[VM] * 4 + [hbm],
-        scratch_shapes=[vbf(rows_here, width), vbf(rows_here, 3 * width), vbf(width, cq), vbf(32 * r, cu // 2),
-                        vbf(32 * r, co // 2), vf(BLK, width), vf(32, r, BLK), vf(r, cq)]
-        + reduce_scratch(*SIZES["up"]) + reduce_scratch(*SIZES["out"]) + reduce_scratch(*SIZES["qkv"])
-        + [pltpu.SemaphoreType.DMA((count,)), pltpu.SemaphoreType.DMA((count,)), pltpu.SemaphoreType.DMA((PARTS,)),
-           pltpu.SemaphoreType.DMA((4,))],
-        compiler_params=pltpu.CompilerParams(collective_id=1, has_side_effects=True, vmem_limit_bytes=LIMIT),
-    )(x, d_proj, gx, g_up, g_out, sums, ubsum)
-
-
 def homes(tokens, w_qkv, w_out, w_up, w_down, vectors, up_bias, cluster_route, upstream):
     pairs = H // 2
     scale = (tokens.shape[1] // H) ** -0.5
     step = up_bias.shape[0]
-    x, w, slots, probs, d_proj, gx, g_up, g_out, sums, ubsum, out_rows, r_down = front_call(
-        scale, pairs, w_qkv, w_out, w_up, w_down, vectors, up_bias[None], cluster_route, tokens, upstream)
-    r_qkv, r_aux, r_up, r_out, gx_rows = back_call(x, d_proj, gx, g_up, g_out, sums, ubsum)
+    out_rows, gx_rows, r_qkv, r_aux, r_out, r_up, r_down = layer_call(
+        scale, pairs, w_qkv, w_out, w_up, w_down, vectors, up_bias[None], cluster_route, tokens, upstream)[4:]
     return (out_rows, gx_rows, r_qkv, r_out, r_up, r_down, r_aux[:, 0:8].T, r_aux[0, 128:128 + step])
 
 

time: 269 us -> 240 us (0.89)
  Pallas kernels: 258 us -> 228 us
    pallas_call x2 -> x1, Pallas kernels: 258 us -> 228 us  [layer_call(): pl.pallas_call(functools.partial(layer_kernel, scale), out_shape=[bf(rows...]
    unnamed x20 -> x18, local copies, waits for them, and re-layouts: 8.58 us -> 9.37 us
where the time goes in v5:
time: 240 us
  Pallas kernels  228 us (95%)
  local copies, waits for them, and re-layouts  11.3 us (5%)
    pallas_call x1, Pallas kernels, layer_call(): pl.pallas_call(functools.partial(layer_kernel, scale), out_shape=[bf(rows...  228 us
    unnamed x18, local copies, waits for them, and re-layouts  9.37 us

profile of v5, /device:TPU:1, one launch (start us, length us, event | category | flops | bytes accessed | tf_op | source)
XLA Modules:
  0.0 240.1 jit_solution(14625830849476477707)
XLA Ops:
  0.6 2.0 copy.17.route
  2.7 228.1 %shard_map.152 = (bf16[1024,768]{1,0:T(8,128)(2,1)}, bf16[768,2560]{1,0:T(8,128)(2,1)}, bf16[6,2048,384]{2,1,0:T(8,128)(2,1)}, bf16[6,2,1024,128]{3,2,1,0:T(8,12...) custom-call(bf16[24,2304]{1,0:T(8,128)(2,1)} %w_shard.1, ...), custom_call_target="tpu_custom_call" | custom-call | tf_op jit(solution)/shard_map/pallas_call | solution.py:991
  230.8 1.2 slice_bitcast_fusion.1
  232.0 0.7 slice_bitcast_fusion
  232.7 0.7 copy.18
  233.4 0.0 copy-start
  233.4 2.8 %copy.25 = bf16[1024,768]{1,0:T(8,128)(2,1)} copy(bf16[1024,768]{1,0:T(8,128)(2,1)} %get-tuple-element.38) | data formatting | bytes 3145728
  236.1 0.0 copy-done
  236.1 0.0 copy-start.3
  236.1 0.0 copy-start.4
  236.1 0.0 copy-start.2
  236.1 0.0 copy-start.1
  236.1 1.1 copy.26
  237.3 0.0 copy-done.3
  237.3 0.7 copy.27
  238.0 0.0 copy-done.4
  238.0 0.6 copy.28
  238.6 0.0 copy-done.2
  238.6 0.7 copy.29
  239.3 0.0 copy-done.1
  239.3 0.7 copy.30
Async XLA Ops:
  233.4 2.8 %copy-start = (bf16[1024,768]{1,0:T(8,128)(2,1)S(1)}, bf16[1024,768]{1,0:T(8,128)(2,1)}, u32[]{:S(2)}) copy-start(bf16[1024,768]{1,0:T(8,128)(2,1)} %get-tuple-element.39) | copy-start | bytes 4718596
  236.1 1.2 copy-start.3
  236.1 1.9 copy-start.4
  236.1 2.5 %copy-start.2 = (f32[24,3072]{1,0:T(8,128)S(1)}, f32[24,3072]{1,0:T(8,128)}, u32[]{:S(2)}) copy-start(f32[24,3072]{1,0:T(8,128)} %get-tuple-element.42) | copy-start | bytes 884740
  236.1 3.2 %copy-start.1 = (f32[96,768]{1,0:T(8,128)S(1)}, f32[96,768]{1,0:T(8,128)}, u32[]{:S(2)}) copy-start(f32[96,768]{1,0:T(8,128)} %get-tuple-element.43) | copy-start | bytes 884740

commit v6 on v5

--- a/solution.py
+++ b/solution.py
@@ -444,12 +444,12 @@
 
 
 def add_into(dst, rows0, cols, src, n):
-    step = 48
+    step = 192
 
     def one(i, _):
         here = pl.ds(mult(i * step, 16), step)
         there = pl.ds(mult(rows0 + i * step, 16), step)
-        dst[there, cols] = (dst[there, cols].astype(jnp.float32) + src[here, :].astype(jnp.float32)).astype(jnp.bfloat16)
+        dst[there, cols] = dst[there, cols] + src[here, :]
         return 0
     lax.fori_loop(0, n // step, one, 0)
 
@@ -504,11 +504,11 @@
 
     def s1():
         core_copy().wait_recv()
-        step = 48
+        step = 192
 
         def one(i, _):
             here = pl.ds(mult(i * step, 16), step)
-            acc[here, :] = (acc[here, :].astype(jnp.float32) + part[here, mine].astype(jnp.float32)).astype(jnp.bfloat16)
+            acc[here, :] = acc[here, :] + part[here, mine]
             return 0
         lax.fori_loop(0, 32 * r // step, one, 0)
         L.go(a_copies[0], b_copies[0], a_copies[1], b_copies[1])
@@ -620,7 +620,8 @@
 BATCH = 8
 
 
-SIZES = {"qkv": (24, 2560, (640, 640)), "out": (24, 768, (256, 128)), "up": (24, 3072, (768, 768)), "down": (96, 768, (128, 256))}
+SIZES = {"qkv": (24, 2560, (640, 640)), "out": (24, 768, (256, 128)), "up": (24, 3072, (768, 768)), "down": (96, 768, (128, 256)),
+         "qk": (24, 1536, (384, 384)), "v": (24, 1024, (256, 256))}
 ALL = ("dp", "seq")
 VM = pl.BlockSpec(memory_space=pltpu.VMEM)
 BF = jnp.bfloat16
@@ -628,10 +629,13 @@
 
 
 def place_rows(route, perm, me):
-    heads, n = route.shape[1], 2 * NZ
-    size = route.shape[2] // n
+    heads, n = 2 * perm.shape[0], 2 * NZ
+    size = route.shape[0] * BLK // (heads * n)
+    chunks = size // BLK
     base = me * BLK
-    head_row = jnp.concatenate([route[0, :, 0:size], jnp.full((16 - heads, size), -1, jnp.int32)], axis=0)
+    pers = [jnp.concatenate([route[pl.ds((h * n) * chunks + c, n, stride=chunks), :] for c in range(chunks)], axis=1)
+            for h in range(heads)]
+    head_row = jnp.concatenate([per[0:1] for per in pers] + [jnp.full((16 - heads, size), -1, jnp.int32)], axis=0)
     mine = (head_row >= base) & (head_row < base + BLK)
     flags = jnp.where(mine, 1.0, 0.0).astype(jnp.bfloat16)
     before = []
@@ -641,7 +645,7 @@
         before.append(dot(flags, jnp.where(row < col, 1.0, 0.0).astype(jnp.bfloat16), 1, 0))
     slot = jnp.where(mine, jnp.concatenate(before, axis=1).astype(jnp.int32), -1)
     for h in range(heads):
-        per = jnp.concatenate([route[0, h:h + 1, k * size:(k + 1) * size] for k in range(n)], axis=0)
+        per = pers[h]
         local = jnp.where((per >= base) & (per < base + BLK), per - base, 0).astype(jnp.float32).astype(jnp.bfloat16)
         pick = jnp.where(slot[h:h + 1, :] == lax.broadcasted_iota(jnp.int32, (BLK, size), 0), 1.0, 0.0).astype(jnp.bfloat16)
         perm[h // 2, :, pl.ds((h % 2) * BLK, BLK)] = dot(local, pick, 1, 1).astype(jnp.int32)
@@ -699,10 +703,10 @@
 def layer_kernel(scale, w_shard, out_shard, up_shard, down_shard, vec_shard, ub_shard, route, x_rows, up_rows,
                  x_home, w_home, slots, probs, out_rows, gx_rows, r_qkv, r_aux, r_out, r_up, r_down,
                  w_out, w_up, w_down, act, gp, x, mixed, n1, s1, low, up, outb, dn, gd, head_ref, vec, ub, auxf,
-                 bq, bo, bu, bd, qkv_shard, perm, d_res, s2, sums, ubsum, ra, *rest):
+                 bq, bo, bu, bd, qkv_shard, perm, d_res, s2, sums, ubsum, ra, rb, *rest):
     own = [rest[i:i + N_SCRATCH] for i in (0, N_SCRATCH)]
-    late = rest[2 * N_SCRATCH:2 * N_SCRATCH + 3 + 2 * N_LINE]
-    ss, rs, ls, cs = rest[2 * N_SCRATCH + 3 + 2 * N_LINE:]
+    late = rest[2 * N_SCRATCH:2 * N_SCRATCH + 3 + 3 * N_LINE]
+    ss, rs, ls, cs = rest[2 * N_SCRATCH + 3 + 3 * N_LINE:]
     rows_here, width = x.shape
     ff = w_up.shape[1]
     pairs = perm.shape[0]
@@ -729,17 +733,24 @@
     gx_begin, gx_finish = spread(L, dn, gx_rows, ls.at[3], PARTS)
     g_up, part = act.at[pl.ds(0, width), :], act.at[pl.ds(0, width), pl.ds(0, SIZES["qkv"][1])]
     spare = [act.at[pl.ds(width, r * 8), pl.ds(i * width, width)] for i in range(4)]
-    hq = SIZES["qkv"][1] // 2
-    spare_q = [w_up.at[:, pl.ds(0, hq)]] + [w_up.at[pl.ds(i * r * 8, r * 8), pl.ds(hq + j * hq // 2, hq // 2)]
-                                          for j in range(2) for i in range(3)]
+    n_qk, n_v = SIZES["qk"][1], SIZES["v"][1]
+
+    def in_w_up(at, size, pieces):
+        q = size // 4
+        return [w_up.at[:, pl.ds(at, size // 2)]] + [w_up.at[pl.ds(i * r * 8, r * 8), pl.ds(pieces + j * q, q)]
+                                                    for j in range(2) for i in range(3)]
+    spare_qk = in_w_up(0, n_qk, (n_qk + n_v) // 2)
+    spare_v = in_w_up(n_qk // 2, n_v, (n_qk + n_v) // 2 + n_qk // 2)
     R = reduce(L, gd, r_down, own[0], *SIZES["down"][::2])
     R = L.under("sum", R[:1]) + R[1:]
     SO = reduce(L, w_out, r_out, own[1], *SIZES["out"][::2])
     SU = reduce(L, g_up, r_up, [late[0], *spare, *late[1:3 + N_LINE]], *SIZES["up"][::2])
     SU = L.under("sum_up", SU[:1]) + SU[1:]
-    SQ = reduce(L, part, ra, [*spare_q, *late[3 + N_LINE:]], *SIZES["qkv"][::2])
+    lines = late[3 + N_LINE:]
+    SK = reduce(L, act.at[pl.ds(0, width), pl.ds(0, n_qk)], ra, [*spare_qk, *lines[:N_LINE]], *SIZES["qk"][::2])
+    SV = reduce(L, act.at[pl.ds(0, width), pl.ds(n_qk, n_v)], rb, [*spare_v, *lines[N_LINE:]], *SIZES["v"][::2])
     plan = PLAN(Q, O, U, D, x_begin, up_begin, R)
-    plan.update(LATE(R, SO, SU, SQ, [functools.partial(gx_begin, i) for i in range(PARTS)]))
+    plan.update(LATE(R, SO, SU, SK, SV, [functools.partial(gx_begin, i) for i in range(PARTS)]))
     row = lambda i: vec[i:i + 1, :]
 
     def run(stages):
@@ -930,7 +941,7 @@
         c = pl.ds(mult(i * FB, FB), FB)
         part[:, c] = dot(x[...], gp[:, c], 0, 0).astype(jnp.bfloat16)
 
-    loop(3 * width // FB, grad_qkv)
+    loop(3 * width // FB, grad_qkv, plan["qkv"])
     d_res[0:BLK, :] = jnp.zeros((BLK, width), jnp.float32)
     d_res[0:2, :] = sums[6:8, :]
     d_res[2:8, :] = sums[0:6, :]
@@ -940,8 +951,9 @@
         auxf[i * r:i * r + 1, 0:step] = ubsum[0:1, i * step:(i + 1) * step]
     part[:, 3 * width + 128:3 * width + 256] = auxf[...].astype(jnp.bfloat16)
     run(plan["end"])
-    r_qkv[...] = ra[:, 0:3 * width]
-    r_aux[...] = ra[:, 3 * width:3 * width + 256]
+    r_qkv[:, 0:n_qk] = ra[...]
+    r_qkv[:, n_qk:3 * width] = rb[:, 0:3 * width - n_qk]
+    r_aux[...] = rb[:, 3 * width - n_qk:n_v]
     out_finish()
     gx_finish()
     L.drain()
@@ -959,16 +971,17 @@
     }
 
 
-def LATE(R, O, U, Q, G):
+def LATE(R, O, U, K, V, G):
     return {
         "third": [(0, R[1])],
         "grad_up": [],
-        "up_ready": [U[0]],
-        "out_ready": [O[0], R[2]],
+        "up_ready": [R[2], U[0]],
+        "out_ready": [O[0]],
         "back": [(0, U[1]), (1, R[3]), (1, R[4]), (2, O[1]), (3, R[5]), (4, R[6]), (5, R[7])],
         "x_ready": [G[0], G[1], U[2], O[2]],
-        "end": [Q[0], R[8], U[3], U[4], G[2], Q[1], O[3], O[4], U[5], G[3], Q[2], U[6], O[5], Q[3], Q[4], O[6], Q[5], U[7], O[7],
-                Q[6], Q[7], U[8], O[8], Q[8]],
+        "qkv": [(1, K[0])],
+        "end": [V[0], R[8], U[3], U[4], G[2], K[1], V[1], O[3], O[4], U[5], G[3], K[2], V[2], U[6], O[5], K[3], K[4], O[6],
+                V[3], V[4], K[5], U[7], O[7], V[5], K[6], V[6], K[7], V[7], U[8], O[8], K[8], V[8]],
     }
 
 
@@ -980,7 +993,7 @@
     ff = w_up.shape[1]
     r, cols, split = SIZES["down"]
     wq = SIZES["qkv"][1]
-    count = 4 * (N_GATHER + N_REDUCE) + 7 * (3 + PARTS)
+    count = 4 * N_GATHER + 5 * N_REDUCE + 7 * (3 + PARTS)
     f32 = lambda *s: jax.ShapeDtypeStruct(s, jnp.float32)
     bf = lambda *s: jax.ShapeDtypeStruct(s, BF)
     vbf = lambda *s: pltpu.VMEM(s, BF)
@@ -1001,9 +1014,10 @@
         + [vbf(ff, width), vbf(2 * rows_here, BLK), vf(8, width), vf(1, ff), vf(width, BLK)]
         + [vbf(SIZES[n][0], SIZES[n][1] // 2) for n in ("qkv", "out", "up", "down")]
         + [vbf(rq, wq), pltpu.VMEM((pairs, 2 * NZ, 2 * BLK), jnp.int32), vf(rows_here, width), vf(rows_here, 1), vf(8, width),
-           vf(8, ff), vf(rq, wq)]
+           vf(8, ff), vf(rq, SIZES["qk"][1]), vf(rq, SIZES["v"][1])]
         + reduce_scratch(r, cols, split) + reduce_scratch(*SIZES["out"])
-        + [vbf(*ru[0]), vbf(*ru[5]), vbf(*ru[6])] + line_scratch(*SIZES["up"][:2]) + line_scratch(rq, wq)
+        + [vbf(*ru[0]), vbf(*ru[5]), vbf(*ru[6])] + line_scratch(*SIZES["up"][:2])
+        + line_scratch(*SIZES["qk"][:2]) + line_scratch(*SIZES["v"][:2])
         + [pltpu.SemaphoreType.DMA((count,)), pltpu.SemaphoreType.DMA((count,)), pltpu.SemaphoreType.DMA((4, PARTS)),
            pltpu.SemaphoreType.DMA((13,))],
         compiler_params=pltpu.CompilerParams(collective_id=0, has_side_effects=True, vmem_limit_bytes=62 * 2**20),
@@ -1048,13 +1062,42 @@
     sums[7:8, col(0)] = total[:, 256:384]
 
 
+def settle_kernel(n, *refs):
+    ins, aux, outs, (gv, gb), bufs, sem = refs[:n], refs[n], refs[n + 1:2 * n + 1], refs[2 * n + 1:2 * n + 3], refs[2 * n + 3:-1], refs[-1]
+    loads = [pltpu.make_async_copy(a, b, sem.at[0, i]) for i, (a, b) in enumerate(zip(ins, bufs))]
+    stores = [pltpu.make_async_copy(a, b, sem.at[1, i]) for i, (a, b) in enumerate(zip(bufs, outs))]
+    for c in loads:
+        c.start()
+    gv[...] = aux[:, 0:128].T[0:gv.shape[0], :]
+    gb[...] = aux[0:1, 128:128 + gb.shape[1]]
+    for c, d in zip(loads, stores):
+        c.wait()
+        d.start()
+    for d in stores:
+        d.wait()
+
+
+def settle(arrays, aux, n_vec, n_bias):
+    hbm = pl.BlockSpec(memory_space=pl.ANY)
+    like = lambda a: jax.ShapeDtypeStruct(a.shape, a.dtype)
+    f32 = lambda *s: jax.ShapeDtypeStruct(s, jnp.float32)
+    return pl.pallas_call(
+        functools.partial(settle_kernel, len(arrays)), out_shape=[like(a) for a in arrays] + [f32(n_vec, aux.shape[0]), f32(1, n_bias)],
+        in_specs=[hbm] * len(arrays) + [VM], out_specs=[hbm] * len(arrays) + [VM] * 2,
+        scratch_shapes=[pltpu.VMEM(a.shape, a.dtype) for a in arrays] + [pltpu.SemaphoreType.DMA((2, len(arrays)))],
+        compiler_params=pltpu.CompilerParams(vmem_limit_bytes=LIMIT),
+    )(*arrays, aux)
+
+
 def homes(tokens, w_qkv, w_out, w_up, w_down, vectors, up_bias, cluster_route, upstream):
     pairs = H // 2
     scale = (tokens.shape[1] // H) ** -0.5
     step = up_bias.shape[0]
     out_rows, gx_rows, r_qkv, r_aux, r_out, r_up, r_down = layer_call(
-        scale, pairs, w_qkv, w_out, w_up, w_down, vectors, up_bias[None], cluster_route, tokens, upstream)[4:]
-    return (out_rows, gx_rows, r_qkv, r_out, r_up, r_down, r_aux[:, 0:8].T, r_aux[0, 128:128 + step])
+        scale, pairs, w_qkv, w_out, w_up, w_down, vectors, up_bias[None], cluster_route.reshape(-1, BLK), tokens, upstream)[4:]
+    gx, out, g_qkv, g_up, g_down, g_out, g_vec, g_bias = settle(
+        [gx_rows, out_rows, r_qkv, r_up, r_down, r_out], r_aux, vectors.shape[0], step)
+    return out, gx, g_qkv, g_out, g_up, g_down, g_vec, g_bias[0]
 
 
 def solution(mesh):

time: 240 us -> 231 us (0.963)
  local copies, waits for them, and re-layouts: 11.3 us -> 0 us
    unnamed x18 -> x0, local copies, waits for them, and re-layouts: 9.37 us -> none
    pallas_call x0 -> x1, Pallas kernels: none -> 4.78 us  [settle(): pl.pallas_call(functools.partial(settle_kernel, len(arrays)), out_shape=[...]
    pallas_call x1, Pallas kernels: 228 us -> 224 us  [layer_call(): pl.pallas_call(functools.partial(layer_kernel, scale), out_shape=[bf(rows...]
where the time goes in v6:
time: 231 us; the launch traced here: 230 us
  Pallas kernels  229 us (99%)
    pallas_call x1, Pallas kernels, layer_call(): pl.pallas_call(functools.partial(layer_kernel, scale), out_shape=[bf(rows...  224 us
    pallas_call x1, Pallas kernels, settle(): pl.pallas_call(functools.partial(settle_kernel, len(arrays)), out_shape=[...  4.78 us

profile of v6, /device:TPU:1, one launch (start us, length us, event | category | flops | bytes accessed | tf_op | source)
XLA Modules:
  0.0 229.7 jit_solution(4604735446729185411)
XLA Ops:
  0.6 224.1 %shard_map.152 = (bf16[1024,768]{1,0:T(8,128)(2,1)}, bf16[768,2560]{1,0:T(8,128)(2,1)}, bf16[6,2048,384]{2,1,0:T(8,128)(2,1)}, bf16[6,2,1024,128]{3,2,1,0:T(8,12...) custom-call(bf16[24,2304]{1,0:T(8,128)(2,1)} %w_shard.1, ...), custom_call_target="tpu_custom_call" | custom-call | tf_op jit(solution)/shard_map/pallas_call | solution.py:1004
  224.8 4.8 %shard_map.153 = (bf16[1024,768]{1,0:T(8,128)(2,1)}, bf16[1024,768]{1,0:T(8,128)(2,1)}, f32[24,2304]{1,0:T(8,128)}, f32[24,3072]{1,0:T(8,128)}, f32[96,768]{1,0:...) custom-call(bf16[1024,768]{1,0:T(8,128)(2,1)} %get-tuple-element.23.refs_0_, ...), custom_call_target="tpu_custom_call" | custom-call | tf_op jit(solution)/shard_map/pallas_call | solution.py:1084

commit v7 on v6

--- a/solution.py
+++ b/solution.py
@@ -432,7 +432,7 @@
 
     def begin(i=0):
         keep(i).start()
-        for j in range(1, 2 * NZ):
+        for j in (1, 7, 2, 6, 3, 5, 4):
             L.go(lambda j=j: move(i, j, lax.rem(L.sq + j, 2 * NZ), L.sq))
 
     def finish():
@@ -965,7 +965,7 @@
         "placed": [Q[6],Q[7]],
         "weights": [O[5],U[5]],
         "project": [(1,D[2])],
-        "attend": [(0,D[3]),(0,up_begin),(0,O[6]),(0,U[6]),(2,O[7]),(2,U[7]),(3,D[4])],
+        "attend": [(0,D[3]),(0,up_begin),(1,O[6]),(1,U[6]),(3,O[7]),(3,U[7]),(3,D[4])],
         "first": [(0,D[5]),(3,D[6])],
         "firsts": [D[7]],
     }

time: 231 us -> 226 us (0.978)
  Pallas kernels: 229 us -> 225 us
    pallas_call x1, Pallas kernels: 224 us -> 220 us  [layer_call(): pl.pallas_call(functools.partial(layer_kernel, scale), out_shape=[bf(rows...]
where the time goes in v7:
time: 226 us
  Pallas kernels  225 us (100%)
    pallas_call x1, Pallas kernels, layer_call(): pl.pallas_call(functools.partial(layer_kernel, scale), out_shape=[bf(rows...  220 us
    pallas_call x1, Pallas kernels, settle(): pl.pallas_call(functools.partial(settle_kernel, len(arrays)), out_shape=[...  4.78 us

profile of v7, /device:TPU:1, one launch (start us, length us, event | category | flops | bytes accessed | tf_op | source)
XLA Modules:
  0.0 225.5 jit_solution(6189243505731129881)
XLA Ops:
  0.6 219.9 %shard_map.152 = (bf16[1024,768]{1,0:T(8,128)(2,1)}, bf16[768,2560]{1,0:T(8,128)(2,1)}, bf16[6,2048,384]{2,1,0:T(8,128)(2,1)}, bf16[6,2,1024,128]{3,2,1,0:T(8,12...) custom-call(bf16[24,2304]{1,0:T(8,128)(2,1)} %w_shard.1, ...), custom_call_target="tpu_custom_call" | custom-call | tf_op jit(solution)/shard_map/pallas_call | solution.py:1004
  220.6 4.8 %shard_map.153 = (bf16[1024,768]{1,0:T(8,128)(2,1)}, bf16[1024,768]{1,0:T(8,128)(2,1)}, f32[24,2304]{1,0:T(8,128)}, f32[24,3072]{1,0:T(8,128)}, f32[96,768]{1,0:...) custom-call(bf16[1024,768]{1,0:T(8,128)(2,1)} %get-tuple-element.23.refs_0_, ...), custom_call_target="tpu_custom_call" | custom-call | tf_op jit(solution)/shard_map/pallas_call | solution.py:1084
